TPU v7x, 32 devices: a whole 2x2x4 slice. The times are simulated.
32 devices in a mesh: ctx: 8 (over z, core), adp: 4 (over y, x).
Axes of the slice: x: 2, y: 2, z: 4, core: 2. Of those that a mesh axis runs over, the one named last changes fastest.
Arguments:
- queries: bfloat16 [2048, 4096], P('ctx', 'adp'), may hold values from -100 to 100
- keys: bfloat16 [2048, 512], P('ctx'), may hold values from -5 to 5
- values: bfloat16 [2048, 512], P('ctx'), may hold values from -6 to 6
- grad_out: bfloat16 [2048, 4096], P('ctx', 'adp'), may hold values from -6 to 6
- docs: int32 [2048], P('ctx'), may hold values from 0 to 15, never falling along the last dimension, each value on 1 to 1536 neighbouring positions
- block_tenant: int32 [16], P('ctx'), may hold values from 0 to 3
- low_rank: bfloat16 [2048, 64], P('ctx'), may hold values from -6 to 6
- adapter_b: bfloat16 [4, 64, 4096], P('adp'), may hold values from -0.75 to 0.75
Outputs:
- grad_queries: bfloat16 [2048, 4096], P('ctx', 'adp')
- grad_low_rank: float32 [2048, 64], P(('ctx', 'adp'))
- grad_adapter: float32 [4, 64, 4096], P('adp', None, 'ctx')
Inputs may be any that keep to these rules, and one draw needn't show every extreme that they name: docs never falls from one position to the next.
All inputs are finite; a program needn't handle non-finite values.
Results may differ from a plain program's by a relative error of at most 0.019.
Values may be sent and summed in bfloat16 or wider, within the bound.
No kernel may reach another device: no remote copies, remote signals or barrier semaphores. Data moves between devices by JAX's collectives and lax.ppermute only.
A program may use at most 64 MiB of HBM per device.

v0:
```python
import jax
import jax.numpy as jnp
from jax import lax
from jax.sharding import PartitionSpec as P

QH = 32
KVH = 4
HD = 128
RANK = 64
BLOCK = 128


adapter_scale_factor = 2.0
far_below = -1e30


def key_blocks(fold_state, key_piece, update):
    key_part, value_part, doc_part = key_piece
    key_total_count = key_part.shape[0]
    block_span = 512

    def advance(step_index, current):
        offset = step_index * block_span
        return update(
            current,
            lax.dynamic_slice_in_dim(key_part, offset, block_span, 0),
            lax.dynamic_slice_in_dim(value_part, offset, block_span, 0),
            lax.dynamic_slice_in_dim(doc_part, offset, block_span, 0),
            offset,
        )

    return lax.fori_loop(0, key_total_count // block_span, advance, fold_state)


def allowed(query_pos, query_doc, doc_block, key_start):
    key_pos = key_start + jnp.arange(doc_block.shape[0], dtype=jnp.int32)
    return (key_pos[None, :] <= query_pos[:, None]) & (doc_block[None, :] == query_doc[:, None])


def on_device(queries, keys, values, grad_out, docs, block_tenant, low_rank, adapter_b):
    tokens = queries.shape[0]
    heads_dev = queries.shape[1] // HD
    kv_head = lax.axis_index("adp") * heads_dev // (QH // KVH)
    my_keys = lax.dynamic_slice_in_dim(keys, kv_head * HD, HD, 1)
    my_values = lax.dynamic_slice_in_dim(values, kv_head * HD, HD, 1)
    query_rows = (
        queries.reshape(tokens, heads_dev, HD).transpose(1, 0, 2).reshape(heads_dev * tokens, HD)
    )
    grad_rows = (
        grad_out.reshape(tokens, heads_dev, HD).transpose(1, 0, 2).reshape(heads_dev * tokens, HD)
    )
    first_pos = lax.axis_index("ctx") * tokens
    query_pos = jnp.tile(first_pos + jnp.arange(tokens, dtype=jnp.int32), heads_dev)
    query_doc = jnp.tile(docs, heads_dev)
    logit_scale = HD ** (-0.5)
    row_count = heads_dev * tokens

    def forward_update(current, key_block, value_block, doc_block, key_start):
        row_top, row_total, weighted = current
        scores = (
            jnp.einsum("qd,kd->qk", query_rows, key_block, preferred_element_type=jnp.float32)
            * logit_scale
        )
        visible = allowed(query_pos, query_doc, doc_block, key_start)
        updated_running_max = jnp.maximum(
            row_top, jnp.max(jnp.where(visible, scores, far_below), axis=1)
        )
        decay_factor = jnp.exp(row_top - updated_running_max)
        weights_f = jnp.where(visible, jnp.exp(scores - updated_running_max[:, None]), 0.0)
        row_total = row_total * decay_factor + jnp.sum(weights_f, axis=1)
        weighted = weighted * decay_factor[:, None] + jnp.dot(
            weights_f.astype(jnp.bfloat16), value_block, preferred_element_type=jnp.float32
        )
        return (updated_running_max, row_total, weighted)

    start_state = (
        jnp.full((row_count,), far_below, jnp.float32),
        jnp.zeros((row_count,), jnp.float32),
        jnp.zeros((row_count, HD), jnp.float32),
    )
    fwd_state = key_blocks(
        start_state,
        (
            lax.all_gather(my_keys, "ctx", axis=0, tiled=True),
            lax.all_gather(my_values, "ctx", axis=0, tiled=True),
            lax.all_gather(docs, "ctx", axis=0, tiled=True),
        ),
        update=forward_update,
    )
    row_top, row_total, weighted = fwd_state
    log_total = row_top + jnp.log(row_total)
    row_delta = jnp.sum(grad_rows.astype(jnp.float32) * (weighted / row_total[:, None]), axis=1)

    def backward_update(grad_acc, key_block, value_block, doc_block, key_start):
        scores = (
            jnp.einsum("qd,kd->qk", query_rows, key_block, preferred_element_type=jnp.float32)
            * logit_scale
        )
        visible = allowed(query_pos, query_doc, doc_block, key_start)
        weights_f = jnp.where(visible, jnp.exp(scores - log_total[:, None]), 0.0)
        grad_weights = jnp.einsum(
            "qd,kd->qk", grad_rows, value_block, preferred_element_type=jnp.float32
        )
        grad_scores = (weights_f * (grad_weights - row_delta[:, None])).astype(jnp.bfloat16)
        return grad_acc + jnp.dot(grad_scores, key_block, preferred_element_type=jnp.float32)

    zero_grad = jnp.zeros((row_count, HD), jnp.float32)
    grad_acc = key_blocks(
        zero_grad,
        (
            lax.all_gather(my_keys, "ctx", axis=0, tiled=True),
            lax.all_gather(my_values, "ctx", axis=0, tiled=True),
            lax.all_gather(docs, "ctx", axis=0, tiled=True),
        ),
        update=backward_update,
    )
    grad_queries = (
        (grad_acc * logit_scale)
        .astype(jnp.bfloat16)
        .reshape(heads_dev, tokens, HD)
        .transpose(1, 0, 2)
        .reshape(tokens, heads_dev * HD)
    )
    columns = lax.all_to_all(adapter_b, "adp", split_axis=2, concat_axis=0, tiled=True)
    blocks = tokens // BLOCK
    col_width = grad_queries.shape[1]
    grad_blocks = grad_queries.reshape(blocks, BLOCK, col_width)
    chosen = jnp.take(columns, block_tenant, axis=0)
    rank_contributions = (
        jnp.einsum("bkc,brc->bkr", grad_blocks, chosen, preferred_element_type=jnp.float32).reshape(
            tokens, RANK
        )
        * adapter_scale_factor
    )
    grad_low_rank = lax.psum_scatter(rank_contributions, "adp", scatter_dimension=0, tiled=True)
    low_blocks = low_rank.reshape(blocks, BLOCK, RANK)
    block_partials = jnp.einsum(
        "bkr,bkc->brc", low_blocks, grad_blocks, preferred_element_type=jnp.float32
    )
    tenants = columns.shape[0]
    tenant_membership = (
        jnp.arange(tenants, dtype=jnp.int32)[:, None] == block_tenant[None, :]
    ).astype(jnp.float32)
    tenant_contributions = (
        jnp.sum(tenant_membership[:, :, None, None] * block_partials[None], axis=1)
        * adapter_scale_factor
    )
    summed_all = lax.psum(tenant_contributions, "ctx")
    owner_view = lax.all_to_all(summed_all, "adp", split_axis=0, concat_axis=2, tiled=True)
    col_share = owner_view.shape[2] // lax.axis_size("ctx")
    grad_adapter = lax.dynamic_slice_in_dim(
        owner_view, lax.axis_index("ctx") * col_share, col_share, 2
    )
    return (grad_queries, grad_low_rank, grad_adapter)


def solution(mesh):
    placed = (
        P("ctx", "adp"),
        P("ctx", None),
        P("ctx", None),
        P("ctx", "adp"),
        P("ctx"),
        P("ctx"),
        P("ctx", None),
        P("adp", None, None),
    )
    return jax.shard_map(
        on_device,
        mesh=mesh,
        in_specs=placed,
        out_specs=(P("ctx", "adp"), P(("ctx", "adp"), None), P("adp", None, "ctx")),
        check_vma=False,
    )
```

profile of v0, /device:TPU:0, one launch (start us, length us, event | category | flops | bytes accessed | tf_op | source)
XLA Modules:
  0.0 235.1 jit_solution(7861803957652518717)
XLA Ops:
  8.1 0.9 constant_dynamic-slice_fusion.2
  9.0 16.6 %all_gather.13 = bf16[2048,128]{1,0:T(8,128)(2,1)S(1)} all-gather(bf16[256,128]{1,0:T(8,128)(2,1)S(1)} %constant_dynamic-slice_fusion.2), channel_id=1, replica_groups=mesh['ctx'=8,'adp'=4] {'ctx'}, dimensions={0}, use_global_device_ids=true | all-gather | bytes 589824 | tf_op jit(solution)/shard_map/all_gather | solution.py:111
  25.6 0.8 constant_dynamic-slice_fusion.1
  26.4 15.8 %all_gather.14 = bf16[2048,128]{1,0:T(8,128)(2,1)} all-gather(bf16[256,128]{1,0:T(8,128)(2,1)S(1)} %constant_dynamic-slice_fusion.1), channel_id=1, replica_groups=mesh['ctx'=8,'adp'=4] {'ctx'}, dimensions={0}, use_global_device_ids=true | all-gather | bytes 589824 | tf_op jit(solution)/shard_map/all_gather | solution.py:112
  42.3 12.1 %all-gather = s32[8,1,256]{2,1,0:T(1,128)S(1)} all-gather(s32[1,1,256]{2,1,0:T(1,128)} %bitcast.140), channel_id=1, replica_groups=mesh['ctx'=8,'adp'=4] {'ctx'}, dimensions={0}, use_global_device_ids=true | all-gather | bytes 9216 | tf_op jit(solution)/shard_map/all_gather | solution.py:113
  54.4 44.1 %while.32 = (s32[]{:T(128)}, f32[2048]{0:T(1024)S(1)}, f32[2048]{0:T(1024)S(1)}, f32[2048,128]{1,0:T(8,128)}, s32[2048]{0:T(1024)S(1)}, /*index=5*/bf16[2048,128...) while((s32[]{:T(128)}, f32[2048]{0:T(1024)S(1)}, ...), condition=%wide.region_3.4_spmd.clone, body=%wide.region_0.3_spmd.clone.sunk | while | flops 558639616 | bytes 32493800 | solution.py:32
  54.5 0.7 broadcast_bitcast_fusion.6
  55.2 3.0 %fusion.70 = (f32[2048]{0:T(1024)S(1)}, f32[512,2048]{1,0:T(8,128)}) fusion(s32[2048]{0:T(1024)S(1)} %bitcast.130, s32[2048]{0:T(1024)S(1)} %bitcast.133, s32[512]{0:T(512)S(1)} %dynamic_slice.85, s32[512]{0:T(512)S(1)} %iota_add_fusion.5, bf16[2048,128]{1,0:T(8,128)(2,1)S(1)} %get-tuple-element.688, bf16[2048,128]{1,0:T(8,128)(2,1)S(1)} %get-tuple-element.687, ...), kind=kOutput, calls=%fused_computation.7.clone.1 | convolution fusion | flops 274724864 | bytes 4878340 | tf_op jit(solution)/shard_map/while/body/eval_jaxpr/qd,kd->qk/dot_general | solution.py:61
  58.2 3.3 %fusion.71 = f32[2048]{0:T(1024)S(1)} fusion(f32[512,2048]{1,0:T(8,128)} %get-tuple-element.638, f32[2048]{0:T(1024)S(1)} %select_maximum_fusion.2, s32[2048]{0:T(1024)S(1)} %bitcast.131, s32[2048]{0:T(1024)S(1)} %bitcast.134, s32[512]{0:T(512)S(1)} %dynamic_slice.85, s32[512]{0:T(512)S(1)} %iota_add_fusion.5), kind=kLoop, calls=%fused_computation.13.clone.1 | loop fusion | flops 7337984 | bytes 4231168 | tf_op jit(solution)/shard_map/while/body/eval_jaxpr/reduce_sum | solution.py:70
  61.6 3.5 %convolution_add_fusion.4 = f32[2048,128]{1,0:T(8,128)} fusion(f32[512,2048]{1,0:T(8,128)S(1)} %copy-done.1, f32[2048]{0:T(1024)S(1)} %select_maximum_fusion.2, s32[2048]{0:T(1024)S(1)} %bitcast.132, s32[2048]{0:T(1024)S(1)} %bitcast.135, s32[512]{0:T(512)S(1)} %dynamic_slice.85, s32[512]{0:T(512)S(1)} %iota_add_fusion.5, ...), kind=kOutput, calls=%fused_computation.11.clone.1 | convolution fusion | flops 276561920 | bytes 6459397 | tf_op jit(solution)/shard_map/while/body/eval_jaxpr/dot_general | solution.py:71
  65.2 0.7 broadcast_bitcast_fusion.6
  65.9 3.0 %fusion.70 = (f32[2048]{0:T(1024)S(1)}, f32[512,2048]{1,0:T(8,128)}) fusion(s32[2048]{0:T(1024)S(1)} %bitcast.130, s32[2048]{0:T(1024)S(1)} %bitcast.133, s32[512]{0:T(512)S(1)} %dynamic_slice.85, s32[512]{0:T(512)S(1)} %iota_add_fusion.5, bf16[2048,128]{1,0:T(8,128)(2,1)S(1)} %get-tuple-element.688, bf16[2048,128]{1,0:T(8,128)(2,1)S(1)} %get-tuple-element.687, ...), kind=kOutput, calls=%fused_computation.7.clone.1 | convolution fusion | flops 274724864 | bytes 4878340 | tf_op jit(solution)/shard_map/while/body/eval_jaxpr/qd,kd->qk/dot_general | solution.py:61
  68.9 3.3 %fusion.71 = f32[2048]{0:T(1024)S(1)} fusion(f32[512,2048]{1,0:T(8,128)} %get-tuple-element.638, f32[2048]{0:T(1024)S(1)} %select_maximum_fusion.2, s32[2048]{0:T(1024)S(1)} %bitcast.131, s32[2048]{0:T(1024)S(1)} %bitcast.134, s32[512]{0:T(512)S(1)} %dynamic_slice.85, s32[512]{0:T(512)S(1)} %iota_add_fusion.5), kind=kLoop, calls=%fused_computation.13.clone.1 | loop fusion | flops 7337984 | bytes 4231168 | tf_op jit(solution)/shard_map/while/body/eval_jaxpr/reduce_sum | solution.py:70
  72.3 3.9 %convolution_add_fusion.4 = f32[2048,128]{1,0:T(8,128)} fusion(f32[512,2048]{1,0:T(8,128)S(1)} %copy-done.1, f32[2048]{0:T(1024)S(1)} %select_maximum_fusion.2, s32[2048]{0:T(1024)S(1)} %bitcast.132, s32[2048]{0:T(1024)S(1)} %bitcast.135, s32[512]{0:T(512)S(1)} %dynamic_slice.85, s32[512]{0:T(512)S(1)} %iota_add_fusion.5, ...), kind=kOutput, calls=%fused_computation.11.clone.1 | convolution fusion | flops 276561920 | bytes 6459397 | tf_op jit(solution)/shard_map/while/body/eval_jaxpr/dot_general | solution.py:71
  76.4 0.7 broadcast_bitcast_fusion.6
  77.0 3.0 %fusion.70 = (f32[2048]{0:T(1024)S(1)}, f32[512,2048]{1,0:T(8,128)}) fusion(s32[2048]{0:T(1024)S(1)} %bitcast.130, s32[2048]{0:T(1024)S(1)} %bitcast.133, s32[512]{0:T(512)S(1)} %dynamic_slice.85, s32[512]{0:T(512)S(1)} %iota_add_fusion.5, bf16[2048,128]{1,0:T(8,128)(2,1)S(1)} %get-tuple-element.688, bf16[2048,128]{1,0:T(8,128)(2,1)S(1)} %get-tuple-element.687, ...), kind=kOutput, calls=%fused_computation.7.clone.1 | convolution fusion | flops 274724864 | bytes 4878340 | tf_op jit(solution)/shard_map/while/body/eval_jaxpr/qd,kd->qk/dot_general | solution.py:61
  80.0 3.3 %fusion.71 = f32[2048]{0:T(1024)S(1)} fusion(f32[512,2048]{1,0:T(8,128)} %get-tuple-element.638, f32[2048]{0:T(1024)S(1)} %select_maximum_fusion.2, s32[2048]{0:T(1024)S(1)} %bitcast.131, s32[2048]{0:T(1024)S(1)} %bitcast.134, s32[512]{0:T(512)S(1)} %dynamic_slice.85, s32[512]{0:T(512)S(1)} %iota_add_fusion.5), kind=kLoop, calls=%fused_computation.13.clone.1 | loop fusion | flops 7337984 | bytes 4231168 | tf_op jit(solution)/shard_map/while/body/eval_jaxpr/reduce_sum | solution.py:70
  83.4 3.9 %convolution_add_fusion.4 = f32[2048,128]{1,0:T(8,128)} fusion(f32[512,2048]{1,0:T(8,128)S(1)} %copy-done.1, f32[2048]{0:T(1024)S(1)} %select_maximum_fusion.2, s32[2048]{0:T(1024)S(1)} %bitcast.132, s32[2048]{0:T(1024)S(1)} %bitcast.135, s32[512]{0:T(512)S(1)} %dynamic_slice.85, s32[512]{0:T(512)S(1)} %iota_add_fusion.5, ...), kind=kOutput, calls=%fused_computation.11.clone.1 | convolution fusion | flops 276561920 | bytes 6459397 | tf_op jit(solution)/shard_map/while/body/eval_jaxpr/dot_general | solution.py:71
  88.2 3.0 %fusion.70 = (f32[2048]{0:T(1024)S(1)}, f32[512,2048]{1,0:T(8,128)}) fusion(s32[2048]{0:T(1024)S(1)} %bitcast.130, s32[2048]{0:T(1024)S(1)} %bitcast.133, s32[512]{0:T(512)S(1)} %dynamic_slice.85, s32[512]{0:T(512)S(1)} %iota_add_fusion.5, bf16[2048,128]{1,0:T(8,128)(2,1)S(1)} %get-tuple-element.688, bf16[2048,128]{1,0:T(8,128)(2,1)S(1)} %get-tuple-element.687, ...), kind=kOutput, calls=%fused_computation.7.clone.1 | convolution fusion | flops 274724864 | bytes 4878340 | tf_op jit(solution)/shard_map/while/body/eval_jaxpr/qd,kd->qk/dot_general | solution.py:61
  91.1 3.3 %fusion.71 = f32[2048]{0:T(1024)S(1)} fusion(f32[512,2048]{1,0:T(8,128)} %get-tuple-element.638, f32[2048]{0:T(1024)S(1)} %select_maximum_fusion.2, s32[2048]{0:T(1024)S(1)} %bitcast.131, s32[2048]{0:T(1024)S(1)} %bitcast.134, s32[512]{0:T(512)S(1)} %dynamic_slice.85, s32[512]{0:T(512)S(1)} %iota_add_fusion.5), kind=kLoop, calls=%fused_computation.13.clone.1 | loop fusion | flops 7337984 | bytes 4231168 | tf_op jit(solution)/shard_map/while/body/eval_jaxpr/reduce_sum | solution.py:70
  94.6 3.9 %convolution_add_fusion.4 = f32[2048,128]{1,0:T(8,128)} fusion(f32[512,2048]{1,0:T(8,128)S(1)} %copy-done.1, f32[2048]{0:T(1024)S(1)} %select_maximum_fusion.2, s32[2048]{0:T(1024)S(1)} %bitcast.132, s32[2048]{0:T(1024)S(1)} %bitcast.135, s32[512]{0:T(512)S(1)} %dynamic_slice.85, s32[512]{0:T(512)S(1)} %iota_add_fusion.5, ...), kind=kOutput, calls=%fused_computation.11.clone.1 | convolution fusion | flops 276561920 | bytes 6459397 | tf_op jit(solution)/shard_map/while/body/eval_jaxpr/dot_general | solution.py:71
  98.5 1.1 copy_bitcast_fusion.1
  99.7 1.9 multiply_reduce_fusion.1
  101.6 30.5 %while.33 = (s32[]{:T(128)}, f32[2048,128]{1,0:T(8,128)S(1)}, s32[2048]{0:T(1024)S(1)}, bf16[2048,128]{1,0:T(8,128)(2,1)S(1)}, bf16[2048,128]{1,0:T(8,128)(2,1)S...) while((s32[]{:T(128)}, f32[2048,128]{1,0:T(8,128)S(1)}, ...), condition=%wide.region_6.7_spmd.clone, body=%wide.region_5.6_spmd.clone.sunk | while | flops 815268352 | bytes 12027628 | solution.py:32
  101.6 2.6 %fusion.78 = f32[512,2048]{1,0:T(8,128)} fusion(bf16[2048,128]{1,0:T(8,128)(2,1)S(1)} %get-tuple-element.730, bf16[2048,128]{1,0:T(8,128)(2,1)S(1)} %get-tuple-element.729, s32[]{:T(128)S(6)} %select_n.101), kind=kOutput, calls=%fused_computation.42.clone.1 | convolution fusion | flops 268435456 | bytes 4849668 | tf_op jit(solution)/shard_map/while/body/eval_jaxpr/qd,kd->qk/dot_general | solution.py:96
  104.3 4.8 %convolution_add_fusion.5 = f32[2048,128]{1,0:T(8,128)S(1)} fusion(f32[512,2048]{1,0:T(8,128)} %fusion.78, bf16[2048,128]{1,0:T(8,128)(2,1)S(1)} %get-tuple-element.733, f32[2048]{0:T(1024)S(1)} %get-tuple-element.734, f32[2048]{0:T(1024)S(1)} %get-tuple-element.731, s32[2048]{0:T(1024)S(1)} %bitcast.138, s32[2048]{0:T(1024)S(1)} %bitcast.139, ...), kind=kOutput, calls=%fused_computation.39.clone.1 | convolution fusion | flops 546832384 | bytes 7116288 | tf_op jit(solution)/shard_map/while/body/eval_jaxpr/dot_general | solution.py:105
  109.2 2.6 %fusion.78 = f32[512,2048]{1,0:T(8,128)} fusion(bf16[2048,128]{1,0:T(8,128)(2,1)S(1)} %get-tuple-element.730, bf16[2048,128]{1,0:T(8,128)(2,1)S(1)} %get-tuple-element.729, s32[]{:T(128)S(6)} %select_n.101), kind=kOutput, calls=%fused_computation.42.clone.1 | convolution fusion | flops 268435456 | bytes 4849668 | tf_op jit(solution)/shard_map/while/body/eval_jaxpr/qd,kd->qk/dot_general | solution.py:96
  112.0 4.8 %convolution_add_fusion.5 = f32[2048,128]{1,0:T(8,128)S(1)} fusion(f32[512,2048]{1,0:T(8,128)} %fusion.78, bf16[2048,128]{1,0:T(8,128)(2,1)S(1)} %get-tuple-element.733, f32[2048]{0:T(1024)S(1)} %get-tuple-element.734, f32[2048]{0:T(1024)S(1)} %get-tuple-element.731, s32[2048]{0:T(1024)S(1)} %bitcast.138, s32[2048]{0:T(1024)S(1)} %bitcast.139, ...), kind=kOutput, calls=%fused_computation.39.clone.1 | convolution fusion | flops 546832384 | bytes 7116288 | tf_op jit(solution)/shard_map/while/body/eval_jaxpr/dot_general | solution.py:105
  116.9 2.6 %fusion.78 = f32[512,2048]{1,0:T(8,128)} fusion(bf16[2048,128]{1,0:T(8,128)(2,1)S(1)} %get-tuple-element.730, bf16[2048,128]{1,0:T(8,128)(2,1)S(1)} %get-tuple-element.729, s32[]{:T(128)S(6)} %select_n.101), kind=kOutput, calls=%fused_computation.42.clone.1 | convolution fusion | flops 268435456 | bytes 4849668 | tf_op jit(solution)/shard_map/while/body/eval_jaxpr/qd,kd->qk/dot_general | solution.py:96
  119.6 4.8 %convolution_add_fusion.5 = f32[2048,128]{1,0:T(8,128)S(1)} fusion(f32[512,2048]{1,0:T(8,128)} %fusion.78, bf16[2048,128]{1,0:T(8,128)(2,1)S(1)} %get-tuple-element.733, f32[2048]{0:T(1024)S(1)} %get-tuple-element.734, f32[2048]{0:T(1024)S(1)} %get-tuple-element.731, s32[2048]{0:T(1024)S(1)} %bitcast.138, s32[2048]{0:T(1024)S(1)} %bitcast.139, ...), kind=kOutput, calls=%fused_computation.39.clone.1 | convolution fusion | flops 546832384 | bytes 7116288 | tf_op jit(solution)/shard_map/while/body/eval_jaxpr/dot_general | solution.py:105
  124.5 2.6 %fusion.78 = f32[512,2048]{1,0:T(8,128)} fusion(bf16[2048,128]{1,0:T(8,128)(2,1)S(1)} %get-tuple-element.730, bf16[2048,128]{1,0:T(8,128)(2,1)S(1)} %get-tuple-element.729, s32[]{:T(128)S(6)} %select_n.101), kind=kOutput, calls=%fused_computation.42.clone.1 | convolution fusion | flops 268435456 | bytes 4849668 | tf_op jit(solution)/shard_map/while/body/eval_jaxpr/qd,kd->qk/dot_general | solution.py:96
  127.2 4.8 %convolution_add_fusion.5 = f32[2048,128]{1,0:T(8,128)S(1)} fusion(f32[512,2048]{1,0:T(8,128)} %fusion.78, bf16[2048,128]{1,0:T(8,128)(2,1)S(1)} %get-tuple-element.733, f32[2048]{0:T(1024)S(1)} %get-tuple-element.734, f32[2048]{0:T(1024)S(1)} %get-tuple-element.731, s32[2048]{0:T(1024)S(1)} %bitcast.138, s32[2048]{0:T(1024)S(1)} %bitcast.139, ...), kind=kOutput, calls=%fused_computation.39.clone.1 | convolution fusion | flops 546832384 | bytes 7116288 | tf_op jit(solution)/shard_map/while/body/eval_jaxpr/dot_general | solution.py:105
  133.3 1.1 broadcast_multiply_fusion
  134.4 4.9 %copy.50 = bf16[1,64,4096]{1,0,2:T(2,128)(2,1)S(1)} copy(bf16[1,64,4096]{2,1,0:T(8,128)(2,1)} %param.19) | data formatting | bytes 1048576 | tf_op args[7]
  139.8 23.6 %reduce = bf16[4096,64]{1,0:T(8,128)(2,1)} reduce(bf16[4096,1,64]{2,1,0:T(2,128)(2,1)S(1)} %bitcast.122, bf16[]{:T(256)} %broadcast.116), dimensions={1}, to_apply=%bitcast.76.reduce_sub_computation | reduce | bytes 1048578
  163.4 1.9 reshape.100
  165.3 12.6 %all_to_all.36 = bf16[4,2,32768]{2,1,0:T(2,128)(2,1)} all-to-all(bf16[4,2,32768]{2,1,0:T(2,128)(2,1)S(1)} %reshape.100), channel_id=1, replica_groups=mesh['ctx'=8,'adp'=4] {'adp'}, dimensions={0} | all-to-all | bytes 1048576 | tf_op jit(solution)/shard_map/all_to_all | solution.py:124
  177.9 13.9 %all-reduce.2.cloned.1.call-done = f32[4,64,1024]{2,1,0:T(8,128)} async-done(((f32[4,64,1024]{2,1,0:T(8,128)}), f32[4,64,1024]{2,1,0:T(8,128)}) %all-reduce.2.cloned.1.call-update) | async-done | bytes 1048592 | tf_op jit(solution)/shard_map/psum | solution.py:148
  191.8 4.3 %all-to-all-start.1 = ((f32[4,64,1024]{2,1,0:T(8,128)}), f32[4,64,1024]{2,1,0:T(8,128)}, u32[]{:S(2)}, u32[]{:S(2)}) async-start(f32[4,64,1024]{2,1,0:T(8,128)} %all-reduce.2.cloned.1.call-done), calls=%async_computation.1 | async-start | bytes 2097152 | tf_op jit(solution)/shard_map/all_to_all | solution.py:149
  196.1 2.5 %reshape.101 = bf16[4096,1,64]{2,1,0:T(2,128)(2,1)S(1)} reshape(bf16[4,2,32768]{2,1,0:T(2,128)(2,1)} %all_to_all.36) | data formatting | bytes 1048576
  198.6 1.1 copy.63
  199.8 1.5 copy.52
  201.9 1.4 convolution_multiply_fusion
  203.3 0.8 copy.61
  204.0 0.9 copy.82
  204.9 3.6 %all-to-all-done.1 = f32[4,64,1024]{2,1,0:T(8,128)} async-done(((f32[4,64,1024]{2,1,0:T(8,128)}), f32[4,64,1024]{2,1,0:T(8,128)}, u32[]{:S(2)}, u32[]{:S(2)}) %all-to-all-start.1) | async-done | bytes 1048608 | tf_op jit(solution)/shard_map/all_to_all | solution.py:149
  208.5 1.3 copy.71
  210.5 17.1 %reduce-scatter.4.cloned.1.call-done = f32[64,64]{1,0:T(8,128)} async-done(((f32[256,64]{1,0:T(8,128)}), f32[64,64]{1,0:T(8,128)}) %reduce-scatter.4.cloned.1.call-update) | async-done | bytes 16400
  (96 shorter events, 5.1 us)
Async XLA Ops:
  8.0 34.2 %copy-start = (bf16[256,1024]{1,0:T(8,128)(2,1)S(1)}, bf16[256,1024]{1,0:T(8,128)(2,1)}, u32[]{:S(2)}) copy-start(bf16[256,1024]{1,0:T(8,128)(2,1)} %param.12) | copy-start | bytes 1572868
  8.0 183.8 %all-reduce.2.cloned.1.call-start = ((), (), s32[]{:S(2)}) async-start(), calls=%async_computation.3 | async-start | bytes 2097152 | tf_op jit(solution)/shard_map/psum | solution.py:148
  58.1 3.4 %copy-start.1 = (f32[512,2048]{1,0:T(8,128)S(1)}, f32[512,2048]{1,0:T(8,128)}, u32[]{:S(2)}) copy-start(f32[512,2048]{1,0:T(8,128)} %get-tuple-element.638) | copy-start | bytes 12582916 | tf_op jit(solution)/shard_map/while
  68.9 3.4 %copy-start.1 = (f32[512,2048]{1,0:T(8,128)S(1)}, f32[512,2048]{1,0:T(8,128)}, u32[]{:S(2)}) copy-start(f32[512,2048]{1,0:T(8,128)} %get-tuple-element.638) | copy-start | bytes 12582916 | tf_op jit(solution)/shard_map/while
  80.0 3.4 %copy-start.1 = (f32[512,2048]{1,0:T(8,128)S(1)}, f32[512,2048]{1,0:T(8,128)}, u32[]{:S(2)}) copy-start(f32[512,2048]{1,0:T(8,128)} %get-tuple-element.638) | copy-start | bytes 12582916 | tf_op jit(solution)/shard_map/while
  91.1 3.4 %copy-start.1 = (f32[512,2048]{1,0:T(8,128)S(1)}, f32[512,2048]{1,0:T(8,128)}, u32[]{:S(2)}) copy-start(f32[512,2048]{1,0:T(8,128)} %get-tuple-element.638) | copy-start | bytes 12582916 | tf_op jit(solution)/shard_map/while
  101.5 31.2 %copy-start.5 = (s32[2]{0:T(128)S(1)}, s32[2]{0:T(128)}, u32[]{:S(2)}) copy-start(s32[2]{0:T(128)} %param.17) | copy-start | bytes 28
  101.5 31.3 %copy-start.4 = (bf16[256,64]{0,1:T(8,128)(2,1)S(1)}, bf16[256,64]{0,1:T(8,128)(2,1)}, u32[]{:S(2)}) copy-start(bf16[256,64]{0,1:T(8,128)(2,1)} %param.18) | copy-start | bytes 98308
  101.6 2.7 %copy-start.3 = (s32[256]{0:T(256)S(1)}, s32[256]{0:T(256)}, u32[]{:S(2)}) copy-start(s32[256]{0:T(256)} %get-tuple-element.736) | copy-start | bytes 3076 | tf_op jit(solution)/shard_map/while
  109.2 2.7 %copy-start.3 = (s32[256]{0:T(256)S(1)}, s32[256]{0:T(256)}, u32[]{:S(2)}) copy-start(s32[256]{0:T(256)} %get-tuple-element.736) | copy-start | bytes 3076 | tf_op jit(solution)/shard_map/while
  116.8 2.7 %copy-start.3 = (s32[256]{0:T(256)S(1)}, s32[256]{0:T(256)}, u32[]{:S(2)}) copy-start(s32[256]{0:T(256)} %get-tuple-element.736) | copy-start | bytes 3076 | tf_op jit(solution)/shard_map/while
  124.5 2.7 %copy-start.3 = (s32[256]{0:T(256)S(1)}, s32[256]{0:T(256)}, u32[]{:S(2)}) copy-start(s32[256]{0:T(256)} %get-tuple-element.736) | copy-start | bytes 3076 | tf_op jit(solution)/shard_map/while
  132.8 1.6 copy-start.2
  191.8 16.7 %all-to-all-start.1 = ((f32[4,64,1024]{2,1,0:T(8,128)}), f32[4,64,1024]{2,1,0:T(8,128)}, u32[]{:S(2)}, u32[]{:S(2)}) async-start(f32[4,64,1024]{2,1,0:T(8,128)} %all-reduce.2.cloned.1.call-done), calls=%async_computation.1 | async-start | bytes 2097152 | tf_op jit(solution)/shard_map/all_to_all | solution.py:149
  196.1 31.6 %reduce-scatter.4.cloned.1.call-start = ((), (), s32[]{:S(2)}) async-start(), calls=%async_computation.4 | async-start | bytes 163840
Sparse Core Ops, SparseCore 0:
  134.5 57.1 all-reduce.1
Sparse Core Ops, SparseCore 1:
  204.1 23.4 reduce-scatter.3
where the time goes:
time: 236 us; the launch traced here: 235 us
  matrix products  58.7 us (25%)
  blocking collectives  57.1 us (24%)
  other arithmetic  40.2 us (17%)
  waiting for transfers between devices  34.6 us (15%)
  local copies, waits for them, and re-layouts  24.1 us (10%)
  between operations  15.7 us (7%)
  starting transfers between devices  4.34 us (2%)
    unnamed x5, other arithmetic  23.6 us
    dot_general x4, matrix products, backward_update(): jnp.dot(grad_scores, key_block, preferred_element_type=jnp.float32)  19.3 us
    unnamed x3, waiting for transfers between devices  17.1 us
    all_gather x1, blocking collectives, on_device(): lax.all_gather(my_keys, 'ctx', axis=0, tiled=True)  16.6 us
    all_gather x1, blocking collectives, on_device(): lax.all_gather(my_values, 'ctx', axis=0, tiled=True)  15.8 us
    dot_general x4, matrix products, forward_update(): jnp.dot(weights_f.astype(jnp.bfloat16), value_block, preferred_element_ty...  15.4 us
    psum x1, waiting for transfers between devices, on_device(): summed_all = lax.psum(tenant_contributions, 'ctx')  13.9 us
    reduce_sum x4, other arithmetic, forward_update(): row_total = row_total * decay_factor + jnp.sum(weights_f, axis=1)  13.2 us
  transfers between devices with their start and end apart: 3, of which 3 were waited for; matrix products, arithmetic and copies ran while one was open for 18% of the time, Pallas kernels for 0%

commit v1 on v0

v1 whole, which is shorter than its diff:
```python
import functools

import jax
import jax.numpy as jnp
from jax import lax
from jax.experimental import pallas as pl
from jax.experimental.pallas import tpu as pltpu
from jax.sharding import PartitionSpec as P

QH = 32
KVH = 4
HD = 128
RANK = 64
BLOCK = 128
CORES = 2
PAD = 16

adapter_scale_factor = 2.0
far_below = -1e30
logit_scale = HD ** (-0.5)
log2_scale = logit_scale * 1.4426950408889634

VMEM = pl.BlockSpec(memory_space=pltpu.VMEM)
SMEM = pl.BlockSpec(memory_space=pltpu.SMEM)
BF16 = jnp.bfloat16
F32 = jnp.float32


def pack_kernel(place, key_ref, value_ref, doc_ref, *refs):
    n = (len(refs) - 2) // 2
    b_refs, message, doc_column, b_outs = refs[:n], refs[n], refs[n + 1], refs[n + 2 :]
    tokens = key_ref.shape[0]
    message[:tokens, :HD] = key_ref[...]
    message[:tokens, HD:] = value_ref[...]
    docs = doc_ref[...].astype(F32)
    message[tokens:, :] = jnp.broadcast_to(docs, (PAD, tokens)).astype(BF16)
    row = lax.broadcasted_iota(jnp.int32, (tokens, tokens), 0)
    lane = lax.broadcasted_iota(jnp.int32, (tokens, tokens), 1)
    column = jnp.sum(jnp.where(row == lane, docs, 0.0), axis=1, keepdims=True)
    doc_column[...] = jnp.broadcast_to(column, doc_column.shape)
    for b_ref, b_out in zip(b_refs, b_outs):
        b_out[...] = b_ref[0]


def pack(place, keys, values, docs, adapter_b, owners, heads_dev):
    tokens = keys.shape[0]
    width = heads_dev * HD
    kv = lambda place: place[2] * heads_dev // (QH // KVH)
    return pl.pallas_call(
        pack_kernel,
        grid_spec=pltpu.PrefetchScalarGridSpec(
            num_scalar_prefetch=1,
            grid=(1,),
            in_specs=[
                pl.BlockSpec((tokens, HD), lambda i, place: (0, kv(place))),
                pl.BlockSpec((tokens, HD), lambda i, place: (0, kv(place))),
                pl.BlockSpec((1, tokens), lambda i, place: (0, 0)),
            ]
            + [
                pl.BlockSpec(
                    (1, RANK, width), lambda i, place, s=s: (0, 0, lax.rem(place[2] + s, owners))
                )
                for s in range(owners)
            ],
            out_specs=[
                pl.BlockSpec((tokens + PAD, 2 * HD), lambda i, place: (0, 0)),
                pl.BlockSpec((tokens, 128), lambda i, place: (0, 0)),
            ]
            + [pl.BlockSpec((RANK, width), lambda i, place: (0, 0))] * owners,
        ),
        out_shape=[
            jax.ShapeDtypeStruct((tokens + PAD, 2 * HD), BF16),
            jax.ShapeDtypeStruct((tokens, 128), F32),
        ]
        + [jax.ShapeDtypeStruct((RANK, width), BF16)] * owners,
        cost_estimate=pl.CostEstimate(flops=0, bytes_accessed=2 << 20, transcendentals=0),
        name="pack",
    )(place, keys, values, docs.reshape(1, tokens), *([adapter_b] * owners))


def lanes(x, times):
    return jnp.concatenate([x] * times, axis=1)


def attend_kernel(chips, owners, place, tenant, *refs):
    refs = list(refs)
    take = lambda count: [refs.pop(0) for _ in range(count)]
    (q_ref, g_ref, doc_column, low_ref) = take(4)
    own, other = take(chips), take(chips)
    b_refs = take(owners)
    (dq_ref,) = take(1)
    rank_outs = take(owners)
    mine_ref, partner_ref = take(2)
    top, by_key, by_grad, bias, chosen, rank_all = take(6)
    tokens, width = q_ref.shape
    heads = width // HD
    z, core, adp = place[0], place[1], place[2]
    doc_row = lambda ref: ref[tokens : tokens + PAD, :][:1].astype(F32)
    first_doc = jnp.min(doc_row(own[0]))
    query_doc = lanes(doc_column[...], 2 * tokens // 128)

    def step(shift):
        keys = jnp.concatenate([own[shift][:tokens, :HD], other[shift][:tokens, :HD]], axis=0)
        values = jnp.concatenate([own[shift][:tokens, HD:], other[shift][:tokens, HD:]], axis=0)
        extended = jnp.concatenate([keys, jnp.ones((2 * tokens, HD), BF16)], axis=1)
        other_doc = doc_row(other[shift])
        if shift == 0:
            other_doc = jnp.where(core == 1, other_doc, -1.0)
        visible = jnp.concatenate([doc_row(own[shift]), other_doc], axis=1) == query_doc
        if shift == 0:
            row = lax.broadcasted_iota(jnp.int32, (tokens, 2 * tokens), 0)
            lane = lax.broadcasted_iota(jnp.int32, (tokens, 2 * tokens), 1)
            visible = visible & ((lane <= row) | (lane >= tokens))
        bias[...] = jnp.where(visible, 0.0, far_below)
        for h in range(heads):
            columns = slice(h * HD, (h + 1) * HD)
            scores = (
                lax.dot_general(
                    q_ref[:, columns], keys, (((1,), (1,)), ((), ())), preferred_element_type=F32
                )
                + bias[...]
            )
            block_top = jnp.broadcast_to(jnp.max(scores, axis=1, keepdims=True), (tokens, 128))
            new_top = block_top if shift == 0 else jnp.maximum(top[h], block_top)
            p = jnp.exp2((scores - lanes(new_top, 2 * tokens // 128)) * log2_scale)
            grads = lax.dot_general(
                g_ref[:, columns], values, (((1,), (1,)), ((), ())), preferred_element_type=F32
            )
            key_sum = jnp.dot(p.astype(BF16), extended, preferred_element_type=F32)
            grad_sum = jnp.dot((p * grads).astype(BF16), extended, preferred_element_type=F32)
            if shift:
                decay = lanes(jnp.exp2((top[h] - new_top) * log2_scale), 2)
                key_sum = key_sum + by_key[h] * decay
                grad_sum = grad_sum + by_grad[h] * decay
            top[h] = new_top
            by_key[h] = key_sum
            by_grad[h] = grad_sum

    step(0)
    for shift in range(1, chips):
        latest = jnp.maximum(jnp.max(doc_row(own[shift])), jnp.max(doc_row(other[shift])))
        pl.when((z >= shift) & (latest == first_doc))(functools.partial(step, shift))

    for h in range(heads):
        columns = slice(h * HD, (h + 1) * HD)
        inverse = 1.0 / by_key[h, :, HD:]
        delta = by_grad[h, :, HD:] * inverse
        dq = (by_grad[h, :, :HD] - delta * by_key[h, :, :HD]) * (inverse * logit_scale)
        dq_ref[:, columns] = dq.astype(BF16)

    half = width // CORES
    for block in range(tokens // BLOCK):
        rows = slice(block * BLOCK, (block + 1) * BLOCK)
        holder = lax.rem(adp - tenant[block] + owners, owners)
        for s in range(owners):

            @pl.when(holder == s)
            def _(s=s):
                chosen[...] = b_refs[s][...]

        rank_all[rows, :] = adapter_scale_factor * lax.dot_general(
            dq_ref[rows, :], chosen[...], (((1,), (1,)), ((), ())), preferred_element_type=F32
        )
        partial = adapter_scale_factor * lax.dot_general(
            low_ref[rows, :], dq_ref[rows, :], (((0,), (0,)), ((), ())), preferred_element_type=F32
        )
        out_rows = slice(block * RANK, (block + 1) * RANK)
        mine_ref[out_rows, :] = jnp.where(core == 0, partial[:, :half], partial[:, half:])
        partner_ref[out_rows, :] = jnp.where(
            core == 0, partial[:, half:], partial[:, :half]
        ).astype(BF16)
    share = tokens // owners
    for s in range(owners):
        start = pl.multiple_of(lax.rem(adp + s, owners) * share, share)
        rank_outs[s][...] = rank_all[pl.ds(start, share), :]


def attend(place, block_tenant, queries, grad_out, doc_column, low_rank, own, other, b_cols):
    tokens, width = queries.shape
    heads = width // HD
    chips, owners = len(own), len(b_cols)
    blocks = tokens // BLOCK
    share = tokens // owners
    inputs = [queries, grad_out, doc_column, low_rank, *own, *other, *b_cols]
    return pl.pallas_call(
        functools.partial(attend_kernel, chips, owners),
        in_specs=[SMEM, SMEM] + [VMEM] * len(inputs),
        out_specs=[VMEM] * (3 + owners),
        out_shape=[jax.ShapeDtypeStruct((tokens, width), BF16)]
        + [jax.ShapeDtypeStruct((share, RANK), F32)] * owners
        + [
            jax.ShapeDtypeStruct((blocks * RANK, width // CORES), F32),
            jax.ShapeDtypeStruct((blocks * RANK, width // CORES), BF16),
        ],
        scratch_shapes=[
            pltpu.VMEM((heads, tokens, 128), F32),
            pltpu.VMEM((heads, tokens, 2 * HD), F32),
            pltpu.VMEM((heads, tokens, 2 * HD), F32),
            pltpu.VMEM((tokens, 2 * tokens), F32),
            pltpu.VMEM((RANK, width), BF16),
            pltpu.VMEM((tokens, RANK), F32),
        ],
        compiler_params=pltpu.CompilerParams(vmem_limit_bytes=40 << 20),
        cost_estimate=pl.CostEstimate(
            flops=chips * 12 * tokens * tokens * width, bytes_accessed=4 << 20, transcendentals=0
        ),
        name="attend",
    )(place, block_tenant, *inputs)


def tenants_kernel(owners, place, tenant, other_tenant, mine_ref, other_ref, *outs):
    blocks = mine_ref.shape[0] // RANK
    z, adp = place[0], place[2]
    for s in range(owners):
        owner = lax.rem(adp + z + s, owners)
        total = None
        for block in range(blocks):
            rows = slice(block * RANK, (block + 1) * RANK)
            term = jnp.where(tenant[block] == owner, mine_ref[rows, :], 0.0)
            total = term if total is None else total + term
            total = total + jnp.where(
                other_tenant[block] == owner, other_ref[rows, :].astype(F32), 0.0
            )
        outs[s][...] = total.astype(BF16)


def by_tenant(place, tenant, other_tenant, mine, other, owners):
    return pl.pallas_call(
        functools.partial(tenants_kernel, owners),
        in_specs=[SMEM] * 3 + [VMEM] * 2,
        out_specs=[VMEM] * owners,
        out_shape=[jax.ShapeDtypeStruct((RANK, mine.shape[1]), BF16)] * owners,
        cost_estimate=pl.CostEstimate(flops=0, bytes_accessed=1 << 20, transcendentals=0),
        name="by_tenant",
    )(place, tenant, other_tenant, mine, other)


def on_device(queries, keys, values, grad_out, docs, block_tenant, low_rank, adapter_b):
    positions, owners = lax.axis_size("ctx"), lax.axis_size("adp")
    chips = positions // CORES
    heads_dev = queries.shape[1] // HD
    ctx, adp = lax.axis_index("ctx"), lax.axis_index("adp")
    place = jnp.stack([ctx // CORES, ctx % CORES, adp]).astype(jnp.int32)
    swap = [(c, c ^ 1) for c in range(positions)]
    up = lambda s: [(c, (c + CORES * s) % positions) for c in range(positions)]
    along = lambda s: [(a, (a + s) % owners) for a in range(owners)]

    message, doc_column, *b_out = pack(
        place, keys, values, docs, adapter_b, owners, heads_dev
    )
    own = [message] + [lax.ppermute(message, "ctx", up(s)) for s in range(1, chips)]
    other = [lax.ppermute(m, "ctx", swap) for m in own]
    other_tenant = lax.ppermute(block_tenant, "ctx", swap)
    b_cols = [b_out[0]] + [lax.ppermute(b_out[s], "adp", along(s)) for s in range(1, owners)]

    grad_queries, *ranks, mine, partner = attend(
        place, block_tenant, queries, grad_out, doc_column, low_rank, own, other, b_cols
    )
    other_part = lax.ppermute(partner, "ctx", swap)
    pieces = by_tenant(place, block_tenant, other_tenant, mine, other_part, owners)

    def sideways(s):
        return [
            ((CORES * z + k) * owners + a, (CORES * z + k) * owners + (a + z + s) % owners)
            for z in range(chips)
            for k in range(CORES)
            for a in range(owners)
        ]

    def upright(s):
        return [
            ((CORES * z + k) * owners + t, (CORES * ((t - z - s) % owners) + k) * owners + t)
            for z in range(chips)
            for k in range(CORES)
            for t in range(owners)
        ]

    both = ("ctx", "adp")
    moved = [lax.ppermute(piece, both, sideways(s)) for s, piece in enumerate(pieces)]
    moved = [lax.ppermute(piece, both, upright(s)) for s, piece in enumerate(moved)]
    grad_adapter = sum(piece.astype(F32) for piece in moved)[None]
    ranks = [ranks[0]] + [lax.ppermute(ranks[s], "adp", along(s)) for s in range(1, owners)]
    return grad_queries, sum(ranks), grad_adapter


def solution(mesh):
    placed = (
        P("ctx", "adp"),
        P("ctx", None),
        P("ctx", None),
        P("ctx", "adp"),
        P("ctx"),
        P("ctx"),
        P("ctx", None),
        P("adp", None, None),
    )
    return jax.shard_map(
        on_device,
        mesh=mesh,
        in_specs=placed,
        out_specs=(P("ctx", "adp"), P(("ctx", "adp"), None), P("adp", None, "ctx")),
        check_vma=False,
    )
```

time: 236 us -> 90.4 us (0.38)
  matrix products: 58.7 us -> 0 us
  blocking collectives: 57.1 us -> 0 us
  starting transfers between devices: 4.34 us -> 53.6 us
  other arithmetic: 40.2 us -> 1.97 us
  local copies, waits for them, and re-layouts: 24.1 us -> 4.82 us
  waiting for transfers between devices: 34.6 us -> 18.4 us
  between operations: 15.7 us -> 0.81 us
  Pallas kernels: 0 us -> 10.2 us
    dot_general x18 -> x0, matrix products: 58.7 us -> none  [the longest x4 19.3 us: backward_update(): jnp.dot(grad_scores, key_block, preferred_element_type=jnp.float32)]
    ppermute x0 -> x23, starting transfers between devices: none -> 53.6 us  [the longest x4 25.1 us: on_device(): lax.ppermute(piece, both, upright(s))]
    all_gather x3 -> x0, blocking collectives: 44.5 us -> none  [the longest x1 16.6 us: on_device(): lax.all_gather(my_keys, 'ctx', axis=0, tiled=True)]
    unnamed x5 -> x0, other arithmetic: 23.6 us -> none
    ppermute x0 -> x23, waiting for transfers between devices: none -> 18.4 us  [the longest x3 6.35 us: on_device(): lax.ppermute(b_out[s], 'adp', along(s))]
    unnamed x3 -> x0, waiting for transfers between devices: 17.1 us -> none
    reduce_sum x6 -> x0, other arithmetic: 15.3 us -> none  [the longest x4 13.2 us: forward_update(): row_total = row_total * decay_factor + jnp.sum(weights_f, axis=1)]
    psum x1 -> x0, waiting for transfers between devices: 13.9 us -> none  [on_device(): summed_all = lax.psum(tenant_contributions, 'ctx')]
  transfers between devices with their start and end apart: 3 -> 23, of which waited for: 3 -> 8; matrix products, arithmetic and copies ran while one was open for 18% -> 1% of each run, Pallas kernels for 0% -> 0%
where the time goes in v1:
time: 90.4 us; the launch traced here: 89.9 us
  starting transfers between devices  53.6 us (59%)
  waiting for transfers between devices  18.4 us (20%)
  Pallas kernels  10.2 us (11%)
  local copies, waits for them, and re-layouts  4.82 us (5%)
  other arithmetic  1.97 us (2%)
    ppermute x4, starting transfers between devices, on_device(): lax.ppermute(piece, both, upright(s))  25.1 us
    ppermute x4, starting transfers between devices, on_device(): lax.ppermute(piece, both, sideways(s))  11.6 us
    ppermute x3, starting transfers between devices, on_device(): lax.ppermute(message, 'ctx', up(s))  6.96 us
    ppermute x3, waiting for transfers between devices, on_device(): lax.ppermute(b_out[s], 'adp', along(s))  6.35 us
    ppermute x3, waiting for transfers between devices, on_device(): lax.ppermute(ranks[s], 'adp', along(s))  6.31 us
    pallas_call x1, Pallas kernels, attend(): pl.pallas_call(functools.partial(attend_kernel, chips, owners), in_specs=...  5.57 us
    ppermute x3, starting transfers between devices, on_device(): lax.ppermute(b_out[s], 'adp', along(s))  5.46 us
    unnamed x23, local copies, waits for them, and re-layouts  4.82 us
  transfers between devices with their start and end apart: 23, of which 8 were waited for; matrix products, arithmetic and copies ran while one was open for 1% of the time, Pallas kernels for 0%

profile of v1, /device:TPU:0, one launch (start us, length us, event | category | flops | bytes accessed | tf_op | source)
XLA Modules:
  0.0 89.9 jit_solution(8930800157214286083)
XLA Ops:
  0.6 0.7 pad_add_fusion.place
  1.3 2.9 %pack.1 = (bf16[272,256]{1,0:T(8,128)(2,1)}, f32[256,128]{1,0:T(8,128)}, bf16[64,1024]{1,0:T(8,128)(2,1)}, bf16[64,1024]{1,0:T(8,128)(2,1)}, bf16[64,1024]{1,0:T(8,128)(2,1)}, /*index=5*/bf16[64,1024]{1,0:T(8,128)(2,1)}) custom-call(s32[3]{0:T(128)} %pad_add_fusion.place, bf16[256,512]{1,0:T(8,128)(2,1)} %key_ref.1, bf16[256,512]{1,0:T(8,128)(2,1)} %value_ref.1, ...), custom_call_target="tpu_custom_call" | custom-call | bytes 2097152 | tf_op jit(solution)/shard_map/pack/pallas_call | solution.py:49
  4.2 3.0 %collective-permute-start = (bf16[272,256]{1,0:T(8,128)(2,1)}, bf16[272,256]{1,0:T(8,128)(2,1)S(1)}, u32[]{:S(2)}, u32[]{:S(2)}) collective-permute-start(bf16[272,256]{1,0:T(8,128)(2,1)} %get-tuple-element.21.refs_4_), channel_id=1, source_target_pairs={{0,8},{4,12},{8,16},{12,20},{16,24},{20,28},{24,0},{28,4},{1,9},{5... | collective-permute-start | bytes 417800 | tf_op jit(solution)/shard_map/ppermute | solution.py:251
  7.2 2.6 %collective-permute-start.1 = (bf16[272,256]{1,0:T(8,128)(2,1)}, bf16[272,256]{1,0:T(8,128)(2,1)S(1)}, u32[]{:S(2)}, u32[]{:S(2)}) collective-permute-start(bf16[272,256]{1,0:T(8,128)(2,1)} %get-tuple-element.21.refs_4_), channel_id=1, source_target_pairs={{0,16},{4,20},{8,24},{12,28},{16,0},{20,4},{24,8},{28,12},{1,17},{... | collective-permute-start | bytes 417800 | tf_op jit(solution)/shard_map/ppermute | solution.py:251
  9.8 1.3 %collective-permute-start.2 = (bf16[272,256]{1,0:T(8,128)(2,1)}, bf16[272,256]{1,0:T(8,128)(2,1)S(1)}, u32[]{:S(2)}, u32[]{:S(2)}) collective-permute-start(bf16[272,256]{1,0:T(8,128)(2,1)} %get-tuple-element.21.refs_4_), channel_id=1, source_target_pairs={{0,24},{4,28},{8,0},{12,4},{16,8},{20,12},{24,16},{28,20},{1,25},{... | collective-permute-start | bytes 417800 | tf_op jit(solution)/shard_map/ppermute | solution.py:251
  11.2 1.5 %collective-permute-start.7 = (bf16[64,1024]{1,0:T(8,128)(2,1)}, bf16[64,1024]{1,0:T(8,128)(2,1)S(1)}, u32[]{:S(2)}, u32[]{:S(2)}) collective-permute-start(bf16[64,1024]{1,0:T(8,128)(2,1)} %get-tuple-element.23), channel_id=1, source_target_pairs={{0,1},{1,2},{2,3},{3,0},{4,5},{5,6},{6,7},{7,4},{8,9},{9,10},{10,1... | collective-permute-start | bytes 393224 | tf_op jit(solution)/shard_map/ppermute | solution.py:254
  12.6 1.5 %collective-permute-start.8 = (bf16[64,1024]{1,0:T(8,128)(2,1)}, bf16[64,1024]{1,0:T(8,128)(2,1)S(1)}, u32[]{:S(2)}, u32[]{:S(2)}) collective-permute-start(bf16[64,1024]{1,0:T(8,128)(2,1)} %get-tuple-element.24), channel_id=1, source_target_pairs={{0,2},{1,3},{2,0},{3,1},{4,6},{5,7},{6,4},{7,5},{8,10},{9,11},{10,... | collective-permute-start | bytes 393224 | tf_op jit(solution)/shard_map/ppermute | solution.py:254
  14.2 3.2 %collective-permute-done.7.refs_13_ = bf16[64,1024]{1,0:T(8,128)(2,1)S(1)} collective-permute-done((bf16[64,1024]{1,0:T(8,128)(2,1)}, bf16[64,1024]{1,0:T(8,128)(2,1)S(1)}, u32[]{:S(2)}, u32[]{:S(2)}) %collective-permute-start.7) | collective-permute-done | bytes 131104 | tf_op jit(solution)/shard_map/ppermute | solution.py:254
  17.3 0.5 collective-permute-start.4
  17.9 1.3 %collective-permute-done.1.refs_6_ = bf16[272,256]{1,0:T(8,128)(2,1)S(1)} collective-permute-done((bf16[272,256]{1,0:T(8,128)(2,1)}, bf16[272,256]{1,0:T(8,128)(2,1)S(1)}, u32[]{:S(2)}, u32[]{:S(2)}) %collective-permute-start.1) | collective-permute-done | bytes 139296 | tf_op jit(solution)/shard_map/ppermute | solution.py:251
  19.2 0.0 collective-permute-start.5
  19.2 0.0 collective-permute-done.2.refs_7_
  19.2 0.5 collective-permute-start.6
  19.7 2.4 %collective-permute-start.9 = (bf16[64,1024]{1,0:T(8,128)(2,1)}, bf16[64,1024]{1,0:T(8,128)(2,1)S(1)}, u32[]{:S(2)}, u32[]{:S(2)}) collective-permute-start(bf16[64,1024]{1,0:T(8,128)(2,1)} %get-tuple-element.25), channel_id=1, source_target_pairs={{0,3},{1,0},{2,1},{3,2},{4,7},{5,4},{6,5},{7,6},{8,11},{9,8},{10,9... | collective-permute-start | bytes 393224 | tf_op jit(solution)/shard_map/ppermute | solution.py:254
  22.1 0.1 copy.11.refs_3_
  22.3 3.2 %collective-permute-done.9.refs_15_ = bf16[64,1024]{1,0:T(8,128)(2,1)S(1)} collective-permute-done((bf16[64,1024]{1,0:T(8,128)(2,1)}, bf16[64,1024]{1,0:T(8,128)(2,1)S(1)}, u32[]{:S(2)}, u32[]{:S(2)}) %collective-permute-start.9) | collective-permute-done | bytes 131104 | tf_op jit(solution)/shard_map/ppermute | solution.py:254
  25.4 0.0 collective-permute-done.3.refs_8_
  25.4 0.0 collective-permute-done.4.refs_9_
  25.4 0.0 collective-permute-done.5.refs_10_
  25.5 0.0 copy-start.2
  25.5 0.6 copy-done.1
  26.1 0.9 %copy-done.5 = bf16[272,256]{1,0:T(8,128)(2,1)S(1)} copy-done((bf16[272,256]{1,0:T(8,128)(2,1)S(1)}, bf16[272,256]{1,0:T(8,128)(2,1)}, u32[]{:S(2)}) %copy-start.5) | copy-done | bytes 139288
  27.0 0.9 %copy-done.6 = f32[256,128]{1,0:T(8,128)S(1)} copy-done((f32[256,128]{1,0:T(8,128)S(1)}, f32[256,128]{1,0:T(8,128)}, u32[]{:S(2)}) %copy-start.6) | copy-done | bytes 131096
  27.9 0.9 %copy-done.7 = bf16[64,1024]{1,0:T(8,128)(2,1)S(1)} copy-done((bf16[64,1024]{1,0:T(8,128)(2,1)S(1)}, bf16[64,1024]{1,0:T(8,128)(2,1)}, u32[]{:S(2)}) %copy-start.7) | copy-done | bytes 131096
  28.9 5.6 %attend.1 = (bf16[256,1024]{1,0:T(8,128)(2,1)}, f32[64,64]{1,0:T(8,128)S(1)}, f32[64,64]{1,0:T(8,128)S(1)}, f32[64,64]{1,0:T(8,128)S(1)}, f32[64,64]{1,0:T(8,128...) custom-call(s32[3]{0:T(128)S(1)} %copy-done.1, s32[2]{0:T(128)S(1)} %copy-done.2, ...), custom_call_target="tpu_custom_call" | custom-call | flops 3221225472 | bytes 4194304 | tf_op jit(solution)/shard_map/attend/pallas_call | solution.py:185
  34.4 0.7 copy-done
  35.1 0.5 collective-permute-start.13
  35.6 0.8 collective-permute-done.13.other_tenant
  36.5 0.5 copy-done.10
  37.0 0.2 copy-done.8
  37.1 1.8 %by_tenant.1 = (bf16[64,512]{1,0:T(8,128)(2,1)}, bf16[64,512]{1,0:T(8,128)(2,1)}, bf16[64,512]{1,0:T(8,128)(2,1)}, bf16[64,512]{1,0:T(8,128)(2,1)}) custom-call(s32[3]{0:T(128)} %pad_add_fusion.place, s32[2]{0:T(128)} %tenant.3, s32[2]{0:T(128)} %copy-done.10, f32[128,512]{1,0:T(8,128)} %copy-done, bf16[128,512]{1,0:T(8,128)(2,1)} %copy-done.8), custom_call_target="tpu_custom_call" | custom-call | bytes 1048576 | tf_op jit(solution)/shard_map/by_tenant/pallas_call | solution.py:228
  38.9 1.5 %collective-permute-start.15 = (bf16[64,512]{1,0:T(8,128)(2,1)}, bf16[64,512]{1,0:T(8,128)(2,1)S(1)}, u32[]{:S(2)}, u32[]{:S(2)}) collective-permute-start(bf16[64,512]{1,0:T(8,128)(2,1)} %get-tuple-element.33), channel_id=1, source_target_pairs={{0,0},{1,1},{2,2},{3,3},{4,4},{5,5},{6,6},{7,7},{8,9},{9,10},{10,1... | collective-permute-start | bytes 196616 | tf_op jit(solution)/shard_map/ppermute | solution.py:279
  40.4 4.2 %collective-permute-start.17 = (bf16[64,512]{1,0:T(8,128)(2,1)}, bf16[64,512]{1,0:T(8,128)(2,1)S(1)}, u32[]{:S(2)}, u32[]{:S(2)}) collective-permute-start(bf16[64,512]{1,0:T(8,128)(2,1)} %get-tuple-element.34), channel_id=1, source_target_pairs={{0,1},{1,2},{2,3},{3,0},{4,5},{5,6},{6,7},{7,4},{8,10},{9,11},{10,... | collective-permute-start | bytes 196616 | tf_op jit(solution)/shard_map/ppermute | solution.py:279
  44.6 3.4 %collective-permute-start.19 = (bf16[64,512]{1,0:T(8,128)(2,1)}, bf16[64,512]{1,0:T(8,128)(2,1)S(1)}, u32[]{:S(2)}, u32[]{:S(2)}) collective-permute-start(bf16[64,512]{1,0:T(8,128)(2,1)} %get-tuple-element.35), channel_id=1, source_target_pairs={{0,2},{1,3},{2,0},{3,1},{4,6},{5,7},{6,4},{7,5},{8,11},{9,8},{10,9... | collective-permute-start | bytes 196616 | tf_op jit(solution)/shard_map/ppermute | solution.py:279
  48.1 2.4 %collective-permute-start.21 = (bf16[64,512]{1,0:T(8,128)(2,1)}, bf16[64,512]{1,0:T(8,128)(2,1)S(1)}, u32[]{:S(2)}, u32[]{:S(2)}) collective-permute-start(bf16[64,512]{1,0:T(8,128)(2,1)} %get-tuple-element.36), channel_id=1, source_target_pairs={{0,3},{1,0},{2,1},{3,2},{4,7},{5,4},{6,5},{7,6},{8,8},{9,9},{10,10... | collective-permute-start | bytes 196616 | tf_op jit(solution)/shard_map/ppermute | solution.py:279
  50.5 1.5 %collective-permute-start.10 = (f32[64,64]{1,0:T(8,128)S(1)}, f32[64,64]{1,0:T(8,128)S(1)}, u32[]{:S(2)}, u32[]{:S(2)}) collective-permute-start(f32[64,64]{1,0:T(8,128)S(1)} %get-tuple-element.28), channel_id=1, source_target_pairs={{0,1},{1,2},{2,3},{3,0},{4,5},{5,6},{6,7},{7,4},{8,9},{9,10},{10,1... | collective-permute-start | bytes 49160 | tf_op jit(solution)/shard_map/ppermute | solution.py:282
  52.1 3.3 %collective-permute-done.10 = f32[64,64]{1,0:T(8,128)S(1)} collective-permute-done((f32[64,64]{1,0:T(8,128)S(1)}, f32[64,64]{1,0:T(8,128)S(1)}, u32[]{:S(2)}, u32[]{:S(2)}) %collective-permute-start.10) | collective-permute-done | bytes 16416 | tf_op jit(solution)/shard_map/ppermute | solution.py:282
  55.4 0.9 %collective-permute-start.11 = (f32[64,64]{1,0:T(8,128)S(1)}, f32[64,64]{1,0:T(8,128)S(1)}, u32[]{:S(2)}, u32[]{:S(2)}) collective-permute-start(f32[64,64]{1,0:T(8,128)S(1)} %get-tuple-element.29), channel_id=1, source_target_pairs={{0,2},{1,3},{2,0},{3,1},{4,6},{5,7},{6,4},{7,5},{8,10},{9,11},{10,... | collective-permute-start | bytes 49160 | tf_op jit(solution)/shard_map/ppermute | solution.py:282
  56.3 3.0 %collective-permute-done.11 = f32[64,64]{1,0:T(8,128)S(1)} collective-permute-done((f32[64,64]{1,0:T(8,128)S(1)}, f32[64,64]{1,0:T(8,128)S(1)}, u32[]{:S(2)}, u32[]{:S(2)}) %collective-permute-start.11) | collective-permute-done | bytes 16416 | tf_op jit(solution)/shard_map/ppermute | solution.py:282
  59.3 0.5 collective-permute-start.12
  59.8 0.7 collective-permute-start.16
  60.5 18.6 %collective-permute-start.18 = (bf16[64,512]{1,0:T(8,128)(2,1)S(1)}, bf16[64,512]{1,0:T(8,128)(2,1)S(1)}, u32[]{:S(2)}, u32[]{:S(2)}) collective-permute-start(bf16[64,512]{1,0:T(8,128)(2,1)S(1)} %collective-permute-done.17), channel_id=1, source_target_pairs={{0,24},{1,1},{2,10},{3,19},{4,28},{5,5},{6,14},{7,23},{8,16},{9,25... | collective-permute-start | bytes 196616 | tf_op jit(solution)/shard_map/ppermute | solution.py:280
  79.1 3.9 %collective-permute-start.20 = (bf16[64,512]{1,0:T(8,128)(2,1)S(1)}, bf16[64,512]{1,0:T(8,128)(2,1)S(1)}, u32[]{:S(2)}, u32[]{:S(2)}) collective-permute-start(bf16[64,512]{1,0:T(8,128)(2,1)S(1)} %collective-permute-done.19), channel_id=1, source_target_pairs={{0,16},{1,25},{2,2},{3,11},{4,20},{5,29},{6,6},{7,15},{8,8},{9,17}... | collective-permute-start | bytes 196616 | tf_op jit(solution)/shard_map/ppermute | solution.py:280
  83.0 1.9 %collective-permute-start.22 = (bf16[64,512]{1,0:T(8,128)(2,1)S(1)}, bf16[64,512]{1,0:T(8,128)(2,1)S(1)}, u32[]{:S(2)}, u32[]{:S(2)}) collective-permute-start(bf16[64,512]{1,0:T(8,128)(2,1)S(1)} %collective-permute-done.21), channel_id=1, source_target_pairs={{0,8},{1,17},{2,26},{3,3},{4,12},{5,21},{6,30},{7,7},{8,0},{9,9},{... | collective-permute-start | bytes 196616 | tf_op jit(solution)/shard_map/ppermute | solution.py:280
  85.0 0.6 add_add_fusion
  85.6 0.5 collective-permute-done.20
  86.2 3.0 %collective-permute-done.22 = bf16[64,512]{1,0:T(8,128)(2,1)S(1)} collective-permute-done((bf16[64,512]{1,0:T(8,128)(2,1)S(1)}, bf16[64,512]{1,0:T(8,128)(2,1)S(1)}, u32[]{:S(2)}, u32[]{:S(2)}) %collective-permute-start.22) | collective-permute-done | bytes 65568 | tf_op jit(solution)/shard_map/ppermute | solution.py:280
  89.2 0.7 add_bitcast_fusion
  (27 shorter events, 0.1 us)
Async XLA Ops:
  1.3 20.8 %copy-start.9 = (bf16[256,64]{0,1:T(8,128)(2,1)S(1)}, bf16[256,64]{0,1:T(8,128)(2,1)}, u32[]{:S(2)}) copy-start(bf16[256,64]{0,1:T(8,128)(2,1)} %param.14) | copy-start | bytes 98308
  1.3 24.2 %copy-start.3 = (bf16[256,1024]{1,0:T(8,128)(2,1)S(1)}, bf16[256,1024]{1,0:T(8,128)(2,1)}, u32[]{:S(2)}) copy-start(bf16[256,1024]{1,0:T(8,128)(2,1)} %refs_0_.3) | copy-start | bytes 1572868
  1.3 24.2 %copy-start.4 = (bf16[256,1024]{1,0:T(8,128)(2,1)S(1)}, bf16[256,1024]{1,0:T(8,128)(2,1)}, u32[]{:S(2)}) copy-start(bf16[256,1024]{1,0:T(8,128)(2,1)} %refs_1_.3) | copy-start | bytes 1572868
  4.2 13.2 %collective-permute-start = (bf16[272,256]{1,0:T(8,128)(2,1)}, bf16[272,256]{1,0:T(8,128)(2,1)S(1)}, u32[]{:S(2)}, u32[]{:S(2)}) collective-permute-start(bf16[272,256]{1,0:T(8,128)(2,1)} %get-tuple-element.21.refs_4_), channel_id=1, source_target_pairs={{0,8},{4,12},{8,16},{12,20},{16,24},{20,28},{24,0},{28,4},{1,9},{5... | collective-permute-start | bytes 417800 | tf_op jit(solution)/shard_map/ppermute | solution.py:251
  7.2 12.0 %collective-permute-start.1 = (bf16[272,256]{1,0:T(8,128)(2,1)}, bf16[272,256]{1,0:T(8,128)(2,1)S(1)}, u32[]{:S(2)}, u32[]{:S(2)}) collective-permute-start(bf16[272,256]{1,0:T(8,128)(2,1)} %get-tuple-element.21.refs_4_), channel_id=1, source_target_pairs={{0,16},{4,20},{8,24},{12,28},{16,0},{20,4},{24,8},{28,12},{1,17},{... | collective-permute-start | bytes 417800 | tf_op jit(solution)/shard_map/ppermute | solution.py:251
  9.8 9.4 %collective-permute-start.2 = (bf16[272,256]{1,0:T(8,128)(2,1)}, bf16[272,256]{1,0:T(8,128)(2,1)S(1)}, u32[]{:S(2)}, u32[]{:S(2)}) collective-permute-start(bf16[272,256]{1,0:T(8,128)(2,1)} %get-tuple-element.21.refs_4_), channel_id=1, source_target_pairs={{0,24},{4,28},{8,0},{12,4},{16,8},{20,12},{24,16},{28,20},{1,25},{... | collective-permute-start | bytes 417800 | tf_op jit(solution)/shard_map/ppermute | solution.py:251
  11.2 6.2 %collective-permute-start.7 = (bf16[64,1024]{1,0:T(8,128)(2,1)}, bf16[64,1024]{1,0:T(8,128)(2,1)S(1)}, u32[]{:S(2)}, u32[]{:S(2)}) collective-permute-start(bf16[64,1024]{1,0:T(8,128)(2,1)} %get-tuple-element.23), channel_id=1, source_target_pairs={{0,1},{1,2},{2,3},{3,0},{4,5},{5,6},{6,7},{7,4},{8,9},{9,10},{10,1... | collective-permute-start | bytes 393224 | tf_op jit(solution)/shard_map/ppermute | solution.py:254
  12.6 7.1 %collective-permute-start.8 = (bf16[64,1024]{1,0:T(8,128)(2,1)}, bf16[64,1024]{1,0:T(8,128)(2,1)S(1)}, u32[]{:S(2)}, u32[]{:S(2)}) collective-permute-start(bf16[64,1024]{1,0:T(8,128)(2,1)} %get-tuple-element.24), channel_id=1, source_target_pairs={{0,2},{1,3},{2,0},{3,1},{4,6},{5,7},{6,4},{7,5},{8,10},{9,11},{10,... | collective-permute-start | bytes 393224 | tf_op jit(solution)/shard_map/ppermute | solution.py:254
  17.3 8.1 %collective-permute-start.3 = (bf16[272,256]{1,0:T(8,128)(2,1)}, bf16[272,256]{1,0:T(8,128)(2,1)S(1)}, u32[]{:S(2)}, u32[]{:S(2)}) collective-permute-start(bf16[272,256]{1,0:T(8,128)(2,1)} %get-tuple-element.21.refs_4_), channel_id=1, source_target_pairs={{0,4},{4,0},{8,12},{12,8},{16,20},{20,16},{24,28},{28,24},{1,5},{5... | collective-permute-start | bytes 417800 | tf_op jit(solution)/shard_map/ppermute | solution.py:252
  17.3 8.1 %collective-permute-start.4 = (bf16[272,256]{1,0:T(8,128)(2,1)S(1)}, bf16[272,256]{1,0:T(8,128)(2,1)S(1)}, u32[]{:S(2)}, u32[]{:S(2)}) collective-permute-start(bf16[272,256]{1,0:T(8,128)(2,1)S(1)} %collective-permute-done.refs_5_), channel_id=1, source_target_pairs={{0,4},{4,0},{8,12},{12,8},{16,20},{20,16},{24,28},{28,24},{1,5},{5... | collective-permute-start | bytes 417800 | tf_op jit(solution)/shard_map/ppermute | solution.py:252
  19.2 6.3 %collective-permute-start.5 = (bf16[272,256]{1,0:T(8,128)(2,1)S(1)}, bf16[272,256]{1,0:T(8,128)(2,1)S(1)}, u32[]{:S(2)}, u32[]{:S(2)}) collective-permute-start(bf16[272,256]{1,0:T(8,128)(2,1)S(1)} %collective-permute-done.1.refs_6_), channel_id=1, source_target_pairs={{0,4},{4,0},{8,12},{12,8},{16,20},{20,16},{24,28},{28,24},{1,5},{5... | collective-permute-start | bytes 417800 | tf_op jit(solution)/shard_map/ppermute | solution.py:252
  19.2 6.3 %collective-permute-start.6 = (bf16[272,256]{1,0:T(8,128)(2,1)S(1)}, bf16[272,256]{1,0:T(8,128)(2,1)S(1)}, u32[]{:S(2)}, u32[]{:S(2)}) collective-permute-start(bf16[272,256]{1,0:T(8,128)(2,1)S(1)} %collective-permute-done.2.refs_7_), channel_id=1, source_target_pairs={{0,4},{4,0},{8,12},{12,8},{16,20},{20,16},{24,28},{28,24},{1,5},{5... | collective-permute-start | bytes 417800 | tf_op jit(solution)/shard_map/ppermute | solution.py:252
  19.7 5.7 %collective-permute-start.9 = (bf16[64,1024]{1,0:T(8,128)(2,1)}, bf16[64,1024]{1,0:T(8,128)(2,1)S(1)}, u32[]{:S(2)}, u32[]{:S(2)}) collective-permute-start(bf16[64,1024]{1,0:T(8,128)(2,1)} %get-tuple-element.25), channel_id=1, source_target_pairs={{0,3},{1,0},{2,1},{3,2},{4,7},{5,4},{6,5},{7,6},{8,11},{9,8},{10,9... | collective-permute-start | bytes 393224 | tf_op jit(solution)/shard_map/ppermute | solution.py:254
  25.5 0.7 copy-start.1
  25.5 0.7 copy-start.2
  26.1 0.9 %copy-start.5 = (bf16[272,256]{1,0:T(8,128)(2,1)S(1)}, bf16[272,256]{1,0:T(8,128)(2,1)}, u32[]{:S(2)}) copy-start(bf16[272,256]{1,0:T(8,128)(2,1)} %get-tuple-element.21.refs_4_) | copy-start | bytes 417796
  27.0 0.9 %copy-start.6 = (f32[256,128]{1,0:T(8,128)S(1)}, f32[256,128]{1,0:T(8,128)}, u32[]{:S(2)}) copy-start(f32[256,128]{1,0:T(8,128)} %get-tuple-element.20.refs_2_) | copy-start | bytes 393220
  27.9 0.9 %copy-start.7 = (bf16[64,1024]{1,0:T(8,128)(2,1)S(1)}, bf16[64,1024]{1,0:T(8,128)(2,1)}, u32[]{:S(2)}) copy-start(bf16[64,1024]{1,0:T(8,128)(2,1)} %get-tuple-element.22.refs_12_) | copy-start | bytes 393220
  34.4 0.7 copy-start
  35.1 1.4 %collective-permute-start.14 = (bf16[128,512]{1,0:T(8,128)(2,1)S(1)}, bf16[128,512]{1,0:T(8,128)(2,1)S(1)}, u32[]{:S(2)}, u32[]{:S(2)}) collective-permute-start(bf16[128,512]{1,0:T(8,128)(2,1)S(1)} %get-tuple-element.32), channel_id=1, source_target_pairs={{0,4},{4,0},{8,12},{12,8},{16,20},{20,16},{24,28},{28,24},{1,5},{5... | collective-permute-start | bytes 393224 | tf_op jit(solution)/shard_map/ppermute | solution.py:259
  35.1 1.3 %collective-permute-start.13 = (s32[2]{0:T(128)S(1)}, s32[2]{0:T(128)S(1)}, u32[]{:S(2)}, u32[]{:S(2)}) collective-permute-start(s32[2]{0:T(128)S(1)} %copy-done.2), channel_id=1, source_target_pairs={{0,4},{4,0},{8,12},{12,8},{16,20},{20,16},{24,28},{28,24},{1,5},{5... | collective-permute-start | bytes 32 | tf_op jit(solution)/shard_map/ppermute | solution.py:253
  36.5 0.5 copy-start.10
  36.5 0.7 copy-start.8
  38.9 20.9 %collective-permute-start.15 = (bf16[64,512]{1,0:T(8,128)(2,1)}, bf16[64,512]{1,0:T(8,128)(2,1)S(1)}, u32[]{:S(2)}, u32[]{:S(2)}) collective-permute-start(bf16[64,512]{1,0:T(8,128)(2,1)} %get-tuple-element.33), channel_id=1, source_target_pairs={{0,0},{1,1},{2,2},{3,3},{4,4},{5,5},{6,6},{7,7},{8,9},{9,10},{10,1... | collective-permute-start | bytes 196616 | tf_op jit(solution)/shard_map/ppermute | solution.py:279
  40.4 20.1 %collective-permute-start.17 = (bf16[64,512]{1,0:T(8,128)(2,1)}, bf16[64,512]{1,0:T(8,128)(2,1)S(1)}, u32[]{:S(2)}, u32[]{:S(2)}) collective-permute-start(bf16[64,512]{1,0:T(8,128)(2,1)} %get-tuple-element.34), channel_id=1, source_target_pairs={{0,1},{1,2},{2,3},{3,0},{4,5},{5,6},{6,7},{7,4},{8,10},{9,11},{10,... | collective-permute-start | bytes 196616 | tf_op jit(solution)/shard_map/ppermute | solution.py:279
  44.6 34.5 %collective-permute-start.19 = (bf16[64,512]{1,0:T(8,128)(2,1)}, bf16[64,512]{1,0:T(8,128)(2,1)S(1)}, u32[]{:S(2)}, u32[]{:S(2)}) collective-permute-start(bf16[64,512]{1,0:T(8,128)(2,1)} %get-tuple-element.35), channel_id=1, source_target_pairs={{0,2},{1,3},{2,0},{3,1},{4,6},{5,7},{6,4},{7,5},{8,11},{9,8},{10,9... | collective-permute-start | bytes 196616 | tf_op jit(solution)/shard_map/ppermute | solution.py:279
  48.1 35.0 %collective-permute-start.21 = (bf16[64,512]{1,0:T(8,128)(2,1)}, bf16[64,512]{1,0:T(8,128)(2,1)S(1)}, u32[]{:S(2)}, u32[]{:S(2)}) collective-permute-start(bf16[64,512]{1,0:T(8,128)(2,1)} %get-tuple-element.36), channel_id=1, source_target_pairs={{0,3},{1,0},{2,1},{3,2},{4,7},{5,4},{6,5},{7,6},{8,8},{9,9},{10,10... | collective-permute-start | bytes 196616 | tf_op jit(solution)/shard_map/ppermute | solution.py:279
  50.5 4.9 %collective-permute-start.10 = (f32[64,64]{1,0:T(8,128)S(1)}, f32[64,64]{1,0:T(8,128)S(1)}, u32[]{:S(2)}, u32[]{:S(2)}) collective-permute-start(f32[64,64]{1,0:T(8,128)S(1)} %get-tuple-element.28), channel_id=1, source_target_pairs={{0,1},{1,2},{2,3},{3,0},{4,5},{5,6},{6,7},{7,4},{8,9},{9,10},{10,1... | collective-permute-start | bytes 49160 | tf_op jit(solution)/shard_map/ppermute | solution.py:282
  55.4 3.9 %collective-permute-start.11 = (f32[64,64]{1,0:T(8,128)S(1)}, f32[64,64]{1,0:T(8,128)S(1)}, u32[]{:S(2)}, u32[]{:S(2)}) collective-permute-start(f32[64,64]{1,0:T(8,128)S(1)} %get-tuple-element.29), channel_id=1, source_target_pairs={{0,2},{1,3},{2,0},{3,1},{4,6},{5,7},{6,4},{7,5},{8,10},{9,11},{10,... | collective-permute-start | bytes 49160 | tf_op jit(solution)/shard_map/ppermute | solution.py:282
  59.3 25.7 %collective-permute-start.12 = (f32[64,64]{1,0:T(8,128)S(1)}, f32[64,64]{1,0:T(8,128)S(1)}, u32[]{:S(2)}, u32[]{:S(2)}) collective-permute-start(f32[64,64]{1,0:T(8,128)S(1)} %get-tuple-element.30), channel_id=1, source_target_pairs={{0,3},{1,0},{2,1},{3,2},{4,7},{5,4},{6,5},{7,6},{8,11},{9,8},{10,9... | collective-permute-start | bytes 49160 | tf_op jit(solution)/shard_map/ppermute | solution.py:282
  59.8 25.8 %collective-permute-start.16 = (bf16[64,512]{1,0:T(8,128)(2,1)S(1)}, bf16[64,512]{1,0:T(8,128)(2,1)S(1)}, u32[]{:S(2)}, u32[]{:S(2)}) collective-permute-start(bf16[64,512]{1,0:T(8,128)(2,1)S(1)} %collective-permute-done.15), channel_id=1, source_target_pairs={{0,0},{1,9},{2,18},{3,27},{4,4},{5,13},{6,22},{7,31},{8,24},{9,1},... | collective-permute-start | bytes 196616 | tf_op jit(solution)/shard_map/ppermute | solution.py:280
  60.5 25.1 %collective-permute-start.18 = (bf16[64,512]{1,0:T(8,128)(2,1)S(1)}, bf16[64,512]{1,0:T(8,128)(2,1)S(1)}, u32[]{:S(2)}, u32[]{:S(2)}) collective-permute-start(bf16[64,512]{1,0:T(8,128)(2,1)S(1)} %collective-permute-done.17), channel_id=1, source_target_pairs={{0,24},{1,1},{2,10},{3,19},{4,28},{5,5},{6,14},{7,23},{8,16},{9,25... | collective-permute-start | bytes 196616 | tf_op jit(solution)/shard_map/ppermute | solution.py:280
  79.1 7.1 %collective-permute-start.20 = (bf16[64,512]{1,0:T(8,128)(2,1)S(1)}, bf16[64,512]{1,0:T(8,128)(2,1)S(1)}, u32[]{:S(2)}, u32[]{:S(2)}) collective-permute-start(bf16[64,512]{1,0:T(8,128)(2,1)S(1)} %collective-permute-done.19), channel_id=1, source_target_pairs={{0,16},{1,25},{2,2},{3,11},{4,20},{5,29},{6,6},{7,15},{8,8},{9,17}... | collective-permute-start | bytes 196616 | tf_op jit(solution)/shard_map/ppermute | solution.py:280
  83.0 6.2 %collective-permute-start.22 = (bf16[64,512]{1,0:T(8,128)(2,1)S(1)}, bf16[64,512]{1,0:T(8,128)(2,1)S(1)}, u32[]{:S(2)}, u32[]{:S(2)}) collective-permute-start(bf16[64,512]{1,0:T(8,128)(2,1)S(1)} %collective-permute-done.21), channel_id=1, source_target_pairs={{0,8},{1,17},{2,26},{3,3},{4,12},{5,21},{6,30},{7,7},{8,0},{9,9},{... | collective-permute-start | bytes 196616 | tf_op jit(solution)/shard_map/ppermute | solution.py:280

commit v2 on v0

v2 whole, which is shorter than its diff:
```python
import functools

import jax
import jax.numpy as jnp
from jax import lax
from jax.experimental import pallas as pl
from jax.experimental.pallas import tpu as pltpu
from jax.sharding import PartitionSpec as P

QH = 32
KVH = 4
HD = 128
RANK = 64
BLOCK = 128
CORES = 2
PAD = 16
GROUP = 4

adapter_scale_factor = 2.0
far_below = -1e30
logit_scale = HD ** (-0.5)
log2_scale = logit_scale * 1.4426950408889634

VMEM = pl.BlockSpec(memory_space=pltpu.VMEM)
SMEM = pl.BlockSpec(memory_space=pltpu.SMEM)
ANY = pl.BlockSpec(memory_space=pl.ANY)
HBM = pl.BlockSpec(memory_space=pltpu.HBM)
BF16 = jnp.bfloat16
F32 = jnp.float32


def small(bytes_accessed):
    return dict(
        compiler_params=pltpu.CompilerParams(vmem_limit_bytes=8 << 20),
        cost_estimate=pl.CostEstimate(flops=0, bytes_accessed=bytes_accessed, transcendentals=0),
    )


def pack_kernel(heads_dev, tenant_hbm, keys, values, docs_hbm, message, tenant, docs, sems):
    tokens = keys.shape[0]
    kv = lax.axis_index("adp") * heads_dev // (QH // KVH)
    head = pl.ds(pl.multiple_of(kv * HD, HD), HD)
    copies = [
        pltpu.make_async_copy(docs_hbm, docs, sems.at[0]),
        pltpu.make_async_copy(tenant_hbm, tenant, sems.at[1]),
        pltpu.make_async_copy(keys.at[:, head], message.at[pl.ds(0, tokens), pl.ds(0, HD)], sems.at[2]),
        pltpu.make_async_copy(values.at[:, head], message.at[pl.ds(0, tokens), pl.ds(HD, HD)], sems.at[3]),
    ]
    for copy in copies:
        copy.start()
    for copy in copies[:2]:
        copy.wait()
    row = lax.broadcasted_iota(jnp.int32, (PAD, tokens), 0)
    told = jnp.broadcast_to(docs[...].astype(F32), (PAD, tokens))
    for block in range(tokens // BLOCK):
        told = jnp.where(row == 1 + block, tenant[block].astype(F32), told)
    message[tokens:, :] = told.astype(BF16)
    for copy in copies[2:]:
        copy.wait()


def pack(block_tenant, keys, values, docs, heads_dev):
    tokens = keys.shape[0]
    return pl.pallas_call(
        functools.partial(pack_kernel, heads_dev),
        in_specs=[HBM] * 4,
        out_specs=VMEM,
        out_shape=jax.ShapeDtypeStruct((tokens + PAD, 2 * HD), BF16),
        scratch_shapes=[
            pltpu.SMEM(block_tenant.shape, jnp.int32),
            pltpu.VMEM((1, tokens), jnp.int32),
            pltpu.SemaphoreType.DMA((4,)),
        ],
        name="pack",
        **small(1 << 18),
    )(block_tenant, keys, values, docs.reshape(1, tokens))


def columns_kernel(owners, adapter_b, after, *refs):
    outs, sems = refs[:owners], refs[owners]
    width = outs[0].shape[1]
    adp = lax.axis_index("adp")
    copies = []
    for s in range(owners):
        start = pl.multiple_of(lax.rem(adp + s, owners) * width, 128)
        copies.append(pltpu.make_async_copy(adapter_b.at[0, :, pl.ds(start, width)], outs[s], sems.at[s]))
        copies[-1].start()
    for copy in copies:
        copy.wait()


def columns(adapter_b, after, owners):
    width = adapter_b.shape[2] // owners
    return pl.pallas_call(
        functools.partial(columns_kernel, owners),
        in_specs=[ANY, ANY],
        out_specs=[VMEM] * owners,
        out_shape=[jax.ShapeDtypeStruct((RANK, width), BF16)] * owners,
        scratch_shapes=[pltpu.SemaphoreType.DMA((owners,))],
        name="columns",
        **small(1 << 19),
    )(adapter_b, after)


def lanes(x, times):
    return jnp.concatenate([x] * times, axis=1)


def rows(x, times):
    return jnp.concatenate([x] * times, axis=0)


def attend_kernel(shifts, first, last, *refs):
    refs = list(refs)
    take = lambda count: [refs.pop(0) for _ in range(count)]
    q_ref, g_ref, docs_ref = take(3)
    own, other = take(len(shifts)), take(len(shifts))
    if not first:
        top_in, by_key_in, by_grad_in = take(3)
    if last:
        low_ref, dq_ref, mine_ref, partner_ref = take(4)
    top, by_key, by_grad, bias = take(4)
    tokens, width = q_ref.shape
    heads = width // HD
    group = min(GROUP, heads)
    ctx = lax.axis_index("ctx")
    z, core = ctx // CORES, lax.rem(ctx, CORES)
    doc_row = lambda ref: ref[tokens : tokens + PAD, :][:1].astype(F32)

    docs = doc_row(docs_ref)
    first_doc = jnp.min(docs)
    row = lax.broadcasted_iota(jnp.int32, (tokens, tokens), 0)
    lane = lax.broadcasted_iota(jnp.int32, (tokens, tokens), 1)
    doc_column = jnp.sum(jnp.where(row == lane, docs, 0.0), axis=1, keepdims=True)

    def stacked(ref, h):
        return jnp.concatenate(
            [ref[:, i * HD : (i + 1) * HD] for i in range(h, h + group)], axis=0
        )

    def step(index, shift, old):
        keys = jnp.concatenate([own[index][:tokens, :HD], other[index][:tokens, :HD]], axis=0)
        values = jnp.concatenate([own[index][:tokens, HD:], other[index][:tokens, HD:]], axis=0)
        extended = jnp.concatenate([keys, jnp.ones((2 * tokens, HD), BF16)], axis=1)
        own_seen = doc_row(own[index]) == doc_column
        other_doc = doc_row(other[index])
        if shift == 0:
            own_seen = own_seen & (lane <= row)
            other_doc = jnp.where(core == 1, other_doc, -1.0)
        other_seen = other_doc == doc_column
        bias[:, :tokens] = jnp.where(own_seen, 0.0, far_below)
        bias[:, tokens:] = jnp.where(other_seen, 0.0, far_below)
        for h in range(0, heads, group):
            part = slice(h * tokens, (h + group) * tokens)
            scores = lax.dot_general(
                stacked(q_ref, h), keys, (((1,), (1,)), ((), ())), preferred_element_type=F32
            ) + rows(bias[...], group)
            block_top = jnp.broadcast_to(
                jnp.max(scores, axis=1, keepdims=True), (group * tokens, 128)
            )
            new_top = block_top if shift == 0 else jnp.maximum(old[0][part, :], block_top)
            p = jnp.exp2((scores - lanes(new_top, 2 * tokens // 128)) * log2_scale)
            grads = lax.dot_general(
                stacked(g_ref, h), values, (((1,), (1,)), ((), ())), preferred_element_type=F32
            )
            key_sum = jnp.dot(p.astype(BF16), extended, preferred_element_type=F32)
            grad_sum = jnp.dot((p * grads).astype(BF16), extended, preferred_element_type=F32)
            if shift:
                decay = lanes(jnp.exp2((old[0][part, :] - new_top) * log2_scale), 2)
                key_sum = key_sum + old[1][part, :] * decay
                grad_sum = grad_sum + old[2][part, :] * decay
            top[part, :] = new_top
            by_key[part, :] = key_sum
            by_grad[part, :] = grad_sum

    for index, shift in enumerate(shifts):
        if shift == 0:
            step(index, shift, None)
            continue
        old = (top, by_key, by_grad)
        latest = jnp.max(jnp.maximum(doc_row(own[index]), doc_row(other[index])))
        needed = (z >= shift) & (latest == first_doc)
        if index == 0:
            old = (top_in, by_key_in, by_grad_in)

            @pl.when(jnp.logical_not(needed))
            def _():
                for kept, given in zip((top, by_key, by_grad), old):
                    kept[...] = given[...]

        pl.when(needed)(functools.partial(step, index, shift, old))

    if not last:
        return
    for h in range(heads):
        part = slice(h * tokens, (h + 1) * tokens)
        inverse = 1.0 / by_key[part, HD:]
        delta = by_grad[part, HD:] * inverse
        dq = (by_grad[part, :HD] - delta * by_key[part, :HD]) * (inverse * logit_scale)
        dq_ref[:, h * HD : (h + 1) * HD] = dq.astype(BF16)

    half = width // CORES
    for block in range(tokens // BLOCK):
        block_rows = slice(block * BLOCK, (block + 1) * BLOCK)
        partial = adapter_scale_factor * jnp.dot(
            low_ref[:, block_rows], dq_ref[block_rows, :], preferred_element_type=F32
        )
        out_rows = slice(block * RANK, (block + 1) * RANK)
        mine_ref[out_rows, :] = jnp.where(core == 0, partial[:, :half], partial[:, half:])
        partner_ref[out_rows, :] = jnp.where(
            core == 0, partial[:, half:], partial[:, :half]
        ).astype(BF16)


def attend(shifts, queries, grad_out, message, own, other, state=None, low_rank=None):
    tokens, width = queries.shape
    heads = width // HD
    blocks = tokens // BLOCK
    sums = [
        ((heads * tokens, 128), F32),
        ((heads * tokens, 2 * HD), F32),
        ((heads * tokens, 2 * HD), F32),
    ]
    inputs = [queries, grad_out, message, *own, *other]
    scratch = [pltpu.VMEM((tokens, 2 * tokens), F32)]
    if state is not None:
        inputs += state
    if low_rank is None:
        outs = sums
    else:
        inputs.append(low_rank.T)
        scratch = [pltpu.VMEM(*each) for each in sums] + scratch
        outs = [
            ((tokens, width), BF16),
            ((blocks * RANK, width // CORES), F32),
            ((blocks * RANK, width // CORES), BF16),
        ]
    return pl.pallas_call(
        functools.partial(attend_kernel, shifts, state is None, low_rank is not None),
        in_specs=[VMEM] * len(inputs),
        out_specs=[VMEM] * len(outs),
        out_shape=[jax.ShapeDtypeStruct(*each) for each in outs],
        scratch_shapes=scratch,
        compiler_params=pltpu.CompilerParams(vmem_limit_bytes=30 << 20),
        cost_estimate=pl.CostEstimate(
            flops=len(shifts) * 12 * tokens * tokens * width,
            bytes_accessed=4 << 20,
            transcendentals=0,
        ),
        name="attend_" + "_".join(map(str, shifts[:4])),
    )(*inputs)


def ranks_kernel(owners, tenant_hbm, dq_ref, *refs):
    b_refs, rank_ref, chosen, tenant, sem = refs[:owners], *refs[owners:]
    copy = pltpu.make_async_copy(tenant_hbm, tenant, sem)
    copy.start()
    copy.wait()
    adp = lax.axis_index("adp")
    for block in range(dq_ref.shape[0] // BLOCK):
        block_rows = slice(block * BLOCK, (block + 1) * BLOCK)
        holder = lax.rem(adp - tenant[block] + owners, owners)
        for s in range(owners):

            @pl.when(holder == s)
            def _(s=s):
                chosen[...] = b_refs[s][...]

        rank_ref[block_rows, :] = adapter_scale_factor * lax.dot_general(
            dq_ref[block_rows, :], chosen[...], (((1,), (1,)), ((), ())), preferred_element_type=F32
        )


def ranks_of(tenant, dq, b_cols):
    tokens, width = dq.shape
    return pl.pallas_call(
        functools.partial(ranks_kernel, len(b_cols)),
        in_specs=[HBM] + [VMEM] * (1 + len(b_cols)),
        out_specs=VMEM,
        out_shape=jax.ShapeDtypeStruct((tokens, RANK), F32),
        scratch_shapes=[
            pltpu.VMEM((RANK, width), BF16),
            pltpu.SMEM(tenant.shape, jnp.int32),
            pltpu.SemaphoreType.DMA,
        ],
        name="ranks",
        **small(1 << 20),
    )(tenant, dq, *b_cols)


def tenants_kernel(owners, mine_ref, other_ref, own_notes, other_notes, rank_ref, *outs):
    blocks = mine_ref.shape[0] // RANK
    width = mine_ref.shape[1]
    share = rank_ref.shape[0] // owners
    adp = lax.axis_index("adp")
    told = [ref[ref.shape[0] - PAD :, :HD].astype(F32) for ref in (own_notes, other_notes)]
    for s in range(owners):
        owner = lax.rem(adp + s, owners)
        total = jnp.zeros((RANK, width), F32)
        for block in range(blocks):
            part = slice(block * RANK, (block + 1) * RANK)
            for each, ref in zip(told, (mine_ref, other_ref)):
                chosen = lanes(each[1 + block : 2 + block] == owner.astype(F32), width // HD)
                total = total + jnp.where(chosen, ref[part, :].astype(F32), 0.0)
        outs[s][:RANK, :] = total.astype(BF16)
        outs[s][RANK:, :] = jnp.zeros((PAD, width), BF16)
        for part in range(share // PAD):
            start = pl.multiple_of(owner * share + part * PAD, PAD)
            outs[s][RANK:, part * HD : part * HD + RANK] = rank_ref[pl.ds(start, PAD), :].astype(BF16)


def by_tenant(mine, other, own_message, other_message, ranks, owners):
    width = mine.shape[1]
    return pl.pallas_call(
        functools.partial(tenants_kernel, owners),
        in_specs=[VMEM] * 5,
        out_specs=[VMEM] * owners,
        out_shape=[jax.ShapeDtypeStruct((RANK + PAD, width), BF16)] * owners,
        name="by_tenant",
        **small(1 << 20),
    )(mine, other, own_message, other_message, ranks)


def columns_owner_kernel(owners, *refs):
    pieces, outs, rank_out = refs[:owners], refs[owners:-1], refs[-1]
    ctx, adp = lax.axis_index("ctx"), lax.axis_index("adp")
    z = ctx // CORES
    share = rank_out.shape[0]
    for part in range(share // PAD):
        rank_out[part * PAD : (part + 1) * PAD, :] = sum(
            piece[RANK:, part * HD : part * HD + RANK].astype(F32) for piece in pieces
        )
    for s in range(owners):
        source = lax.rem(adp - z - s + 2 * owners, owners)
        for j in range(owners):

            @pl.when(source == j)
            def _(s=s, j=j):
                outs[s][...] = pieces[j][:RANK, :]


def by_columns_owner(pieces, share):
    owners = len(pieces)
    width = pieces[0].shape[1]
    return pl.pallas_call(
        functools.partial(columns_owner_kernel, owners),
        in_specs=[VMEM] * owners,
        out_specs=[VMEM] * (owners + 1),
        out_shape=[jax.ShapeDtypeStruct((RANK, width), BF16)] * owners
        + [jax.ShapeDtypeStruct((share, RANK), F32)],
        name="by_columns_owner",
        **small(1 << 20),
    )(*pieces)


def on_device(queries, keys, values, grad_out, docs, block_tenant, low_rank, adapter_b):
    positions, owners = lax.axis_size("ctx"), lax.axis_size("adp")
    chips = positions // CORES
    tokens = queries.shape[0]
    heads_dev = queries.shape[1] // HD
    swap = [(c, c ^ 1) for c in range(positions)]
    up = lambda s: [(c, (c + CORES * s) % positions) for c in range(positions)]
    along = lambda s: [(a, (a + s) % owners) for a in range(owners)]

    message = pack(block_tenant, keys, values, docs, heads_dev)
    own = [message] + [lax.ppermute(message, "ctx", up(s)) for s in range(1, chips)]
    other = [lax.ppermute(message, "ctx", swap)]
    b_out = columns(adapter_b, other[0], owners)
    b_cols = [b_out[0]] + [lax.ppermute(b_out[s], "adp", along(s)) for s in range(1, owners)]
    state = attend((0,), queries, grad_out, message, own[:1], other[:1])
    own, state, b_cols = lax.optimization_barrier((own, state, b_cols))
    other += [lax.ppermute(m, "ctx", swap) for m in own[1:]]

    grad_queries, mine, partner = attend(
        tuple(range(1, chips)), queries, grad_out, message, own[1:], other[1:], state, low_rank
    )
    other_part = lax.ppermute(partner, "ctx", swap)
    ranks = ranks_of(block_tenant, grad_queries, b_cols)
    pieces = by_tenant(mine, other_part, message, other[0], ranks, owners)
    pieces = [pieces[0]] + [
        lax.ppermute(pieces[s], "adp", along(s)) for s in range(1, owners)
    ]
    *pieces, grad_low_rank = by_columns_owner(pieces, tokens // owners)
    pieces = [pieces[0]] + [lax.ppermute(pieces[s], "ctx", up(s)) for s in range(1, chips)]
    grad_adapter = sum(piece.astype(F32) for piece in pieces)[None]
    return grad_queries, grad_low_rank, grad_adapter


def solution(mesh):
    placed = (
        P("ctx", "adp"),
        P("ctx", None),
        P("ctx", None),
        P("ctx", "adp"),
        P("ctx"),
        P("ctx"),
        P("ctx", None),
        P("adp", None, None),
    )
    return jax.shard_map(
        on_device,
        mesh=mesh,
        in_specs=placed,
        out_specs=(P("ctx", "adp"), P(("ctx", "adp"), None), P("adp", None, "ctx")),
        check_vma=False,
    )
```

time: 236 us -> 51.5 us (0.22)
  matrix products: 58.7 us -> 0 us
  blocking collectives: 57.1 us -> 0 us
  other arithmetic: 40.2 us -> 0.69 us
  waiting for transfers between devices: 34.6 us -> 9.77 us
  starting transfers between devices: 4.34 us -> 26.3 us
  local copies, waits for them, and re-layouts: 24.1 us -> 7.4 us
  between operations: 15.7 us -> 0.73 us
  Pallas kernels: 0 us -> 7.46 us
    dot_general x18 -> x0, matrix products: 58.7 us -> none  [the longest x4 19.3 us: backward_update(): jnp.dot(grad_scores, key_block, preferred_element_type=jnp.float32)]
    all_gather x3 -> x0, blocking collectives: 44.5 us -> none  [the longest x1 16.6 us: on_device(): lax.all_gather(my_keys, 'ctx', axis=0, tiled=True)]
    ppermute x0 -> x17, starting transfers between devices: none -> 26.3 us  [the longest x3 10.3 us: on_device(): lax.ppermute(pieces[s], 'ctx', up(s))]
    unnamed x5 -> x0, other arithmetic: 23.6 us -> none
    unnamed x3 -> x0, waiting for transfers between devices: 17.1 us -> none
    reduce_sum x6 -> x0, other arithmetic: 15.3 us -> none  [the longest x4 13.2 us: forward_update(): row_total = row_total * decay_factor + jnp.sum(weights_f, axis=1)]
    psum x1 -> x0, waiting for transfers between devices: 13.9 us -> none  [on_device(): summed_all = lax.psum(tenant_contributions, 'ctx')]
    all_to_all x1 -> x0, blocking collectives: 12.6 us -> none  [on_device(): lax.all_to_all(adapter_b, 'adp', split_axis=2, concat_axis=0, tiled=True)]
  transfers between devices with their start and end apart: 3 -> 17, of which waited for: 3 -> 10; matrix products, arithmetic and copies ran while one was open for 18% -> 0% of each run, Pallas kernels for 0% -> 8%
where the time goes in v2:
time: 51.5 us; the launch traced here: 52.3 us
  starting transfers between devices  26.3 us (51%)
  waiting for transfers between devices  9.77 us (19%)
  Pallas kernels  7.46 us (14%)
  local copies, waits for them, and re-layouts  7.4 us (14%)
  between operations  0.73 us (1%)
  other arithmetic  0.69 us (1%)
    ppermute x3, starting transfers between devices, on_device(): lax.ppermute(pieces[s], 'ctx', up(s))  10.3 us
    unnamed x20, local copies, waits for them, and re-layouts  7.4 us
    ppermute x3, starting transfers between devices, on_device(): lax.ppermute(message, 'ctx', up(s))  5.68 us
    pallas_call x2, Pallas kernels, attend(): pl.pallas_call(functools.partial(attend_kernel, shifts, state is None, lo...  4.7 us
    ppermute x3, starting transfers between devices, on_device(): lax.ppermute(b_out[s], 'adp', along(s))  4.5 us
    ppermute x3, starting transfers between devices, on_device(): lax.ppermute(pieces[s], 'adp', along(s))  4.49 us
    ppermute x3, waiting for transfers between devices, on_device(): lax.ppermute(pieces[s], 'ctx', up(s))  4.4 us
    ppermute x3, waiting for transfers between devices, on_device(): lax.ppermute(pieces[s], 'adp', along(s))  3.02 us
  transfers between devices with their start and end apart: 17, of which 10 were waited for; matrix products, arithmetic and copies ran while one was open for 0% of the time, Pallas kernels for 8%

profile of v2, /device:TPU:0, one launch (start us, length us, event | category | flops | bytes accessed | tf_op | source)
XLA Modules:
  0.0 52.3 jit_solution(1285583483876288361)
XLA Ops:
  0.6 0.9 %copy-done.2 = bf16[256,512]{1,0:T(8,128)(2,1)S(1)} copy-done((bf16[256,512]{1,0:T(8,128)(2,1)S(1)}, bf16[256,512]{1,0:T(8,128)(2,1)}, u32[]{:S(2)}) %copy-start.2) | copy-done | bytes 262168
  1.6 0.9 %copy-done.3 = bf16[256,512]{1,0:T(8,128)(2,1)S(1)} copy-done((bf16[256,512]{1,0:T(8,128)(2,1)S(1)}, bf16[256,512]{1,0:T(8,128)(2,1)}, u32[]{:S(2)}) %copy-start.3) | copy-done | bytes 262168
  2.5 0.7 %copy-done.4 = s32[2]{0:T(128)S(1)} copy-done((s32[2]{0:T(128)S(1)}, s32[2]{0:T(128)}, u32[]{:S(2)}) %copy-start.4) | copy-done | bytes 32
  3.2 0.7 %copy-done.6 = s32[256]{0:T(256)S(1)} copy-done((s32[256]{0:T(256)S(1)}, s32[256]{0:T(256)}, u32[]{:S(2)}) %copy-start.6) | copy-done | bytes 1048
  3.9 0.6 %pack.1.refs_2_.refs_3_.own_notes = bf16[272,256]{1,0:T(8,128)(2,1)S(1)} custom-call(s32[2]{0:T(128)S(1)} %copy-done.4, bf16[256,512]{1,0:T(8,128)(2,1)S(1)} %copy-done.2, bf16[256,512]{1,0:T(8,128)(2,1)S(1)} %copy-done.3, s32[1,256]{1,0:T(1,128)S(1)} %bitcast.4), custom_call_target="tpu_custom_call" | custom-call | bytes 262144 | tf_op jit(solution)/shard_map/pack/pallas_call | solution.py:64
  4.5 0.5 collective-permute-start.3
  5.0 4.7 %collective-permute-start.2 = (bf16[272,256]{1,0:T(8,128)(2,1)S(1)}, bf16[272,256]{1,0:T(8,128)(2,1)S(1)}, u32[]{:S(2)}, u32[]{:S(2)}) collective-permute-start(bf16[272,256]{1,0:T(8,128)(2,1)S(1)} %pack.1.refs_2_.refs_3_.own_notes), channel_id=1, source_target_pairs={{0,24},{4,28},{8,0},{12,4},{16,8},{20,12},{24,16},{28,20},{1,25},{... | collective-permute-start | bytes 417800 | tf_op jit(solution)/shard_map/ppermute | solution.py:366
  9.6 0.0 collective-permute-start.1
  9.6 1.0 %collective-permute-start = (bf16[272,256]{1,0:T(8,128)(2,1)S(1)}, bf16[272,256]{1,0:T(8,128)(2,1)S(1)}, u32[]{:S(2)}, u32[]{:S(2)}) collective-permute-start(bf16[272,256]{1,0:T(8,128)(2,1)S(1)} %pack.1.refs_2_.refs_3_.own_notes), channel_id=1, source_target_pairs={{0,8},{4,12},{8,16},{12,20},{16,24},{20,28},{24,0},{28,4},{1,9},{5... | collective-permute-start | bytes 417800 | tf_op jit(solution)/shard_map/ppermute | solution.py:366
  10.7 0.0 collective-permute-done.3.refs_4_.after.other_notes
  10.7 1.0 %copy-done = bf16[1,64,4096]{2,1,0:T(8,128)(2,1)S(1)} copy-done((bf16[1,64,4096]{2,1,0:T(8,128)(2,1)S(1)}, bf16[1,64,4096]{2,1,0:T(8,128)(2,1)}, u32[]{:S(2)}) %copy-start) | copy-done | bytes 524312
  11.7 0.1 columns.1
  11.9 1.5 %collective-permute-start.4 = (bf16[64,1024]{1,0:T(8,128)(2,1)S(1)}, bf16[64,1024]{1,0:T(8,128)(2,1)S(1)}, u32[]{:S(2)}, u32[]{:S(2)}) collective-permute-start(bf16[64,1024]{1,0:T(8,128)(2,1)S(1)} %get-tuple-element.36), channel_id=1, source_target_pairs={{0,1},{1,2},{2,3},{3,0},{4,5},{5,6},{6,7},{7,4},{8,9},{9,10},{10,1... | collective-permute-start | bytes 393224 | tf_op jit(solution)/shard_map/ppermute | solution.py:369
  13.4 1.5 %collective-permute-start.5 = (bf16[64,1024]{1,0:T(8,128)(2,1)S(1)}, bf16[64,1024]{1,0:T(8,128)(2,1)S(1)}, u32[]{:S(2)}, u32[]{:S(2)}) collective-permute-start(bf16[64,1024]{1,0:T(8,128)(2,1)S(1)} %get-tuple-element.37), channel_id=1, source_target_pairs={{0,2},{1,3},{2,0},{3,1},{4,6},{5,7},{6,4},{7,5},{8,10},{9,11},{10,... | collective-permute-start | bytes 393224 | tf_op jit(solution)/shard_map/ppermute | solution.py:369
  14.9 0.0 collective-permute-done.2.refs_5_
  14.9 1.4 %collective-permute-start.6 = (bf16[64,1024]{1,0:T(8,128)(2,1)S(1)}, bf16[64,1024]{1,0:T(8,128)(2,1)S(1)}, u32[]{:S(2)}, u32[]{:S(2)}) collective-permute-start(bf16[64,1024]{1,0:T(8,128)(2,1)S(1)} %get-tuple-element.38), channel_id=1, source_target_pairs={{0,3},{1,0},{2,1},{3,2},{4,7},{5,4},{6,5},{7,6},{8,11},{9,8},{10,9... | collective-permute-start | bytes 393224 | tf_op jit(solution)/shard_map/ppermute | solution.py:369
  16.4 1.0 %copy-done.7 = bf16[256,1024]{1,0:T(8,128)(2,1)S(1)} copy-done((bf16[256,1024]{1,0:T(8,128)(2,1)S(1)}, bf16[256,1024]{1,0:T(8,128)(2,1)}, u32[]{:S(2)}) %copy-start.7) | copy-done | bytes 524312
  17.4 1.0 %copy-done.8 = bf16[256,1024]{1,0:T(8,128)(2,1)S(1)} copy-done((bf16[256,1024]{1,0:T(8,128)(2,1)S(1)}, bf16[256,1024]{1,0:T(8,128)(2,1)}, u32[]{:S(2)}) %copy-start.8) | copy-done | bytes 524312
  18.4 2.8 %attend_0.1 = (f32[2048,128]{1,0:T(8,128)S(1)}, f32[2048,256]{1,0:T(8,128)S(1)}, f32[2048,256]{1,0:T(8,128)S(1)}) custom-call(bf16[256,1024]{1,0:T(8,128)(2,1)S(1)} %copy-done.7, bf16[256,1024]{1,0:T(8,128)(2,1)S(1)} %copy-done.8, bf16[272,256]{1,0:T(8,128)(2,1)S(1)} %pack.1.refs_2_.refs_3_.own_notes, bf16[272,256]{1,0:T(8,128)(2,1)S(1)} %pack.1.refs_2_.refs_3_.own_notes, ...), custom_call_target="tpu_custom_call" | custom-call | flops 805306368 | bytes 4194304 | tf_op jit(solution)/shard_map/attend_0/pallas_call | solution.py:238
  21.2 1.1 %collective-permute-done.1.refs_4_ = bf16[272,256]{1,0:T(8,128)(2,1)S(1)} collective-permute-done((bf16[272,256]{1,0:T(8,128)(2,1)S(1)}, bf16[272,256]{1,0:T(8,128)(2,1)S(1)}, u32[]{:S(2)}, u32[]{:S(2)}) %collective-permute-start.1) | collective-permute-done | bytes 139296 | tf_op jit(solution)/shard_map/ppermute | solution.py:366
  22.3 0.0 collective-permute-done.refs_3_
  22.3 0.0 collective-permute-done.4.refs_1_
  22.3 0.1 collective-permute-start.7
  22.4 0.5 collective-permute-start.8
  22.9 0.1 collective-permute-start.9
  22.9 0.8 %collective-permute-done.7.refs_6_ = bf16[272,256]{1,0:T(8,128)(2,1)S(1)} collective-permute-done((bf16[272,256]{1,0:T(8,128)(2,1)S(1)}, bf16[272,256]{1,0:T(8,128)(2,1)S(1)}, u32[]{:S(2)}, u32[]{:S(2)}) %collective-permute-start.7) | collective-permute-done | bytes 139296 | tf_op jit(solution)/shard_map/ppermute | solution.py:372
  23.7 0.2 collective-permute-done.8.refs_7_
  23.9 0.3 collective-permute-done.9.refs_8_
  24.2 1.9 %attend_1_2_3.1 = (bf16[256,1024]{1,0:T(8,128)(2,1)}, f32[128,512]{1,0:T(8,128)S(1)}, bf16[128,512]{1,0:T(8,128)(2,1)S(1)}) custom-call(bf16[256,1024]{1,0:T(8,128)(2,1)S(1)} %copy-done.7, bf16[256,1024]{1,0:T(8,128)(2,1)S(1)} %copy-done.8, bf16[272,256]{1,0:T(8,128)(2,1)S(1)} %pack.1.refs_2_.refs_3_.own_notes, ...), custom_call_target="tpu_custom_call" | custom-call | flops 2415919104 | bytes 4194304 | tf_op jit(solution)/shard_map/attend_1_2_3/pallas_call | solution.py:238
  26.2 0.2 collective-permute-start.10
  26.4 1.0 %copy-done.1 = bf16[256,1024]{1,0:T(8,128)(2,1)S(1)} copy-done((bf16[256,1024]{1,0:T(8,128)(2,1)S(1)}, bf16[256,1024]{1,0:T(8,128)(2,1)}, u32[]{:S(2)}) %copy-start.1) | copy-done | bytes 524312
  27.4 1.1 %ranks.1.rank_ref = f32[256,64]{1,0:T(8,128)S(1)} custom-call(s32[2]{0:T(128)S(1)} %copy-done.5, bf16[256,1024]{1,0:T(8,128)(2,1)S(1)} %copy-done.1, bf16[64,1024]{1,0:T(8,128)(2,1)S(1)} %get-tuple-element.48.refs_0_, bf16[64,1024]{1,0:T(8,128)(2,1)S(1)} %collective-permute-done.4.refs_1_, bf16[64,1024]{1,0:T(8,128)(2,1)S(1)} %collective-permute-done.5.refs_2_, ...), custom_call_target="tpu_custom_call" | custom-call | bytes 1048576 | tf_op jit(solution)/shard_map/ranks/pallas_call | solution.py:276
  28.5 0.0 collective-permute-done.10.other_ref
  28.6 0.2 by_tenant.1
  28.8 1.5 %collective-permute-start.11 = (bf16[80,512]{1,0:T(8,128)(2,1)S(1)}, bf16[80,512]{1,0:T(8,128)(2,1)S(1)}, u32[]{:S(2)}, u32[]{:S(2)}) collective-permute-start(bf16[80,512]{1,0:T(8,128)(2,1)S(1)} %get-tuple-element.53), channel_id=1, source_target_pairs={{0,1},{1,2},{2,3},{3,0},{4,5},{5,6},{6,7},{7,4},{8,9},{9,10},{10,1... | collective-permute-start | bytes 245768 | tf_op jit(solution)/shard_map/ppermute | solution.py:381
  30.3 1.5 %collective-permute-start.12 = (bf16[80,512]{1,0:T(8,128)(2,1)S(1)}, bf16[80,512]{1,0:T(8,128)(2,1)S(1)}, u32[]{:S(2)}, u32[]{:S(2)}) collective-permute-start(bf16[80,512]{1,0:T(8,128)(2,1)S(1)} %get-tuple-element.54), channel_id=1, source_target_pairs={{0,2},{1,3},{2,0},{3,1},{4,6},{5,7},{6,4},{7,5},{8,10},{9,11},{10,... | collective-permute-start | bytes 245768 | tf_op jit(solution)/shard_map/ppermute | solution.py:381
  31.8 1.4 %collective-permute-start.13 = (bf16[80,512]{1,0:T(8,128)(2,1)S(1)}, bf16[80,512]{1,0:T(8,128)(2,1)S(1)}, u32[]{:S(2)}, u32[]{:S(2)}) collective-permute-start(bf16[80,512]{1,0:T(8,128)(2,1)S(1)} %get-tuple-element.55), channel_id=1, source_target_pairs={{0,3},{1,0},{2,1},{3,2},{4,7},{5,4},{6,5},{7,6},{8,11},{9,8},{10,9... | collective-permute-start | bytes 245768 | tf_op jit(solution)/shard_map/ppermute | solution.py:381
  33.2 1.4 %collective-permute-done.11.refs_1_ = bf16[80,512]{1,0:T(8,128)(2,1)S(1)} collective-permute-done((bf16[80,512]{1,0:T(8,128)(2,1)S(1)}, bf16[80,512]{1,0:T(8,128)(2,1)S(1)}, u32[]{:S(2)}, u32[]{:S(2)}) %collective-permute-start.11) | collective-permute-done | bytes 81952 | tf_op jit(solution)/shard_map/ppermute | solution.py:381
  34.6 1.5 %collective-permute-done.12.refs_2_ = bf16[80,512]{1,0:T(8,128)(2,1)S(1)} collective-permute-done((bf16[80,512]{1,0:T(8,128)(2,1)S(1)}, bf16[80,512]{1,0:T(8,128)(2,1)S(1)}, u32[]{:S(2)}, u32[]{:S(2)}) %collective-permute-start.12) | collective-permute-done | bytes 81952 | tf_op jit(solution)/shard_map/ppermute | solution.py:381
  36.1 0.1 collective-permute-done.13.refs_3_
  36.3 0.7 %by_columns_owner.1 = (bf16[64,512]{1,0:T(8,128)(2,1)S(1)}, bf16[64,512]{1,0:T(8,128)(2,1)S(1)}, bf16[64,512]{1,0:T(8,128)(2,1)S(1)}, bf16[64,512]{1,0:T(8,128)(2,1)S(1)}, f32[64,64]{1,0:T(8,128)}) custom-call(bf16[80,512]{1,0:T(8,128)(2,1)S(1)} %get-tuple-element.52.refs_0_, bf16[80,512]{1,0:T(8,128)(2,1)S(1)} %collective-permute-done.11.refs_1_, ...), custom_call_target="tpu_custom_call" | custom-call | bytes 1048576 | tf_op jit(solution)/shard_map/by_columns_owner/pallas_call | solution.py:345
  37.0 3.5 %collective-permute-start.14 = (bf16[64,512]{1,0:T(8,128)(2,1)S(1)}, bf16[64,512]{1,0:T(8,128)(2,1)S(1)}, u32[]{:S(2)}, u32[]{:S(2)}) collective-permute-start(bf16[64,512]{1,0:T(8,128)(2,1)S(1)} %get-tuple-element.58), channel_id=1, source_target_pairs={{0,8},{4,12},{8,16},{12,20},{16,24},{20,28},{24,0},{28,4},{1,9},{5... | collective-permute-start | bytes 196616 | tf_op jit(solution)/shard_map/ppermute | solution.py:384
  40.5 6.5 %collective-permute-start.15 = (bf16[64,512]{1,0:T(8,128)(2,1)S(1)}, bf16[64,512]{1,0:T(8,128)(2,1)S(1)}, u32[]{:S(2)}, u32[]{:S(2)}) collective-permute-start(bf16[64,512]{1,0:T(8,128)(2,1)S(1)} %get-tuple-element.59), channel_id=1, source_target_pairs={{0,16},{4,20},{8,24},{12,28},{16,0},{20,4},{24,8},{28,12},{1,17},{... | collective-permute-start | bytes 196616 | tf_op jit(solution)/shard_map/ppermute | solution.py:384
  47.0 0.3 collective-permute-start.16
  47.2 2.2 %collective-permute-done.14 = bf16[64,512]{1,0:T(8,128)(2,1)S(1)} collective-permute-done((bf16[64,512]{1,0:T(8,128)(2,1)S(1)}, bf16[64,512]{1,0:T(8,128)(2,1)S(1)}, u32[]{:S(2)}, u32[]{:S(2)}) %collective-permute-start.14) | collective-permute-done | bytes 65568 | tf_op jit(solution)/shard_map/ppermute | solution.py:384
  49.5 1.6 %collective-permute-done.15 = bf16[64,512]{1,0:T(8,128)(2,1)S(1)} collective-permute-done((bf16[64,512]{1,0:T(8,128)(2,1)S(1)}, bf16[64,512]{1,0:T(8,128)(2,1)S(1)}, u32[]{:S(2)}, u32[]{:S(2)}) %collective-permute-start.15) | collective-permute-done | bytes 65568 | tf_op jit(solution)/shard_map/ppermute | solution.py:384
  51.0 0.6 %collective-permute-done.16 = bf16[64,512]{1,0:T(8,128)(2,1)S(1)} collective-permute-done((bf16[64,512]{1,0:T(8,128)(2,1)S(1)}, bf16[64,512]{1,0:T(8,128)(2,1)S(1)}, u32[]{:S(2)}, u32[]{:S(2)}) %collective-permute-start.16) | collective-permute-done | bytes 65568 | tf_op jit(solution)/shard_map/ppermute | solution.py:384
  51.6 0.7 %add_bitcast_fusion = f32[1,64,512]{2,1,0:T(8,128)} fusion(bf16[64,512]{1,0:T(8,128)(2,1)S(1)} %collective-permute-done.16, bf16[64,512]{1,0:T(8,128)(2,1)S(1)} %collective-permute-done.15, bf16[64,512]{1,0:T(8,128)(2,1)S(1)} %collective-permute-done.14, bf16[64,512]{1,0:T(8,128)(2,1)S(1)} %get-tuple-element.57), kind=kLoop, calls=%fused_computation | loop fusion | flops 229376 | bytes 393216 | tf_op jit(solution)/shard_map/broadcast_in_dim | solution.py:385
  (14 shorter events, 0.0 us)
Async XLA Ops:
  0.6 1.0 %copy-start.2 = (bf16[256,512]{1,0:T(8,128)(2,1)S(1)}, bf16[256,512]{1,0:T(8,128)(2,1)}, u32[]{:S(2)}) copy-start(bf16[256,512]{1,0:T(8,128)(2,1)} %keys.1) | copy-start | bytes 786436
  1.6 0.9 %copy-start.3 = (bf16[256,512]{1,0:T(8,128)(2,1)S(1)}, bf16[256,512]{1,0:T(8,128)(2,1)}, u32[]{:S(2)}) copy-start(bf16[256,512]{1,0:T(8,128)(2,1)} %values.1) | copy-start | bytes 786436
  2.5 0.7 %copy-start.4 = (s32[2]{0:T(128)S(1)}, s32[2]{0:T(128)}, u32[]{:S(2)}) copy-start(s32[2]{0:T(128)} %tenant_hbm.3) | copy-start | bytes 28
  3.2 0.7 %copy-start.6 = (s32[256]{0:T(256)S(1)}, s32[256]{0:T(256)}, u32[]{:S(2)}) copy-start(s32[256]{0:T(256)} %param.12) | copy-start | bytes 3076
  3.9 20.4 %copy-start.9 = (bf16[256,64]{0,1:T(8,128)(2,1)S(1)}, bf16[256,64]{0,1:T(8,128)(2,1)}, u32[]{:S(2)}) copy-start(bf16[256,64]{0,1:T(8,128)(2,1)} %param.14) | copy-start | bytes 98308
  4.5 6.2 %collective-permute-start.3 = (bf16[272,256]{1,0:T(8,128)(2,1)S(1)}, bf16[272,256]{1,0:T(8,128)(2,1)S(1)}, u32[]{:S(2)}, u32[]{:S(2)}) collective-permute-start(bf16[272,256]{1,0:T(8,128)(2,1)S(1)} %pack.1.refs_2_.refs_3_.own_notes), channel_id=1, source_target_pairs={{0,4},{4,0},{8,12},{12,8},{16,20},{20,16},{24,28},{28,24},{1,5},{5... | collective-permute-start | bytes 417800 | tf_op jit(solution)/shard_map/ppermute | solution.py:367
  5.0 9.9 %collective-permute-start.2 = (bf16[272,256]{1,0:T(8,128)(2,1)S(1)}, bf16[272,256]{1,0:T(8,128)(2,1)S(1)}, u32[]{:S(2)}, u32[]{:S(2)}) collective-permute-start(bf16[272,256]{1,0:T(8,128)(2,1)S(1)} %pack.1.refs_2_.refs_3_.own_notes), channel_id=1, source_target_pairs={{0,24},{4,28},{8,0},{12,4},{16,8},{20,12},{24,16},{28,20},{1,25},{... | collective-permute-start | bytes 417800 | tf_op jit(solution)/shard_map/ppermute | solution.py:366
  9.6 12.6 %collective-permute-start.1 = (bf16[272,256]{1,0:T(8,128)(2,1)S(1)}, bf16[272,256]{1,0:T(8,128)(2,1)S(1)}, u32[]{:S(2)}, u32[]{:S(2)}) collective-permute-start(bf16[272,256]{1,0:T(8,128)(2,1)S(1)} %pack.1.refs_2_.refs_3_.own_notes), channel_id=1, source_target_pairs={{0,16},{4,20},{8,24},{12,28},{16,0},{20,4},{24,8},{28,12},{1,17},{... | collective-permute-start | bytes 417800 | tf_op jit(solution)/shard_map/ppermute | solution.py:366
  9.6 12.6 %collective-permute-start = (bf16[272,256]{1,0:T(8,128)(2,1)S(1)}, bf16[272,256]{1,0:T(8,128)(2,1)S(1)}, u32[]{:S(2)}, u32[]{:S(2)}) collective-permute-start(bf16[272,256]{1,0:T(8,128)(2,1)S(1)} %pack.1.refs_2_.refs_3_.own_notes), channel_id=1, source_target_pairs={{0,8},{4,12},{8,16},{12,20},{16,24},{20,28},{24,0},{28,4},{1,9},{5... | collective-permute-start | bytes 417800 | tf_op jit(solution)/shard_map/ppermute | solution.py:366
  10.7 1.0 %copy-start = (bf16[1,64,4096]{2,1,0:T(8,128)(2,1)S(1)}, bf16[1,64,4096]{2,1,0:T(8,128)(2,1)}, u32[]{:S(2)}) copy-start(bf16[1,64,4096]{2,1,0:T(8,128)(2,1)} %adapter_b.1) | copy-start | bytes 1572868
  11.9 10.4 %collective-permute-start.4 = (bf16[64,1024]{1,0:T(8,128)(2,1)S(1)}, bf16[64,1024]{1,0:T(8,128)(2,1)S(1)}, u32[]{:S(2)}, u32[]{:S(2)}) collective-permute-start(bf16[64,1024]{1,0:T(8,128)(2,1)S(1)} %get-tuple-element.36), channel_id=1, source_target_pairs={{0,1},{1,2},{2,3},{3,0},{4,5},{5,6},{6,7},{7,4},{8,9},{9,10},{10,1... | collective-permute-start | bytes 393224 | tf_op jit(solution)/shard_map/ppermute | solution.py:369
  13.4 8.9 %collective-permute-start.5 = (bf16[64,1024]{1,0:T(8,128)(2,1)S(1)}, bf16[64,1024]{1,0:T(8,128)(2,1)S(1)}, u32[]{:S(2)}, u32[]{:S(2)}) collective-permute-start(bf16[64,1024]{1,0:T(8,128)(2,1)S(1)} %get-tuple-element.37), channel_id=1, source_target_pairs={{0,2},{1,3},{2,0},{3,1},{4,6},{5,7},{6,4},{7,5},{8,10},{9,11},{10,... | collective-permute-start | bytes 393224 | tf_op jit(solution)/shard_map/ppermute | solution.py:369
  14.9 7.4 %collective-permute-start.6 = (bf16[64,1024]{1,0:T(8,128)(2,1)S(1)}, bf16[64,1024]{1,0:T(8,128)(2,1)S(1)}, u32[]{:S(2)}, u32[]{:S(2)}) collective-permute-start(bf16[64,1024]{1,0:T(8,128)(2,1)S(1)} %get-tuple-element.38), channel_id=1, source_target_pairs={{0,3},{1,0},{2,1},{3,2},{4,7},{5,4},{6,5},{7,6},{8,11},{9,8},{10,9... | collective-permute-start | bytes 393224 | tf_op jit(solution)/shard_map/ppermute | solution.py:369
  16.4 1.0 %copy-start.7 = (bf16[256,1024]{1,0:T(8,128)(2,1)S(1)}, bf16[256,1024]{1,0:T(8,128)(2,1)}, u32[]{:S(2)}) copy-start(bf16[256,1024]{1,0:T(8,128)(2,1)} %refs_0_.3) | copy-start | bytes 1572868
  17.4 1.0 %copy-start.8 = (bf16[256,1024]{1,0:T(8,128)(2,1)S(1)}, bf16[256,1024]{1,0:T(8,128)(2,1)}, u32[]{:S(2)}) copy-start(bf16[256,1024]{1,0:T(8,128)(2,1)} %refs_1_.3) | copy-start | bytes 1572868
  22.3 1.4 %collective-permute-start.7 = (bf16[272,256]{1,0:T(8,128)(2,1)S(1)}, bf16[272,256]{1,0:T(8,128)(2,1)S(1)}, u32[]{:S(2)}, u32[]{:S(2)}) collective-permute-start(bf16[272,256]{1,0:T(8,128)(2,1)S(1)} %collective-permute-done.refs_3_), channel_id=1, source_target_pairs={{0,4},{4,0},{8,12},{12,8},{16,20},{20,16},{24,28},{28,24},{1,5},{5... | collective-permute-start | bytes 417800 | tf_op jit(solution)/shard_map/ppermute | solution.py:372
  22.4 1.5 %collective-permute-start.8 = (bf16[272,256]{1,0:T(8,128)(2,1)S(1)}, bf16[272,256]{1,0:T(8,128)(2,1)S(1)}, u32[]{:S(2)}, u32[]{:S(2)}) collective-permute-start(bf16[272,256]{1,0:T(8,128)(2,1)S(1)} %collective-permute-done.1.refs_4_), channel_id=1, source_target_pairs={{0,4},{4,0},{8,12},{12,8},{16,20},{20,16},{24,28},{28,24},{1,5},{5... | collective-permute-start | bytes 417800 | tf_op jit(solution)/shard_map/ppermute | solution.py:372
  22.9 1.4 %collective-permute-start.9 = (bf16[272,256]{1,0:T(8,128)(2,1)S(1)}, bf16[272,256]{1,0:T(8,128)(2,1)S(1)}, u32[]{:S(2)}, u32[]{:S(2)}) collective-permute-start(bf16[272,256]{1,0:T(8,128)(2,1)S(1)} %collective-permute-done.2.refs_5_), channel_id=1, source_target_pairs={{0,4},{4,0},{8,12},{12,8},{16,20},{20,16},{24,28},{28,24},{1,5},{5... | collective-permute-start | bytes 417800 | tf_op jit(solution)/shard_map/ppermute | solution.py:372
  24.2 2.1 %copy-start.5 = (s32[2]{0:T(128)S(1)}, s32[2]{0:T(128)}, u32[]{:S(2)}) copy-start(s32[2]{0:T(128)} %tenant_hbm.3) | copy-start | bytes 28
  26.2 2.4 %collective-permute-start.10 = (bf16[128,512]{1,0:T(8,128)(2,1)S(1)}, bf16[128,512]{1,0:T(8,128)(2,1)S(1)}, u32[]{:S(2)}, u32[]{:S(2)}) collective-permute-start(bf16[128,512]{1,0:T(8,128)(2,1)S(1)} %get-tuple-element.47), channel_id=1, source_target_pairs={{0,4},{4,0},{8,12},{12,8},{16,20},{20,16},{24,28},{28,24},{1,5},{5... | collective-permute-start | bytes 393224 | tf_op jit(solution)/shard_map/ppermute | solution.py:377
  26.4 1.0 %copy-start.1 = (bf16[256,1024]{1,0:T(8,128)(2,1)S(1)}, bf16[256,1024]{1,0:T(8,128)(2,1)}, u32[]{:S(2)}) copy-start(bf16[256,1024]{1,0:T(8,128)(2,1)} %get-tuple-element.29.dq_ref) | copy-start | bytes 1572868
  28.8 5.9 %collective-permute-start.11 = (bf16[80,512]{1,0:T(8,128)(2,1)S(1)}, bf16[80,512]{1,0:T(8,128)(2,1)S(1)}, u32[]{:S(2)}, u32[]{:S(2)}) collective-permute-start(bf16[80,512]{1,0:T(8,128)(2,1)S(1)} %get-tuple-element.53), channel_id=1, source_target_pairs={{0,1},{1,2},{2,3},{3,0},{4,5},{5,6},{6,7},{7,4},{8,9},{9,10},{10,1... | collective-permute-start | bytes 245768 | tf_op jit(solution)/shard_map/ppermute | solution.py:381
  30.3 5.8 %collective-permute-start.12 = (bf16[80,512]{1,0:T(8,128)(2,1)S(1)}, bf16[80,512]{1,0:T(8,128)(2,1)S(1)}, u32[]{:S(2)}, u32[]{:S(2)}) collective-permute-start(bf16[80,512]{1,0:T(8,128)(2,1)S(1)} %get-tuple-element.54), channel_id=1, source_target_pairs={{0,2},{1,3},{2,0},{3,1},{4,6},{5,7},{6,4},{7,5},{8,10},{9,11},{10,... | collective-permute-start | bytes 245768 | tf_op jit(solution)/shard_map/ppermute | solution.py:381
  31.8 4.4 %collective-permute-start.13 = (bf16[80,512]{1,0:T(8,128)(2,1)S(1)}, bf16[80,512]{1,0:T(8,128)(2,1)S(1)}, u32[]{:S(2)}, u32[]{:S(2)}) collective-permute-start(bf16[80,512]{1,0:T(8,128)(2,1)S(1)} %get-tuple-element.55), channel_id=1, source_target_pairs={{0,3},{1,0},{2,1},{3,2},{4,7},{5,4},{6,5},{7,6},{8,11},{9,8},{10,9... | collective-permute-start | bytes 245768 | tf_op jit(solution)/shard_map/ppermute | solution.py:381
  37.0 12.5 %collective-permute-start.14 = (bf16[64,512]{1,0:T(8,128)(2,1)S(1)}, bf16[64,512]{1,0:T(8,128)(2,1)S(1)}, u32[]{:S(2)}, u32[]{:S(2)}) collective-permute-start(bf16[64,512]{1,0:T(8,128)(2,1)S(1)} %get-tuple-element.58), channel_id=1, source_target_pairs={{0,8},{4,12},{8,16},{12,20},{16,24},{20,28},{24,0},{28,4},{1,9},{5... | collective-permute-start | bytes 196616 | tf_op jit(solution)/shard_map/ppermute | solution.py:384
  40.5 10.5 %collective-permute-start.15 = (bf16[64,512]{1,0:T(8,128)(2,1)S(1)}, bf16[64,512]{1,0:T(8,128)(2,1)S(1)}, u32[]{:S(2)}, u32[]{:S(2)}) collective-permute-start(bf16[64,512]{1,0:T(8,128)(2,1)S(1)} %get-tuple-element.59), channel_id=1, source_target_pairs={{0,16},{4,20},{8,24},{12,28},{16,0},{20,4},{24,8},{28,12},{1,17},{... | collective-permute-start | bytes 196616 | tf_op jit(solution)/shard_map/ppermute | solution.py:384
  47.0 4.7 %collective-permute-start.16 = (bf16[64,512]{1,0:T(8,128)(2,1)S(1)}, bf16[64,512]{1,0:T(8,128)(2,1)S(1)}, u32[]{:S(2)}, u32[]{:S(2)}) collective-permute-start(bf16[64,512]{1,0:T(8,128)(2,1)S(1)} %get-tuple-element.60), channel_id=1, source_target_pairs={{0,24},{4,28},{8,0},{12,4},{16,8},{20,12},{24,16},{28,20},{1,25},{... | collective-permute-start | bytes 196616 | tf_op jit(solution)/shard_map/ppermute | solution.py:384

commit v3 on v2

--- a/solution.py
+++ b/solution.py
@@ -15,6 +15,7 @@
 CORES = 2
 PAD = 16
 GROUP = 4
+PACK_LIMIT = (64 << 20) - (1 << 18)
 
 adapter_scale_factor = 2.0
 far_below = -1e30
@@ -72,7 +73,8 @@
             pltpu.SemaphoreType.DMA((4,)),
         ],
         name="pack",
-        **small(1 << 18),
+        compiler_params=pltpu.CompilerParams(vmem_limit_bytes=PACK_LIMIT),
+        cost_estimate=pl.CostEstimate(flops=0, bytes_accessed=1 << 18, transcendentals=0),
     )(block_tenant, keys, values, docs.reshape(1, tokens))
 
 
@@ -98,7 +100,8 @@
         out_shape=[jax.ShapeDtypeStruct((RANK, width), BF16)] * owners,
         scratch_shapes=[pltpu.SemaphoreType.DMA((owners,))],
         name="columns",
-        **small(1 << 19),
+        compiler_params=pltpu.CompilerParams(vmem_limit_bytes=8 << 20),
+        cost_estimate=pl.CostEstimate(flops=1 << 33, bytes_accessed=1 << 19, transcendentals=0),
     )(adapter_b, after)
 
 
@@ -110,7 +113,7 @@
     return jnp.concatenate([x] * times, axis=0)
 
 
-def attend_kernel(shifts, first, last, *refs):
+def attend_kernel(shifts, first, last, owners, *refs):
     refs = list(refs)
     take = lambda count: [refs.pop(0) for _ in range(count)]
     q_ref, g_ref, docs_ref = take(3)
@@ -118,8 +121,12 @@
     if not first:
         top_in, by_key_in, by_grad_in = take(3)
     if last:
-        low_ref, dq_ref, mine_ref, partner_ref = take(4)
+        (low_ref,) = take(1)
+        b_refs = take(owners)
+        dq_hbm, rank_ref, mine_ref, partner_ref = take(4)
     top, by_key, by_grad, bias = take(4)
+    if last:
+        dq_ref, chosen, dq_sem = take(3)
     tokens, width = q_ref.shape
     heads = width // HD
     group = min(GROUP, heads)
@@ -192,14 +199,25 @@
 
     if not last:
         return
+    copies = []
     for h in range(heads):
         part = slice(h * tokens, (h + 1) * tokens)
         inverse = 1.0 / by_key[part, HD:]
         delta = by_grad[part, HD:] * inverse
         dq = (by_grad[part, :HD] - delta * by_key[part, :HD]) * (inverse * logit_scale)
         dq_ref[:, h * HD : (h + 1) * HD] = dq.astype(BF16)
+        if (h + 1) % group == 0:
+            columns = pl.ds((h + 1 - group) * HD, group * HD)
+            copies.append(
+                pltpu.make_async_copy(
+                    dq_ref.at[:, columns], dq_hbm.at[:, columns], dq_sem.at[h // group]
+                )
+            )
+            copies[-1].start()
 
     half = width // CORES
+    adp = lax.axis_index("adp")
+    told = docs_ref[tokens:, :HD].astype(F32)
     for block in range(tokens // BLOCK):
         block_rows = slice(block * BLOCK, (block + 1) * BLOCK)
         partial = adapter_scale_factor * jnp.dot(
@@ -211,8 +229,22 @@
             core == 0, partial[:, half:], partial[:, :half]
         ).astype(BF16)
 
-
-def attend(shifts, queries, grad_out, message, own, other, state=None, low_rank=None):
+        tenant = jnp.max(told[1 + block : 2 + block]).astype(jnp.int32)
+        holder = lax.rem(adp - tenant + owners, owners)
+        for s in range(owners):
+
+            @pl.when(holder == s)
+            def _(s=s):
+                chosen[...] = b_refs[s][...]
+
+        rank_ref[block_rows, :] = adapter_scale_factor * lax.dot_general(
+            dq_ref[block_rows, :], chosen[...], (((1,), (1,)), ((), ())), preferred_element_type=F32
+        )
+    for copy in copies:
+        copy.wait()
+
+
+def attend(shifts, queries, grad_out, message, own, other, state=None, low_rank=None, b_cols=()):
     tokens, width = queries.shape
     heads = width // HD
     blocks = tokens // BLOCK
@@ -228,17 +260,25 @@
     if low_rank is None:
         outs = sums
     else:
-        inputs.append(low_rank.T)
+        inputs += [low_rank.T, *b_cols]
         scratch = [pltpu.VMEM(*each) for each in sums] + scratch
+        scratch += [
+            pltpu.VMEM((tokens, width), BF16),
+            pltpu.VMEM((RANK, width), BF16),
+            pltpu.SemaphoreType.DMA((max(1, heads // GROUP),)),
+        ]
         outs = [
             ((tokens, width), BF16),
+            ((tokens, RANK), F32),
             ((blocks * RANK, width // CORES), F32),
             ((blocks * RANK, width // CORES), BF16),
         ]
     return pl.pallas_call(
-        functools.partial(attend_kernel, shifts, state is None, low_rank is not None),
+        functools.partial(
+            attend_kernel, shifts, state is None, low_rank is not None, len(b_cols)
+        ),
         in_specs=[VMEM] * len(inputs),
-        out_specs=[VMEM] * len(outs),
+        out_specs=([VMEM] if low_rank is None else [ANY]) + [VMEM] * (len(outs) - 1),
         out_shape=[jax.ShapeDtypeStruct(*each) for each in outs],
         scratch_shapes=scratch,
         compiler_params=pltpu.CompilerParams(vmem_limit_bytes=30 << 20),
@@ -249,43 +289,6 @@
         ),
         name="attend_" + "_".join(map(str, shifts[:4])),
     )(*inputs)
-
-
-def ranks_kernel(owners, tenant_hbm, dq_ref, *refs):
-    b_refs, rank_ref, chosen, tenant, sem = refs[:owners], *refs[owners:]
-    copy = pltpu.make_async_copy(tenant_hbm, tenant, sem)
-    copy.start()
-    copy.wait()
-    adp = lax.axis_index("adp")
-    for block in range(dq_ref.shape[0] // BLOCK):
-        block_rows = slice(block * BLOCK, (block + 1) * BLOCK)
-        holder = lax.rem(adp - tenant[block] + owners, owners)
-        for s in range(owners):
-
-            @pl.when(holder == s)
-            def _(s=s):
-                chosen[...] = b_refs[s][...]
-
-        rank_ref[block_rows, :] = adapter_scale_factor * lax.dot_general(
-            dq_ref[block_rows, :], chosen[...], (((1,), (1,)), ((), ())), preferred_element_type=F32
-        )
-
-
-def ranks_of(tenant, dq, b_cols):
-    tokens, width = dq.shape
-    return pl.pallas_call(
-        functools.partial(ranks_kernel, len(b_cols)),
-        in_specs=[HBM] + [VMEM] * (1 + len(b_cols)),
-        out_specs=VMEM,
-        out_shape=jax.ShapeDtypeStruct((tokens, RANK), F32),
-        scratch_shapes=[
-            pltpu.VMEM((RANK, width), BF16),
-            pltpu.SMEM(tenant.shape, jnp.int32),
-            pltpu.SemaphoreType.DMA,
-        ],
-        name="ranks",
-        **small(1 << 20),
-    )(tenant, dq, *b_cols)
 
 
 def tenants_kernel(owners, mine_ref, other_ref, own_notes, other_notes, rank_ref, *outs):
@@ -363,19 +366,26 @@
     along = lambda s: [(a, (a + s) % owners) for a in range(owners)]
 
     message = pack(block_tenant, keys, values, docs, heads_dev)
-    own = [message] + [lax.ppermute(message, "ctx", up(s)) for s in range(1, chips)]
+    far = {s: lax.ppermute(message, "ctx", up(s)) for s in reversed(range(1, chips))}
+    own = [message] + [far[s] for s in range(1, chips)]
     other = [lax.ppermute(message, "ctx", swap)]
     b_out = columns(adapter_b, other[0], owners)
     b_cols = [b_out[0]] + [lax.ppermute(b_out[s], "adp", along(s)) for s in range(1, owners)]
     state = attend((0,), queries, grad_out, message, own[:1], other[:1])
-    own, state, b_cols = lax.optimization_barrier((own, state, b_cols))
+    own[:3], state, b_cols = lax.optimization_barrier((own[:3], state, b_cols))
     other += [lax.ppermute(m, "ctx", swap) for m in own[1:]]
-
-    grad_queries, mine, partner = attend(
-        tuple(range(1, chips)), queries, grad_out, message, own[1:], other[1:], state, low_rank
+    grad_queries, ranks, mine, partner = attend(
+        tuple(range(1, chips)),
+        queries,
+        grad_out,
+        message,
+        own[1:],
+        other[1:],
+        state,
+        low_rank,
+        b_cols,
     )
     other_part = lax.ppermute(partner, "ctx", swap)
-    ranks = ranks_of(block_tenant, grad_queries, b_cols)
     pieces = by_tenant(mine, other_part, message, other[0], ranks, owners)
     pieces = [pieces[0]] + [
         lax.ppermute(pieces[s], "adp", along(s)) for s in range(1, owners)

time: 51.5 us -> 47.4 us (0.920)
  local copies, waits for them, and re-layouts: 7.4 us -> 1.06 us
  waiting for transfers between devices: 9.77 us -> 12.6 us
    unnamed x20 -> x10, local copies, waits for them, and re-layouts: 7.4 us -> 1.06 us
    ppermute x3, waiting for transfers between devices: 1.06 us -> 3.31 us  [on_device(): lax.ppermute(message, 'ctx', up(s))]
    ppermute x1, waiting for transfers between devices: 0.01 us -> 1.15 us  [on_device(): other_part = lax.ppermute(partner, 'ctx', swap)]
    pallas_call x1 -> x0, Pallas kernels: 1.13 us -> none  [ranks_of(): pl.pallas_call(functools.partial(ranks_kernel, len(b_cols)), in_specs=[HB...]
    pallas_call x1, Pallas kernels: 0.59 us -> 1.58 us  [pack(): pl.pallas_call(functools.partial(pack_kernel, heads_dev), in_specs=[HBM]...]
    ppermute x3, waiting for transfers between devices: 4.4 us -> 3.87 us  [on_device(): lax.ppermute(pieces[s], 'ctx', up(s))]
  transfers between devices with their start and end apart: 17 -> 17, of which waited for: 10 -> 11; matrix products, arithmetic and copies ran while one was open for 0% -> 0% of each run, Pallas kernels for 8% -> 6%
where the time goes in v3:
time: 47.4 us; the launch traced here: 48.1 us
  starting transfers between devices  25.9 us (55%)
  waiting for transfers between devices  12.6 us (27%)
  Pallas kernels  7.11 us (15%)
  local copies, waits for them, and re-layouts  1.06 us (2%)
  between operations  0.72 us (2%)
  other arithmetic  0.69 us (1%)
    ppermute x3, starting transfers between devices, on_device(): lax.ppermute(pieces[s], 'ctx', up(s))  9.74 us
    ppermute x3, starting transfers between devices, on_device(): lax.ppermute(message, 'ctx', up(s))  5.67 us
    ppermute x3, starting transfers between devices, on_device(): lax.ppermute(b_out[s], 'adp', along(s))  4.61 us
    ppermute x3, starting transfers between devices, on_device(): lax.ppermute(pieces[s], 'adp', along(s))  4.49 us
    pallas_call x2, Pallas kernels, attend(): pl.pallas_call(functools.partial(attend_kernel, shifts, state is None, lo...  4.48 us
    ppermute x3, waiting for transfers between devices, on_device(): lax.ppermute(pieces[s], 'ctx', up(s))  3.87 us
    ppermute x3, waiting for transfers between devices, on_device(): lax.ppermute(message, 'ctx', up(s))  3.31 us
    ppermute x3, waiting for transfers between devices, on_device(): lax.ppermute(pieces[s], 'adp', along(s))  3 us
  transfers between devices with their start and end apart: 17, of which 11 were waited for; matrix products, arithmetic and copies ran while one was open for 0% of the time, Pallas kernels for 6%

profile of v3, /device:TPU:0, one launch (start us, length us, event | category | flops | bytes accessed | tf_op | source)
XLA Modules:
  0.0 48.1 jit_solution(4381680427884154075)
XLA Ops:
  0.6 1.6 %pack.1.refs_2_.refs_3_.own_notes = bf16[272,256]{1,0:T(8,128)(2,1)} custom-call(s32[2]{0:T(128)} %tenant_hbm.1, bf16[256,512]{1,0:T(8,128)(2,1)} %keys.1, bf16[256,512]{1,0:T(8,128)(2,1)} %values.1, s32[1,256]{1,0:T(1,128)} %bitcast.5), custom_call_target="tpu_custom_call" | custom-call | bytes 262144 | tf_op jit(solution)/shard_map/pack/pallas_call | solution.py:65
  2.2 0.0 copy-start
  2.2 0.5 %collective-permute-start.2 = (bf16[272,256]{1,0:T(8,128)(2,1)}, bf16[272,256]{1,0:T(8,128)(2,1)S(1)}, u32[]{:S(2)}, u32[]{:S(2)}) collective-permute-start(bf16[272,256]{1,0:T(8,128)(2,1)} %pack.1.refs_2_.refs_3_.own_notes), channel_id=1, source_target_pairs={{0,4},{4,0},{8,12},{12,8},{16,20},{20,16},{24,28},{28,24},{1,5},{5... | collective-permute-start | bytes 417800 | tf_op jit(solution)/shard_map/ppermute | solution.py:371
  2.8 4.7 %collective-permute-start.6 = (bf16[272,256]{1,0:T(8,128)(2,1)}, bf16[272,256]{1,0:T(8,128)(2,1)S(1)}, u32[]{:S(2)}, u32[]{:S(2)}) collective-permute-start(bf16[272,256]{1,0:T(8,128)(2,1)} %pack.1.refs_2_.refs_3_.own_notes), channel_id=1, source_target_pairs={{0,24},{4,28},{8,0},{12,4},{16,8},{20,12},{24,16},{28,20},{1,25},{... | collective-permute-start | bytes 417800 | tf_op jit(solution)/shard_map/ppermute | solution.py:369
  7.4 0.0 collective-permute-start.1
  7.4 1.0 %collective-permute-start = (bf16[272,256]{1,0:T(8,128)(2,1)}, bf16[272,256]{1,0:T(8,128)(2,1)S(1)}, u32[]{:S(2)}, u32[]{:S(2)}) collective-permute-start(bf16[272,256]{1,0:T(8,128)(2,1)} %pack.1.refs_2_.refs_3_.own_notes), channel_id=1, source_target_pairs={{0,8},{4,12},{8,16},{12,20},{16,24},{20,28},{24,0},{28,4},{1,9},{5... | collective-permute-start | bytes 417800 | tf_op jit(solution)/shard_map/ppermute | solution.py:369
  8.4 0.0 collective-permute-done.2.refs_4_.after.other_notes
  8.4 1.0 %copy-done.1 = bf16[1,64,4096]{2,1,0:T(8,128)(2,1)S(1)} copy-done((bf16[1,64,4096]{2,1,0:T(8,128)(2,1)S(1)}, bf16[1,64,4096]{2,1,0:T(8,128)(2,1)}, u32[]{:S(2)}) %copy-start.1) | copy-done | bytes 524312
  9.5 0.1 columns.1
  9.6 0.0 copy-start.4
  9.6 1.5 %collective-permute-start.3 = (bf16[64,1024]{1,0:T(8,128)(2,1)S(1)}, bf16[64,1024]{1,0:T(8,128)(2,1)S(1)}, u32[]{:S(2)}, u32[]{:S(2)}) collective-permute-start(bf16[64,1024]{1,0:T(8,128)(2,1)S(1)} %get-tuple-element.36), channel_id=1, source_target_pairs={{0,1},{1,2},{2,3},{3,0},{4,5},{5,6},{6,7},{7,4},{8,9},{9,10},{10,1... | collective-permute-start | bytes 393224 | tf_op jit(solution)/shard_map/ppermute | solution.py:373
  11.2 1.5 %collective-permute-start.4 = (bf16[64,1024]{1,0:T(8,128)(2,1)S(1)}, bf16[64,1024]{1,0:T(8,128)(2,1)S(1)}, u32[]{:S(2)}, u32[]{:S(2)}) collective-permute-start(bf16[64,1024]{1,0:T(8,128)(2,1)S(1)} %get-tuple-element.37), channel_id=1, source_target_pairs={{0,2},{1,3},{2,0},{3,1},{4,6},{5,7},{6,4},{7,5},{8,10},{9,11},{10,... | collective-permute-start | bytes 393224 | tf_op jit(solution)/shard_map/ppermute | solution.py:373
  12.7 0.0 collective-permute-done.6.refs_5_
  12.7 1.6 %collective-permute-start.5 = (bf16[64,1024]{1,0:T(8,128)(2,1)S(1)}, bf16[64,1024]{1,0:T(8,128)(2,1)S(1)}, u32[]{:S(2)}, u32[]{:S(2)}) collective-permute-start(bf16[64,1024]{1,0:T(8,128)(2,1)S(1)} %get-tuple-element.38), channel_id=1, source_target_pairs={{0,3},{1,0},{2,1},{3,2},{4,7},{5,4},{6,5},{7,6},{8,11},{9,8},{10,9... | collective-permute-start | bytes 393224 | tf_op jit(solution)/shard_map/ppermute | solution.py:373
  14.3 0.0 copy-done
  14.3 0.0 copy-done.2
  14.3 0.0 copy-done.3
  14.3 2.7 %attend_0.1 = (f32[2048,128]{1,0:T(8,128)S(1)}, f32[2048,256]{1,0:T(8,128)S(1)}, f32[2048,256]{1,0:T(8,128)S(1)}) custom-call(bf16[256,1024]{1,0:T(8,128)(2,1)S(1)} %copy-done.2, bf16[256,1024]{1,0:T(8,128)(2,1)S(1)} %copy-done.3, bf16[272,256]{1,0:T(8,128)(2,1)S(1)} %copy-done, bf16[272,256]{1,0:T(8,128)(2,1)S(1)} %copy-done, ...), custom_call_target="tpu_custom_call" | custom-call | flops 805306368 | bytes 4194304 | tf_op jit(solution)/shard_map/attend_0/pallas_call | solution.py:276
  16.9 3.3 %collective-permute-done.1.refs_4_ = bf16[272,256]{1,0:T(8,128)(2,1)S(1)} collective-permute-done((bf16[272,256]{1,0:T(8,128)(2,1)}, bf16[272,256]{1,0:T(8,128)(2,1)S(1)}, u32[]{:S(2)}, u32[]{:S(2)}) %collective-permute-start.1) | collective-permute-done | bytes 139296 | tf_op jit(solution)/shard_map/ppermute | solution.py:369
  20.2 0.0 collective-permute-start.9
  20.2 0.0 collective-permute-done.refs_3_
  20.2 0.0 collective-permute-done.3.refs_14_
  20.2 0.0 collective-permute-done.4.refs_15_
  20.3 0.0 collective-permute-done.5.refs_16_
  20.3 0.6 %collective-permute-start.7 = (bf16[272,256]{1,0:T(8,128)(2,1)S(1)}, bf16[272,256]{1,0:T(8,128)(2,1)S(1)}, u32[]{:S(2)}, u32[]{:S(2)}) collective-permute-start(bf16[272,256]{1,0:T(8,128)(2,1)S(1)} %collective-permute-done.refs_3_), channel_id=1, source_target_pairs={{0,4},{4,0},{8,12},{12,8},{16,20},{20,16},{24,28},{28,24},{1,5},{5... | collective-permute-start | bytes 417800 | tf_op jit(solution)/shard_map/ppermute | solution.py:376
  20.8 0.1 collective-permute-start.8
  20.9 0.7 %collective-permute-done.9.refs_8_ = bf16[272,256]{1,0:T(8,128)(2,1)S(1)} collective-permute-done((bf16[272,256]{1,0:T(8,128)(2,1)S(1)}, bf16[272,256]{1,0:T(8,128)(2,1)S(1)}, u32[]{:S(2)}, u32[]{:S(2)}) %collective-permute-start.9) | collective-permute-done | bytes 139296 | tf_op jit(solution)/shard_map/ppermute | solution.py:376
  21.6 0.2 collective-permute-done.7.refs_6_
  21.8 0.4 collective-permute-done.8.refs_7_
  22.2 0.0 copy-done.4
  22.2 1.8 %attend_1_2_3.1 = (bf16[256,1024]{1,0:T(8,128)(2,1)}, f32[256,64]{1,0:T(8,128)S(1)}, f32[128,512]{1,0:T(8,128)S(1)}, bf16[128,512]{1,0:T(8,128)(2,1)S(1)}) custom-call(bf16[256,1024]{1,0:T(8,128)(2,1)S(1)} %copy-done.2, bf16[256,1024]{1,0:T(8,128)(2,1)S(1)} %copy-done.3, bf16[272,256]{1,0:T(8,128)(2,1)S(1)} %copy-done, ...), custom_call_target="tpu_custom_call" | custom-call | flops 2415919104 | bytes 4194304 | tf_op jit(solution)/shard_map/attend_1_2_3/pallas_call | solution.py:276
  24.0 0.3 collective-permute-start.10
  24.3 1.2 %collective-permute-done.10.other_ref = bf16[128,512]{1,0:T(8,128)(2,1)S(1)} collective-permute-done((bf16[128,512]{1,0:T(8,128)(2,1)S(1)}, bf16[128,512]{1,0:T(8,128)(2,1)S(1)}, u32[]{:S(2)}, u32[]{:S(2)}) %collective-permute-start.10) | collective-permute-done | bytes 131104 | tf_op jit(solution)/shard_map/ppermute | solution.py:388
  25.4 0.2 by_tenant.1
  25.6 1.5 %collective-permute-start.11 = (bf16[80,512]{1,0:T(8,128)(2,1)S(1)}, bf16[80,512]{1,0:T(8,128)(2,1)S(1)}, u32[]{:S(2)}, u32[]{:S(2)}) collective-permute-start(bf16[80,512]{1,0:T(8,128)(2,1)S(1)} %get-tuple-element.53), channel_id=1, source_target_pairs={{0,1},{1,2},{2,3},{3,0},{4,5},{5,6},{6,7},{7,4},{8,9},{9,10},{10,1... | collective-permute-start | bytes 245768 | tf_op jit(solution)/shard_map/ppermute | solution.py:391
  27.2 1.5 %collective-permute-start.12 = (bf16[80,512]{1,0:T(8,128)(2,1)S(1)}, bf16[80,512]{1,0:T(8,128)(2,1)S(1)}, u32[]{:S(2)}, u32[]{:S(2)}) collective-permute-start(bf16[80,512]{1,0:T(8,128)(2,1)S(1)} %get-tuple-element.54), channel_id=1, source_target_pairs={{0,2},{1,3},{2,0},{3,1},{4,6},{5,7},{6,4},{7,5},{8,10},{9,11},{10,... | collective-permute-start | bytes 245768 | tf_op jit(solution)/shard_map/ppermute | solution.py:391
  28.7 1.4 %collective-permute-start.13 = (bf16[80,512]{1,0:T(8,128)(2,1)S(1)}, bf16[80,512]{1,0:T(8,128)(2,1)S(1)}, u32[]{:S(2)}, u32[]{:S(2)}) collective-permute-start(bf16[80,512]{1,0:T(8,128)(2,1)S(1)} %get-tuple-element.55), channel_id=1, source_target_pairs={{0,3},{1,0},{2,1},{3,2},{4,7},{5,4},{6,5},{7,6},{8,11},{9,8},{10,9... | collective-permute-start | bytes 245768 | tf_op jit(solution)/shard_map/ppermute | solution.py:391
  30.1 1.3 %collective-permute-done.11.refs_1_ = bf16[80,512]{1,0:T(8,128)(2,1)S(1)} collective-permute-done((bf16[80,512]{1,0:T(8,128)(2,1)S(1)}, bf16[80,512]{1,0:T(8,128)(2,1)S(1)}, u32[]{:S(2)}, u32[]{:S(2)}) %collective-permute-start.11) | collective-permute-done | bytes 81952 | tf_op jit(solution)/shard_map/ppermute | solution.py:391
  31.4 1.5 %collective-permute-done.12.refs_2_ = bf16[80,512]{1,0:T(8,128)(2,1)S(1)} collective-permute-done((bf16[80,512]{1,0:T(8,128)(2,1)S(1)}, bf16[80,512]{1,0:T(8,128)(2,1)S(1)}, u32[]{:S(2)}, u32[]{:S(2)}) %collective-permute-start.12) | collective-permute-done | bytes 81952 | tf_op jit(solution)/shard_map/ppermute | solution.py:391
  32.9 0.2 collective-permute-done.13.refs_3_
  33.1 0.7 %by_columns_owner.1 = (bf16[64,512]{1,0:T(8,128)(2,1)S(1)}, bf16[64,512]{1,0:T(8,128)(2,1)S(1)}, bf16[64,512]{1,0:T(8,128)(2,1)S(1)}, bf16[64,512]{1,0:T(8,128)(2,1)S(1)}, f32[64,64]{1,0:T(8,128)}) custom-call(bf16[80,512]{1,0:T(8,128)(2,1)S(1)} %get-tuple-element.52.refs_0_, bf16[80,512]{1,0:T(8,128)(2,1)S(1)} %collective-permute-done.11.refs_1_, ...), custom_call_target="tpu_custom_call" | custom-call | bytes 1048576 | tf_op jit(solution)/shard_map/by_columns_owner/pallas_call | solution.py:348
  33.8 2.6 %collective-permute-start.14 = (bf16[64,512]{1,0:T(8,128)(2,1)S(1)}, bf16[64,512]{1,0:T(8,128)(2,1)S(1)}, u32[]{:S(2)}, u32[]{:S(2)}) collective-permute-start(bf16[64,512]{1,0:T(8,128)(2,1)S(1)} %get-tuple-element.58), channel_id=1, source_target_pairs={{0,8},{4,12},{8,16},{12,20},{16,24},{20,28},{24,0},{28,4},{1,9},{5... | collective-permute-start | bytes 196616 | tf_op jit(solution)/shard_map/ppermute | solution.py:394
  36.4 6.2 %collective-permute-start.15 = (bf16[64,512]{1,0:T(8,128)(2,1)S(1)}, bf16[64,512]{1,0:T(8,128)(2,1)S(1)}, u32[]{:S(2)}, u32[]{:S(2)}) collective-permute-start(bf16[64,512]{1,0:T(8,128)(2,1)S(1)} %get-tuple-element.59), channel_id=1, source_target_pairs={{0,16},{4,20},{8,24},{12,28},{16,0},{20,4},{24,8},{28,12},{1,17},{... | collective-permute-start | bytes 196616 | tf_op jit(solution)/shard_map/ppermute | solution.py:394
  42.7 0.9 %collective-permute-start.16 = (bf16[64,512]{1,0:T(8,128)(2,1)S(1)}, bf16[64,512]{1,0:T(8,128)(2,1)S(1)}, u32[]{:S(2)}, u32[]{:S(2)}) collective-permute-start(bf16[64,512]{1,0:T(8,128)(2,1)S(1)} %get-tuple-element.60), channel_id=1, source_target_pairs={{0,24},{4,28},{8,0},{12,4},{16,8},{20,12},{24,16},{28,20},{1,25},{... | collective-permute-start | bytes 196616 | tf_op jit(solution)/shard_map/ppermute | solution.py:394
  43.6 1.3 %collective-permute-done.14 = bf16[64,512]{1,0:T(8,128)(2,1)S(1)} collective-permute-done((bf16[64,512]{1,0:T(8,128)(2,1)S(1)}, bf16[64,512]{1,0:T(8,128)(2,1)S(1)}, u32[]{:S(2)}, u32[]{:S(2)}) %collective-permute-start.14) | collective-permute-done | bytes 65568 | tf_op jit(solution)/shard_map/ppermute | solution.py:394
  44.9 2.2 %collective-permute-done.15 = bf16[64,512]{1,0:T(8,128)(2,1)S(1)} collective-permute-done((bf16[64,512]{1,0:T(8,128)(2,1)S(1)}, bf16[64,512]{1,0:T(8,128)(2,1)S(1)}, u32[]{:S(2)}, u32[]{:S(2)}) %collective-permute-start.15) | collective-permute-done | bytes 65568 | tf_op jit(solution)/shard_map/ppermute | solution.py:394
  47.1 0.3 collective-permute-done.16
  47.5 0.7 %add_bitcast_fusion = f32[1,64,512]{2,1,0:T(8,128)} fusion(bf16[64,512]{1,0:T(8,128)(2,1)S(1)} %collective-permute-done.16, bf16[64,512]{1,0:T(8,128)(2,1)S(1)} %collective-permute-done.15, bf16[64,512]{1,0:T(8,128)(2,1)S(1)} %collective-permute-done.14, bf16[64,512]{1,0:T(8,128)(2,1)S(1)} %get-tuple-element.57), kind=kLoop, calls=%fused_computation | loop fusion | flops 229376 | bytes 393216 | tf_op jit(solution)/shard_map/broadcast_in_dim | solution.py:395
  (3 shorter events, 0.0 us)
Async XLA Ops:
  2.2 12.0 %copy-start = (bf16[272,256]{1,0:T(8,128)(2,1)S(1)}, bf16[272,256]{1,0:T(8,128)(2,1)}, u32[]{:S(2)}) copy-start(bf16[272,256]{1,0:T(8,128)(2,1)} %pack.1.refs_2_.refs_3_.own_notes) | copy-start | bytes 417796
  2.2 6.2 %collective-permute-start.2 = (bf16[272,256]{1,0:T(8,128)(2,1)}, bf16[272,256]{1,0:T(8,128)(2,1)S(1)}, u32[]{:S(2)}, u32[]{:S(2)}) collective-permute-start(bf16[272,256]{1,0:T(8,128)(2,1)} %pack.1.refs_2_.refs_3_.own_notes), channel_id=1, source_target_pairs={{0,4},{4,0},{8,12},{12,8},{16,20},{20,16},{24,28},{28,24},{1,5},{5... | collective-permute-start | bytes 417800 | tf_op jit(solution)/shard_map/ppermute | solution.py:371
  2.8 10.0 %collective-permute-start.6 = (bf16[272,256]{1,0:T(8,128)(2,1)}, bf16[272,256]{1,0:T(8,128)(2,1)S(1)}, u32[]{:S(2)}, u32[]{:S(2)}) collective-permute-start(bf16[272,256]{1,0:T(8,128)(2,1)} %pack.1.refs_2_.refs_3_.own_notes), channel_id=1, source_target_pairs={{0,24},{4,28},{8,0},{12,4},{16,8},{20,12},{24,16},{28,20},{1,25},{... | collective-permute-start | bytes 417800 | tf_op jit(solution)/shard_map/ppermute | solution.py:369
  7.4 12.8 %collective-permute-start.1 = (bf16[272,256]{1,0:T(8,128)(2,1)}, bf16[272,256]{1,0:T(8,128)(2,1)S(1)}, u32[]{:S(2)}, u32[]{:S(2)}) collective-permute-start(bf16[272,256]{1,0:T(8,128)(2,1)} %pack.1.refs_2_.refs_3_.own_notes), channel_id=1, source_target_pairs={{0,16},{4,20},{8,24},{12,28},{16,0},{20,4},{24,8},{28,12},{1,17},{... | collective-permute-start | bytes 417800 | tf_op jit(solution)/shard_map/ppermute | solution.py:369
  7.4 12.8 %collective-permute-start = (bf16[272,256]{1,0:T(8,128)(2,1)}, bf16[272,256]{1,0:T(8,128)(2,1)S(1)}, u32[]{:S(2)}, u32[]{:S(2)}) collective-permute-start(bf16[272,256]{1,0:T(8,128)(2,1)} %pack.1.refs_2_.refs_3_.own_notes), channel_id=1, source_target_pairs={{0,8},{4,12},{8,16},{12,20},{16,24},{20,28},{24,0},{28,4},{1,9},{5... | collective-permute-start | bytes 417800 | tf_op jit(solution)/shard_map/ppermute | solution.py:369
  8.4 1.0 %copy-start.1 = (bf16[1,64,4096]{2,1,0:T(8,128)(2,1)S(1)}, bf16[1,64,4096]{2,1,0:T(8,128)(2,1)}, u32[]{:S(2)}) copy-start(bf16[1,64,4096]{2,1,0:T(8,128)(2,1)} %adapter_b.1) | copy-start | bytes 1572868
  9.5 4.8 %copy-start.2 = (bf16[256,1024]{1,0:T(8,128)(2,1)S(1)}, bf16[256,1024]{1,0:T(8,128)(2,1)}, u32[]{:S(2)}) copy-start(bf16[256,1024]{1,0:T(8,128)(2,1)} %refs_0_.3) | copy-start | bytes 1572868
  9.5 4.8 %copy-start.3 = (bf16[256,1024]{1,0:T(8,128)(2,1)S(1)}, bf16[256,1024]{1,0:T(8,128)(2,1)}, u32[]{:S(2)}) copy-start(bf16[256,1024]{1,0:T(8,128)(2,1)} %refs_1_.3) | copy-start | bytes 1572868
  9.6 12.6 %copy-start.4 = (bf16[256,64]{0,1:T(8,128)(2,1)S(1)}, bf16[256,64]{0,1:T(8,128)(2,1)}, u32[]{:S(2)}) copy-start(bf16[256,64]{0,1:T(8,128)(2,1)} %param.14) | copy-start | bytes 98308
  9.6 10.6 %collective-permute-start.3 = (bf16[64,1024]{1,0:T(8,128)(2,1)S(1)}, bf16[64,1024]{1,0:T(8,128)(2,1)S(1)}, u32[]{:S(2)}, u32[]{:S(2)}) collective-permute-start(bf16[64,1024]{1,0:T(8,128)(2,1)S(1)} %get-tuple-element.36), channel_id=1, source_target_pairs={{0,1},{1,2},{2,3},{3,0},{4,5},{5,6},{6,7},{7,4},{8,9},{9,10},{10,1... | collective-permute-start | bytes 393224 | tf_op jit(solution)/shard_map/ppermute | solution.py:373
  11.2 9.1 %collective-permute-start.4 = (bf16[64,1024]{1,0:T(8,128)(2,1)S(1)}, bf16[64,1024]{1,0:T(8,128)(2,1)S(1)}, u32[]{:S(2)}, u32[]{:S(2)}) collective-permute-start(bf16[64,1024]{1,0:T(8,128)(2,1)S(1)} %get-tuple-element.37), channel_id=1, source_target_pairs={{0,2},{1,3},{2,0},{3,1},{4,6},{5,7},{6,4},{7,5},{8,10},{9,11},{10,... | collective-permute-start | bytes 393224 | tf_op jit(solution)/shard_map/ppermute | solution.py:373
  12.7 7.6 %collective-permute-start.5 = (bf16[64,1024]{1,0:T(8,128)(2,1)S(1)}, bf16[64,1024]{1,0:T(8,128)(2,1)S(1)}, u32[]{:S(2)}, u32[]{:S(2)}) collective-permute-start(bf16[64,1024]{1,0:T(8,128)(2,1)S(1)} %get-tuple-element.38), channel_id=1, source_target_pairs={{0,3},{1,0},{2,1},{3,2},{4,7},{5,4},{6,5},{7,6},{8,11},{9,8},{10,9... | collective-permute-start | bytes 393224 | tf_op jit(solution)/shard_map/ppermute | solution.py:373
  20.2 1.4 %collective-permute-start.9 = (bf16[272,256]{1,0:T(8,128)(2,1)S(1)}, bf16[272,256]{1,0:T(8,128)(2,1)S(1)}, u32[]{:S(2)}, u32[]{:S(2)}) collective-permute-start(bf16[272,256]{1,0:T(8,128)(2,1)S(1)} %collective-permute-done.6.refs_5_), channel_id=1, source_target_pairs={{0,4},{4,0},{8,12},{12,8},{16,20},{20,16},{24,28},{28,24},{1,5},{5... | collective-permute-start | bytes 417800 | tf_op jit(solution)/shard_map/ppermute | solution.py:376
  20.3 1.6 %collective-permute-start.7 = (bf16[272,256]{1,0:T(8,128)(2,1)S(1)}, bf16[272,256]{1,0:T(8,128)(2,1)S(1)}, u32[]{:S(2)}, u32[]{:S(2)}) collective-permute-start(bf16[272,256]{1,0:T(8,128)(2,1)S(1)} %collective-permute-done.refs_3_), channel_id=1, source_target_pairs={{0,4},{4,0},{8,12},{12,8},{16,20},{20,16},{24,28},{28,24},{1,5},{5... | collective-permute-start | bytes 417800 | tf_op jit(solution)/shard_map/ppermute | solution.py:376
  20.8 1.4 %collective-permute-start.8 = (bf16[272,256]{1,0:T(8,128)(2,1)S(1)}, bf16[272,256]{1,0:T(8,128)(2,1)S(1)}, u32[]{:S(2)}, u32[]{:S(2)}) collective-permute-start(bf16[272,256]{1,0:T(8,128)(2,1)S(1)} %collective-permute-done.1.refs_4_), channel_id=1, source_target_pairs={{0,4},{4,0},{8,12},{12,8},{16,20},{20,16},{24,28},{28,24},{1,5},{5... | collective-permute-start | bytes 417800 | tf_op jit(solution)/shard_map/ppermute | solution.py:376
  24.0 1.4 %collective-permute-start.10 = (bf16[128,512]{1,0:T(8,128)(2,1)S(1)}, bf16[128,512]{1,0:T(8,128)(2,1)S(1)}, u32[]{:S(2)}, u32[]{:S(2)}) collective-permute-start(bf16[128,512]{1,0:T(8,128)(2,1)S(1)} %get-tuple-element.50), channel_id=1, source_target_pairs={{0,4},{4,0},{8,12},{12,8},{16,20},{20,16},{24,28},{28,24},{1,5},{5... | collective-permute-start | bytes 393224 | tf_op jit(solution)/shard_map/ppermute | solution.py:388
  25.6 5.8 %collective-permute-start.11 = (bf16[80,512]{1,0:T(8,128)(2,1)S(1)}, bf16[80,512]{1,0:T(8,128)(2,1)S(1)}, u32[]{:S(2)}, u32[]{:S(2)}) collective-permute-start(bf16[80,512]{1,0:T(8,128)(2,1)S(1)} %get-tuple-element.53), channel_id=1, source_target_pairs={{0,1},{1,2},{2,3},{3,0},{4,5},{5,6},{6,7},{7,4},{8,9},{9,10},{10,1... | collective-permute-start | bytes 245768 | tf_op jit(solution)/shard_map/ppermute | solution.py:391
  27.2 5.7 %collective-permute-start.12 = (bf16[80,512]{1,0:T(8,128)(2,1)S(1)}, bf16[80,512]{1,0:T(8,128)(2,1)S(1)}, u32[]{:S(2)}, u32[]{:S(2)}) collective-permute-start(bf16[80,512]{1,0:T(8,128)(2,1)S(1)} %get-tuple-element.54), channel_id=1, source_target_pairs={{0,2},{1,3},{2,0},{3,1},{4,6},{5,7},{6,4},{7,5},{8,10},{9,11},{10,... | collective-permute-start | bytes 245768 | tf_op jit(solution)/shard_map/ppermute | solution.py:391
  28.7 4.4 %collective-permute-start.13 = (bf16[80,512]{1,0:T(8,128)(2,1)S(1)}, bf16[80,512]{1,0:T(8,128)(2,1)S(1)}, u32[]{:S(2)}, u32[]{:S(2)}) collective-permute-start(bf16[80,512]{1,0:T(8,128)(2,1)S(1)} %get-tuple-element.55), channel_id=1, source_target_pairs={{0,3},{1,0},{2,1},{3,2},{4,7},{5,4},{6,5},{7,6},{8,11},{9,8},{10,9... | collective-permute-start | bytes 245768 | tf_op jit(solution)/shard_map/ppermute | solution.py:391
  33.8 11.1 %collective-permute-start.14 = (bf16[64,512]{1,0:T(8,128)(2,1)S(1)}, bf16[64,512]{1,0:T(8,128)(2,1)S(1)}, u32[]{:S(2)}, u32[]{:S(2)}) collective-permute-start(bf16[64,512]{1,0:T(8,128)(2,1)S(1)} %get-tuple-element.58), channel_id=1, source_target_pairs={{0,8},{4,12},{8,16},{12,20},{16,24},{20,28},{24,0},{28,4},{1,9},{5... | collective-permute-start | bytes 196616 | tf_op jit(solution)/shard_map/ppermute | solution.py:394
  36.4 10.7 %collective-permute-start.15 = (bf16[64,512]{1,0:T(8,128)(2,1)S(1)}, bf16[64,512]{1,0:T(8,128)(2,1)S(1)}, u32[]{:S(2)}, u32[]{:S(2)}) collective-permute-start(bf16[64,512]{1,0:T(8,128)(2,1)S(1)} %get-tuple-element.59), channel_id=1, source_target_pairs={{0,16},{4,20},{8,24},{12,28},{16,0},{20,4},{24,8},{28,12},{1,17},{... | collective-permute-start | bytes 196616 | tf_op jit(solution)/shard_map/ppermute | solution.py:394
  42.7 4.8 %collective-permute-start.16 = (bf16[64,512]{1,0:T(8,128)(2,1)S(1)}, bf16[64,512]{1,0:T(8,128)(2,1)S(1)}, u32[]{:S(2)}, u32[]{:S(2)}) collective-permute-start(bf16[64,512]{1,0:T(8,128)(2,1)S(1)} %get-tuple-element.60), channel_id=1, source_target_pairs={{0,24},{4,28},{8,0},{12,4},{16,8},{20,12},{24,16},{28,20},{1,25},{... | collective-permute-start | bytes 196616 | tf_op jit(solution)/shard_map/ppermute | solution.py:394

commit v4 on v3

--- a/solution.py
+++ b/solution.py
@@ -123,10 +123,10 @@
     if last:
         (low_ref,) = take(1)
         b_refs = take(owners)
-        dq_hbm, rank_ref, mine_ref, partner_ref = take(4)
+        dq_ref, rank_ref, mine_ref, partner_ref = take(4)
     top, by_key, by_grad, bias = take(4)
     if last:
-        dq_ref, chosen, dq_sem = take(3)
+        (chosen,) = take(1)
     tokens, width = q_ref.shape
     heads = width // HD
     group = min(GROUP, heads)
@@ -199,21 +199,12 @@
 
     if not last:
         return
-    copies = []
     for h in range(heads):
         part = slice(h * tokens, (h + 1) * tokens)
         inverse = 1.0 / by_key[part, HD:]
         delta = by_grad[part, HD:] * inverse
         dq = (by_grad[part, :HD] - delta * by_key[part, :HD]) * (inverse * logit_scale)
         dq_ref[:, h * HD : (h + 1) * HD] = dq.astype(BF16)
-        if (h + 1) % group == 0:
-            columns = pl.ds((h + 1 - group) * HD, group * HD)
-            copies.append(
-                pltpu.make_async_copy(
-                    dq_ref.at[:, columns], dq_hbm.at[:, columns], dq_sem.at[h // group]
-                )
-            )
-            copies[-1].start()
 
     half = width // CORES
     adp = lax.axis_index("adp")
@@ -240,8 +231,6 @@
         rank_ref[block_rows, :] = adapter_scale_factor * lax.dot_general(
             dq_ref[block_rows, :], chosen[...], (((1,), (1,)), ((), ())), preferred_element_type=F32
         )
-    for copy in copies:
-        copy.wait()
 
 
 def attend(shifts, queries, grad_out, message, own, other, state=None, low_rank=None, b_cols=()):
@@ -263,9 +252,7 @@
         inputs += [low_rank.T, *b_cols]
         scratch = [pltpu.VMEM(*each) for each in sums] + scratch
         scratch += [
-            pltpu.VMEM((tokens, width), BF16),
             pltpu.VMEM((RANK, width), BF16),
-            pltpu.SemaphoreType.DMA((max(1, heads // GROUP),)),
         ]
         outs = [
             ((tokens, width), BF16),
@@ -278,7 +265,7 @@
             attend_kernel, shifts, state is None, low_rank is not None, len(b_cols)
         ),
         in_specs=[VMEM] * len(inputs),
-        out_specs=([VMEM] if low_rank is None else [ANY]) + [VMEM] * (len(outs) - 1),
+        out_specs=[VMEM] * len(outs),
         out_shape=[jax.ShapeDtypeStruct(*each) for each in outs],
         scratch_shapes=scratch,
         compiler_params=pltpu.CompilerParams(vmem_limit_bytes=30 << 20),
@@ -325,35 +312,57 @@
 
 
 def columns_owner_kernel(owners, *refs):
-    pieces, outs, rank_out = refs[:owners], refs[owners:-1], refs[-1]
+    pieces, outs = refs[:owners], refs[owners:]
     ctx, adp = lax.axis_index("ctx"), lax.axis_index("adp")
     z = ctx // CORES
-    share = rank_out.shape[0]
-    for part in range(share // PAD):
+    for s in range(owners):
+        source = lax.rem(adp - z - s + 2 * owners, owners)
+        for j in range(owners):
+
+            @pl.when(source == j)
+            def _(s=s, j=j):
+                outs[s][...] = pieces[j][:RANK, :]
+
+
+def by_columns_owner(pieces):
+    owners = len(pieces)
+    width = pieces[0].shape[1]
+    return pl.pallas_call(
+        functools.partial(columns_owner_kernel, owners),
+        in_specs=[VMEM] * owners,
+        out_specs=[VMEM] * owners,
+        out_shape=[jax.ShapeDtypeStruct((RANK, width), BF16)] * owners,
+        name="by_columns_owner",
+        **small(1 << 20),
+    )(*pieces)
+
+
+def finish_kernel(owners, *refs):
+    dq_ref, pieces = refs[0], refs[1 : owners + 1]
+    dq_hbm, rank_out, sem = refs[owners + 1 :]
+    copy = pltpu.make_async_copy(dq_ref, dq_hbm, sem)
+    copy.start()
+    for part in range(rank_out.shape[0] // PAD):
         rank_out[part * PAD : (part + 1) * PAD, :] = sum(
             piece[RANK:, part * HD : part * HD + RANK].astype(F32) for piece in pieces
         )
-    for s in range(owners):
-        source = lax.rem(adp - z - s + 2 * owners, owners)
-        for j in range(owners):
-
-            @pl.when(source == j)
-            def _(s=s, j=j):
-                outs[s][...] = pieces[j][:RANK, :]
-
-
-def by_columns_owner(pieces, share):
+    copy.wait()
+
+
+def finish(dq, pieces, share):
     owners = len(pieces)
-    width = pieces[0].shape[1]
-    return pl.pallas_call(
-        functools.partial(columns_owner_kernel, owners),
-        in_specs=[VMEM] * owners,
-        out_specs=[VMEM] * (owners + 1),
-        out_shape=[jax.ShapeDtypeStruct((RANK, width), BF16)] * owners
-        + [jax.ShapeDtypeStruct((share, RANK), F32)],
-        name="by_columns_owner",
+    return pl.pallas_call(
+        functools.partial(finish_kernel, owners),
+        in_specs=[VMEM] * (1 + owners),
+        out_specs=[ANY, VMEM],
+        out_shape=[
+            jax.ShapeDtypeStruct(dq.shape, BF16),
+            jax.ShapeDtypeStruct((share, RANK), F32),
+        ],
+        scratch_shapes=[pltpu.SemaphoreType.DMA],
+        name="finish",
         **small(1 << 20),
-    )(*pieces)
+    )(dq, *pieces)
 
 
 def on_device(queries, keys, values, grad_out, docs, block_tenant, low_rank, adapter_b):
@@ -372,15 +381,18 @@
     b_out = columns(adapter_b, other[0], owners)
     b_cols = [b_out[0]] + [lax.ppermute(b_out[s], "adp", along(s)) for s in range(1, owners)]
     state = attend((0,), queries, grad_out, message, own[:1], other[:1])
-    own[:3], state, b_cols = lax.optimization_barrier((own[:3], state, b_cols))
-    other += [lax.ppermute(m, "ctx", swap) for m in own[1:]]
+    own[-1], b_cols[1] = lax.optimization_barrier((own[-1], b_cols[1]))
+    far_other = lax.ppermute(own[-1], "ctx", swap)
+    near, state, b_cols = lax.optimization_barrier((own[1:-1], state, b_cols))
+    near_other = [lax.ppermute(m, "ctx", swap) for m in near]
+    state = attend((chips - 1,), queries, grad_out, message, own[-1:], [far_other], state)
     grad_queries, ranks, mine, partner = attend(
-        tuple(range(1, chips)),
+        tuple(range(1, chips - 1)),
         queries,
         grad_out,
         message,
-        own[1:],
-        other[1:],
+        near,
+        near_other,
         state,
         low_rank,
         b_cols,
@@ -390,7 +402,8 @@
     pieces = [pieces[0]] + [
         lax.ppermute(pieces[s], "adp", along(s)) for s in range(1, owners)
     ]
-    *pieces, grad_low_rank = by_columns_owner(pieces, tokens // owners)
+    grad_queries, grad_low_rank = finish(grad_queries, pieces, tokens // owners)
+    pieces = by_columns_owner(pieces)
     pieces = [pieces[0]] + [lax.ppermute(pieces[s], "ctx", up(s)) for s in range(1, chips)]
     grad_adapter = sum(piece.astype(F32) for piece in pieces)[None]
     return grad_queries, grad_low_rank, grad_adapter

time: 47.4 us -> 46.6 us (0.983); the launches traced: 48.1 us -> 46.4 us
  waiting for transfers between devices: 12.6 us -> 8.76 us
  Pallas kernels: 7.11 us -> 8.16 us
  starting transfers between devices: 25.9 us -> 26.9 us
    ppermute x3, waiting for transfers between devices: 3.87 us -> 0.64 us  [on_device(): lax.ppermute(pieces[s], 'ctx', up(s))]
    pallas_call x0 -> x1, Pallas kernels: none -> 1.41 us  [finish(): pl.pallas_call(functools.partial(finish_kernel, owners), in_specs=[VMEM]...]
    ppermute x3, starting transfers between devices: 5.67 us -> 6.73 us  [on_device(): lax.ppermute(message, 'ctx', up(s))]
    ppermute x3, waiting for transfers between devices: 1.28 us -> 0.57 us  [the longest x2 0.57 us: on_device(): near_other = [lax.ppermute(m, 'ctx', swap) for m in near]]
    pallas_call x1, Pallas kernels: 0.72 us -> 0.05 us  [by_columns_owner(): pl.pallas_call(functools.partial(columns_owner_kernel, owners), in_specs=...]
    pallas_call x2 -> x3, Pallas kernels: 4.48 us -> 4.79 us  [attend(): pl.pallas_call(functools.partial(attend_kernel, shifts, state is None, lo...]
  transfers between devices with their start and end apart: 17 -> 17, of which waited for: 11 -> 10; matrix products, arithmetic and copies ran while one was open for 0% -> 0% of each run, Pallas kernels for 6% -> 10%
where the time goes in v4:
time: 46.6 us; the launch traced here: 46.4 us
  starting transfers between devices  26.9 us (58%)
  waiting for transfers between devices  8.76 us (19%)
  Pallas kernels  8.16 us (18%)
  local copies, waits for them, and re-layouts  1.07 us (2%)
  between operations  0.76 us (2%)
  other arithmetic  0.69 us (1%)
    ppermute x3, starting transfers between devices, on_device(): lax.ppermute(pieces[s], 'ctx', up(s))  9.73 us
    ppermute x3, starting transfers between devices, on_device(): lax.ppermute(message, 'ctx', up(s))  6.73 us
    pallas_call x3, Pallas kernels, attend(): pl.pallas_call(functools.partial(attend_kernel, shifts, state is None, lo...  4.79 us
    ppermute x3, starting transfers between devices, on_device(): lax.ppermute(pieces[s], 'adp', along(s))  4.5 us
    ppermute x3, starting transfers between devices, on_device(): lax.ppermute(b_out[s], 'adp', along(s))  4.5 us
    ppermute x3, waiting for transfers between devices, on_device(): lax.ppermute(message, 'ctx', up(s))  3.47 us
    ppermute x3, waiting for transfers between devices, on_device(): lax.ppermute(pieces[s], 'adp', along(s))  2.97 us
    pallas_call x1, Pallas kernels, pack(): pl.pallas_call(functools.partial(pack_kernel, heads_dev), in_specs=[HBM]...  1.58 us
  transfers between devices with their start and end apart: 17, of which 10 were waited for; matrix products, arithmetic and copies ran while one was open for 0% of the time, Pallas kernels for 10%

profile of v4, /device:TPU:0, one launch (start us, length us, event | category | flops | bytes accessed | tf_op | source)
XLA Modules:
  0.0 46.4 jit_solution(15713574952284660599)
XLA Ops:
  0.6 1.6 %pack.1.refs_2_.refs_3_.own_notes = bf16[272,256]{1,0:T(8,128)(2,1)} custom-call(s32[2]{0:T(128)} %tenant_hbm.1, bf16[256,512]{1,0:T(8,128)(2,1)} %keys.1, bf16[256,512]{1,0:T(8,128)(2,1)} %values.1, s32[1,256]{1,0:T(1,128)} %bitcast.5), custom_call_target="tpu_custom_call" | custom-call | bytes 262144 | tf_op jit(solution)/shard_map/pack/pallas_call | solution.py:65
  2.2 0.0 copy-start
  2.2 0.0 copy-start.1
  2.2 0.0 copy-start.2
  2.3 0.5 %collective-permute-start.2 = (bf16[272,256]{1,0:T(8,128)(2,1)}, bf16[272,256]{1,0:T(8,128)(2,1)S(1)}, u32[]{:S(2)}, u32[]{:S(2)}) collective-permute-start(bf16[272,256]{1,0:T(8,128)(2,1)} %pack.1.refs_2_.refs_3_.own_notes), channel_id=1, source_target_pairs={{0,4},{4,0},{8,12},{12,8},{16,20},{20,16},{24,28},{28,24},{1,5},{5... | collective-permute-start | bytes 417800 | tf_op jit(solution)/shard_map/ppermute | solution.py:380
  2.8 4.7 %collective-permute-start.3 = (bf16[272,256]{1,0:T(8,128)(2,1)}, bf16[272,256]{1,0:T(8,128)(2,1)S(1)}, u32[]{:S(2)}, u32[]{:S(2)}) collective-permute-start(bf16[272,256]{1,0:T(8,128)(2,1)} %pack.1.refs_2_.refs_3_.own_notes), channel_id=1, source_target_pairs={{0,24},{4,28},{8,0},{12,4},{16,8},{20,12},{24,16},{28,20},{1,25},{... | collective-permute-start | bytes 417800 | tf_op jit(solution)/shard_map/ppermute | solution.py:378
  7.4 0.0 collective-permute-done.2.refs_4_.after.other_notes
  7.4 1.0 %copy-done.4 = bf16[1,64,4096]{2,1,0:T(8,128)(2,1)S(1)} copy-done((bf16[1,64,4096]{2,1,0:T(8,128)(2,1)S(1)}, bf16[1,64,4096]{2,1,0:T(8,128)(2,1)}, u32[]{:S(2)}) %copy-start.4) | copy-done | bytes 524312
  8.5 0.1 columns.1
  8.6 1.5 %collective-permute-start.4 = (bf16[64,1024]{1,0:T(8,128)(2,1)S(1)}, bf16[64,1024]{1,0:T(8,128)(2,1)S(1)}, u32[]{:S(2)}, u32[]{:S(2)}) collective-permute-start(bf16[64,1024]{1,0:T(8,128)(2,1)S(1)} %get-tuple-element.42), channel_id=1, source_target_pairs={{0,1},{1,2},{2,3},{3,0},{4,5},{5,6},{6,7},{7,4},{8,9},{9,10},{10,1... | collective-permute-start | bytes 393224 | tf_op jit(solution)/shard_map/ppermute | solution.py:382
  10.2 0.5 %collective-permute-start.1 = (bf16[272,256]{1,0:T(8,128)(2,1)S(1)}, bf16[272,256]{1,0:T(8,128)(2,1)S(1)}, u32[]{:S(2)}, u32[]{:S(2)}) collective-permute-start(bf16[272,256]{1,0:T(8,128)(2,1)S(1)} %copy-done), channel_id=1, source_target_pairs={{0,16},{4,20},{8,24},{12,28},{16,0},{20,4},{24,8},{28,12},{1,17},{... | collective-permute-start | bytes 417800 | tf_op jit(solution)/shard_map/ppermute | solution.py:378
  10.7 1.6 %collective-permute-start = (bf16[272,256]{1,0:T(8,128)(2,1)S(1)}, bf16[272,256]{1,0:T(8,128)(2,1)S(1)}, u32[]{:S(2)}, u32[]{:S(2)}) collective-permute-start(bf16[272,256]{1,0:T(8,128)(2,1)S(1)} %copy-done), channel_id=1, source_target_pairs={{0,8},{4,12},{8,16},{12,20},{16,24},{20,28},{24,0},{28,4},{1,9},{5... | collective-permute-start | bytes 417800 | tf_op jit(solution)/shard_map/ppermute | solution.py:378
  12.2 1.5 %collective-permute-start.5 = (bf16[64,1024]{1,0:T(8,128)(2,1)S(1)}, bf16[64,1024]{1,0:T(8,128)(2,1)S(1)}, u32[]{:S(2)}, u32[]{:S(2)}) collective-permute-start(bf16[64,1024]{1,0:T(8,128)(2,1)S(1)} %get-tuple-element.44), channel_id=1, source_target_pairs={{0,2},{1,3},{2,0},{3,1},{4,6},{5,7},{6,4},{7,5},{8,10},{9,11},{10,... | collective-permute-start | bytes 393224 | tf_op jit(solution)/shard_map/ppermute | solution.py:382
  13.8 0.0 collective-permute-done.3.refs_3_
  13.8 1.4 %collective-permute-start.6 = (bf16[64,1024]{1,0:T(8,128)(2,1)S(1)}, bf16[64,1024]{1,0:T(8,128)(2,1)S(1)}, u32[]{:S(2)}, u32[]{:S(2)}) collective-permute-start(bf16[64,1024]{1,0:T(8,128)(2,1)S(1)} %get-tuple-element.45), channel_id=1, source_target_pairs={{0,3},{1,0},{2,1},{3,2},{4,7},{5,4},{6,5},{7,6},{8,11},{9,8},{10,9... | collective-permute-start | bytes 393224 | tf_op jit(solution)/shard_map/ppermute | solution.py:382
  15.2 0.1 collective-permute-done.4.refs_12_
  15.3 0.0 collective-permute-start.9
  15.3 2.7 %attend_0.1 = (f32[2048,128]{1,0:T(8,128)S(1)}, f32[2048,256]{1,0:T(8,128)S(1)}, f32[2048,256]{1,0:T(8,128)S(1)}) custom-call(bf16[256,1024]{1,0:T(8,128)(2,1)S(1)} %copy-done.1, bf16[256,1024]{1,0:T(8,128)(2,1)S(1)} %copy-done.2, bf16[272,256]{1,0:T(8,128)(2,1)S(1)} %copy-done, bf16[272,256]{1,0:T(8,128)(2,1)S(1)} %copy-done, ...), custom_call_target="tpu_custom_call" | custom-call | flops 805306368 | bytes 4194304 | tf_op jit(solution)/shard_map/attend_0/pallas_call | solution.py:263
  17.9 3.5 %collective-permute-done.1.refs_4_ = bf16[272,256]{1,0:T(8,128)(2,1)S(1)} collective-permute-done((bf16[272,256]{1,0:T(8,128)(2,1)S(1)}, bf16[272,256]{1,0:T(8,128)(2,1)S(1)}, u32[]{:S(2)}, u32[]{:S(2)}) %collective-permute-start.1) | collective-permute-done | bytes 139296 | tf_op jit(solution)/shard_map/ppermute | solution.py:378
  21.4 0.0 collective-permute-done.refs_3_
  21.4 0.0 collective-permute-done.5.refs_13_
  21.4 0.0 collective-permute-done.6.refs_14_
  21.4 0.0 copy-start.3
  21.4 0.1 collective-permute-start.7
  21.5 0.5 %collective-permute-start.8 = (bf16[272,256]{1,0:T(8,128)(2,1)S(1)}, bf16[272,256]{1,0:T(8,128)(2,1)S(1)}, u32[]{:S(2)}, u32[]{:S(2)}) collective-permute-start(bf16[272,256]{1,0:T(8,128)(2,1)S(1)} %collective-permute-done.1.refs_4_), channel_id=1, source_target_pairs={{0,4},{4,0},{8,12},{12,8},{16,20},{20,16},{24,28},{28,24},{1,5},{5... | collective-permute-start | bytes 417800 | tf_op jit(solution)/shard_map/ppermute | solution.py:387
  22.0 0.0 collective-permute-done.9.refs_4_
  22.0 0.5 %attend_3.1 = (f32[2048,128]{1,0:T(8,128)S(1)}, f32[2048,256]{1,0:T(8,128)S(1)}, f32[2048,256]{1,0:T(8,128)S(1)}) custom-call(bf16[256,1024]{1,0:T(8,128)(2,1)S(1)} %copy-done.1, bf16[256,1024]{1,0:T(8,128)(2,1)S(1)} %copy-done.2, bf16[272,256]{1,0:T(8,128)(2,1)S(1)} %copy-done, bf16[272,256]{1,0:T(8,128)(2,1)S(1)} %collective-permute-done.3.refs_3_, ...), custom_call_target="tpu_custom_call" | custom-call | flops 805306368 | bytes 4194304 | tf_op jit(solution)/shard_map/attend_3/pallas_call | solution.py:263
  22.5 0.4 collective-permute-done.7.refs_5_
  22.9 0.2 collective-permute-done.8.refs_6_
  23.1 1.7 %attend_1_2.1 = (bf16[256,1024]{1,0:T(8,128)(2,1)S(1)}, f32[256,64]{1,0:T(8,128)S(1)}, f32[128,512]{1,0:T(8,128)S(1)}, bf16[128,512]{1,0:T(8,128)(2,1)S(1)}) custom-call(bf16[256,1024]{1,0:T(8,128)(2,1)S(1)} %copy-done.1, bf16[256,1024]{1,0:T(8,128)(2,1)S(1)} %copy-done.2, bf16[272,256]{1,0:T(8,128)(2,1)S(1)} %copy-done, ...), custom_call_target="tpu_custom_call" | custom-call | flops 1610612736 | bytes 4194304 | tf_op jit(solution)/shard_map/attend_1_2/pallas_call | solution.py:263
  24.7 0.4 collective-permute-start.10
  25.1 1.0 %collective-permute-done.10.other_ref = bf16[128,512]{1,0:T(8,128)(2,1)S(1)} collective-permute-done((bf16[128,512]{1,0:T(8,128)(2,1)S(1)}, bf16[128,512]{1,0:T(8,128)(2,1)S(1)}, u32[]{:S(2)}, u32[]{:S(2)}) %collective-permute-start.10) | collective-permute-done | bytes 131104 | tf_op jit(solution)/shard_map/ppermute | solution.py:400
  26.1 0.2 by_tenant.1
  26.3 1.6 %collective-permute-start.11 = (bf16[80,512]{1,0:T(8,128)(2,1)S(1)}, bf16[80,512]{1,0:T(8,128)(2,1)S(1)}, u32[]{:S(2)}, u32[]{:S(2)}) collective-permute-start(bf16[80,512]{1,0:T(8,128)(2,1)S(1)} %get-tuple-element.64), channel_id=1, source_target_pairs={{0,1},{1,2},{2,3},{3,0},{4,5},{5,6},{6,7},{7,4},{8,9},{9,10},{10,1... | collective-permute-start | bytes 245768 | tf_op jit(solution)/shard_map/ppermute | solution.py:403
  27.9 1.2 %collective-permute-start.12 = (bf16[80,512]{1,0:T(8,128)(2,1)S(1)}, bf16[80,512]{1,0:T(8,128)(2,1)S(1)}, u32[]{:S(2)}, u32[]{:S(2)}) collective-permute-start(bf16[80,512]{1,0:T(8,128)(2,1)S(1)} %get-tuple-element.65), channel_id=1, source_target_pairs={{0,2},{1,3},{2,0},{3,1},{4,6},{5,7},{6,4},{7,5},{8,10},{9,11},{10,... | collective-permute-start | bytes 245768 | tf_op jit(solution)/shard_map/ppermute | solution.py:403
  29.0 1.8 %collective-permute-start.13 = (bf16[80,512]{1,0:T(8,128)(2,1)S(1)}, bf16[80,512]{1,0:T(8,128)(2,1)S(1)}, u32[]{:S(2)}, u32[]{:S(2)}) collective-permute-start(bf16[80,512]{1,0:T(8,128)(2,1)S(1)} %get-tuple-element.66), channel_id=1, source_target_pairs={{0,3},{1,0},{2,1},{3,2},{4,7},{5,4},{6,5},{7,6},{8,11},{9,8},{10,9... | collective-permute-start | bytes 245768 | tf_op jit(solution)/shard_map/ppermute | solution.py:403
  30.8 1.4 %collective-permute-done.11.refs_2_.refs_1_ = bf16[80,512]{1,0:T(8,128)(2,1)S(1)} collective-permute-done((bf16[80,512]{1,0:T(8,128)(2,1)S(1)}, bf16[80,512]{1,0:T(8,128)(2,1)S(1)}, u32[]{:S(2)}, u32[]{:S(2)}) %collective-permute-start.11) | collective-permute-done | bytes 81952 | tf_op jit(solution)/shard_map/ppermute | solution.py:403
  32.2 1.5 %collective-permute-done.12.refs_3_.refs_2_ = bf16[80,512]{1,0:T(8,128)(2,1)S(1)} collective-permute-done((bf16[80,512]{1,0:T(8,128)(2,1)S(1)}, bf16[80,512]{1,0:T(8,128)(2,1)S(1)}, u32[]{:S(2)}, u32[]{:S(2)}) %collective-permute-start.12) | collective-permute-done | bytes 81952 | tf_op jit(solution)/shard_map/ppermute | solution.py:403
  33.7 0.1 collective-permute-done.13.refs_4_.refs_3_
  33.8 0.1 by_columns_owner.1
  33.9 2.4 %collective-permute-start.14 = (bf16[64,512]{1,0:T(8,128)(2,1)S(1)}, bf16[64,512]{1,0:T(8,128)(2,1)S(1)}, u32[]{:S(2)}, u32[]{:S(2)}) collective-permute-start(bf16[64,512]{1,0:T(8,128)(2,1)S(1)} %get-tuple-element.70), channel_id=1, source_target_pairs={{0,8},{4,12},{8,16},{12,20},{16,24},{20,28},{24,0},{28,4},{1,9},{5... | collective-permute-start | bytes 196616 | tf_op jit(solution)/shard_map/ppermute | solution.py:407
  36.3 4.9 %collective-permute-start.15 = (bf16[64,512]{1,0:T(8,128)(2,1)S(1)}, bf16[64,512]{1,0:T(8,128)(2,1)S(1)}, u32[]{:S(2)}, u32[]{:S(2)}) collective-permute-start(bf16[64,512]{1,0:T(8,128)(2,1)S(1)} %get-tuple-element.71), channel_id=1, source_target_pairs={{0,16},{4,20},{8,24},{12,28},{16,0},{20,4},{24,8},{28,12},{1,17},{... | collective-permute-start | bytes 196616 | tf_op jit(solution)/shard_map/ppermute | solution.py:407
  41.2 2.4 %collective-permute-start.16 = (bf16[64,512]{1,0:T(8,128)(2,1)S(1)}, bf16[64,512]{1,0:T(8,128)(2,1)S(1)}, u32[]{:S(2)}, u32[]{:S(2)}) collective-permute-start(bf16[64,512]{1,0:T(8,128)(2,1)S(1)} %get-tuple-element.72), channel_id=1, source_target_pairs={{0,24},{4,28},{8,0},{12,4},{16,8},{20,12},{24,16},{28,20},{1,25},{... | collective-permute-start | bytes 196616 | tf_op jit(solution)/shard_map/ppermute | solution.py:407
  43.6 1.4 %finish.1 = (bf16[256,1024]{1,0:T(8,128)(2,1)}, f32[64,64]{1,0:T(8,128)}) custom-call(bf16[256,1024]{1,0:T(8,128)(2,1)S(1)} %get-tuple-element.59.refs_0_, bf16[80,512]{1,0:T(8,128)(2,1)S(1)} %get-tuple-element.63.refs_1_.refs_0_, bf16[80,512]{1,0:T(8,128)(2,1)S(1)} %collective-permute-done.11.refs_2_.refs_1_, ...), custom_call_target="tpu_custom_call" | custom-call | bytes 1048576 | tf_op jit(solution)/shard_map/finish/pallas_call | solution.py:354
  45.0 0.0 collective-permute-done.14
  45.0 0.1 collective-permute-done.15
  45.1 0.5 %collective-permute-done.16 = bf16[64,512]{1,0:T(8,128)(2,1)S(1)} collective-permute-done((bf16[64,512]{1,0:T(8,128)(2,1)S(1)}, bf16[64,512]{1,0:T(8,128)(2,1)S(1)}, u32[]{:S(2)}, u32[]{:S(2)}) %collective-permute-start.16) | collective-permute-done | bytes 65568 | tf_op jit(solution)/shard_map/ppermute | solution.py:407
  45.7 0.7 %add_bitcast_fusion = f32[1,64,512]{2,1,0:T(8,128)} fusion(bf16[64,512]{1,0:T(8,128)(2,1)S(1)} %collective-permute-done.16, bf16[64,512]{1,0:T(8,128)(2,1)S(1)} %collective-permute-done.15, bf16[64,512]{1,0:T(8,128)(2,1)S(1)} %collective-permute-done.14, bf16[64,512]{1,0:T(8,128)(2,1)S(1)} %get-tuple-element.69), kind=kLoop, calls=%fused_computation | loop fusion | flops 229376 | bytes 393216 | tf_op jit(solution)/shard_map/broadcast_in_dim | solution.py:408
  (5 shorter events, 0.0 us)
Async XLA Ops:
  2.2 8.0 %copy-start = (bf16[272,256]{1,0:T(8,128)(2,1)S(1)}, bf16[272,256]{1,0:T(8,128)(2,1)}, u32[]{:S(2)}) copy-start(bf16[272,256]{1,0:T(8,128)(2,1)} %pack.1.refs_2_.refs_3_.own_notes) | copy-start | bytes 417796
  2.2 13.0 %copy-start.1 = (bf16[256,1024]{1,0:T(8,128)(2,1)S(1)}, bf16[256,1024]{1,0:T(8,128)(2,1)}, u32[]{:S(2)}) copy-start(bf16[256,1024]{1,0:T(8,128)(2,1)} %refs_0_.5) | copy-start | bytes 1572868
  2.2 13.0 %copy-start.2 = (bf16[256,1024]{1,0:T(8,128)(2,1)S(1)}, bf16[256,1024]{1,0:T(8,128)(2,1)}, u32[]{:S(2)}) copy-start(bf16[256,1024]{1,0:T(8,128)(2,1)} %refs_1_.5) | copy-start | bytes 1572868
  2.3 5.2 %collective-permute-start.2 = (bf16[272,256]{1,0:T(8,128)(2,1)}, bf16[272,256]{1,0:T(8,128)(2,1)S(1)}, u32[]{:S(2)}, u32[]{:S(2)}) collective-permute-start(bf16[272,256]{1,0:T(8,128)(2,1)} %pack.1.refs_2_.refs_3_.own_notes), channel_id=1, source_target_pairs={{0,4},{4,0},{8,12},{12,8},{16,20},{20,16},{24,28},{28,24},{1,5},{5... | collective-permute-start | bytes 417800 | tf_op jit(solution)/shard_map/ppermute | solution.py:380
  2.8 11.0 %collective-permute-start.3 = (bf16[272,256]{1,0:T(8,128)(2,1)}, bf16[272,256]{1,0:T(8,128)(2,1)S(1)}, u32[]{:S(2)}, u32[]{:S(2)}) collective-permute-start(bf16[272,256]{1,0:T(8,128)(2,1)} %pack.1.refs_2_.refs_3_.own_notes), channel_id=1, source_target_pairs={{0,24},{4,28},{8,0},{12,4},{16,8},{20,12},{24,16},{28,20},{1,25},{... | collective-permute-start | bytes 417800 | tf_op jit(solution)/shard_map/ppermute | solution.py:378
  7.4 1.0 %copy-start.4 = (bf16[1,64,4096]{2,1,0:T(8,128)(2,1)S(1)}, bf16[1,64,4096]{2,1,0:T(8,128)(2,1)}, u32[]{:S(2)}) copy-start(bf16[1,64,4096]{2,1,0:T(8,128)(2,1)} %adapter_b.1) | copy-start | bytes 1572868
  8.6 6.6 %collective-permute-start.4 = (bf16[64,1024]{1,0:T(8,128)(2,1)S(1)}, bf16[64,1024]{1,0:T(8,128)(2,1)S(1)}, u32[]{:S(2)}, u32[]{:S(2)}) collective-permute-start(bf16[64,1024]{1,0:T(8,128)(2,1)S(1)} %get-tuple-element.42), channel_id=1, source_target_pairs={{0,1},{1,2},{2,3},{3,0},{4,5},{5,6},{6,7},{7,4},{8,9},{9,10},{10,1... | collective-permute-start | bytes 393224 | tf_op jit(solution)/shard_map/ppermute | solution.py:382
  10.2 11.2 %collective-permute-start.1 = (bf16[272,256]{1,0:T(8,128)(2,1)S(1)}, bf16[272,256]{1,0:T(8,128)(2,1)S(1)}, u32[]{:S(2)}, u32[]{:S(2)}) collective-permute-start(bf16[272,256]{1,0:T(8,128)(2,1)S(1)} %copy-done), channel_id=1, source_target_pairs={{0,16},{4,20},{8,24},{12,28},{16,0},{20,4},{24,8},{28,12},{1,17},{... | collective-permute-start | bytes 417800 | tf_op jit(solution)/shard_map/ppermute | solution.py:378
  10.7 10.7 %collective-permute-start = (bf16[272,256]{1,0:T(8,128)(2,1)S(1)}, bf16[272,256]{1,0:T(8,128)(2,1)S(1)}, u32[]{:S(2)}, u32[]{:S(2)}) collective-permute-start(bf16[272,256]{1,0:T(8,128)(2,1)S(1)} %copy-done), channel_id=1, source_target_pairs={{0,8},{4,12},{8,16},{12,20},{16,24},{20,28},{24,0},{28,4},{1,9},{5... | collective-permute-start | bytes 417800 | tf_op jit(solution)/shard_map/ppermute | solution.py:378
  12.2 9.2 %collective-permute-start.5 = (bf16[64,1024]{1,0:T(8,128)(2,1)S(1)}, bf16[64,1024]{1,0:T(8,128)(2,1)S(1)}, u32[]{:S(2)}, u32[]{:S(2)}) collective-permute-start(bf16[64,1024]{1,0:T(8,128)(2,1)S(1)} %get-tuple-element.44), channel_id=1, source_target_pairs={{0,2},{1,3},{2,0},{3,1},{4,6},{5,7},{6,4},{7,5},{8,10},{9,11},{10,... | collective-permute-start | bytes 393224 | tf_op jit(solution)/shard_map/ppermute | solution.py:382
  13.8 7.6 %collective-permute-start.6 = (bf16[64,1024]{1,0:T(8,128)(2,1)S(1)}, bf16[64,1024]{1,0:T(8,128)(2,1)S(1)}, u32[]{:S(2)}, u32[]{:S(2)}) collective-permute-start(bf16[64,1024]{1,0:T(8,128)(2,1)S(1)} %get-tuple-element.45), channel_id=1, source_target_pairs={{0,3},{1,0},{2,1},{3,2},{4,7},{5,4},{6,5},{7,6},{8,11},{9,8},{10,9... | collective-permute-start | bytes 393224 | tf_op jit(solution)/shard_map/ppermute | solution.py:382
  15.3 6.8 %collective-permute-start.9 = (bf16[272,256]{1,0:T(8,128)(2,1)S(1)}, bf16[272,256]{1,0:T(8,128)(2,1)S(1)}, u32[]{:S(2)}, u32[]{:S(2)}) collective-permute-start(bf16[272,256]{1,0:T(8,128)(2,1)S(1)} %collective-permute-done.3.refs_3_), channel_id=1, source_target_pairs={{0,4},{4,0},{8,12},{12,8},{16,20},{20,16},{24,28},{28,24},{1,5},{5... | collective-permute-start | bytes 417800 | tf_op jit(solution)/shard_map/ppermute | solution.py:385
  21.4 1.6 %copy-start.3 = (bf16[256,64]{0,1:T(8,128)(2,1)S(1)}, bf16[256,64]{0,1:T(8,128)(2,1)}, u32[]{:S(2)}) copy-start(bf16[256,64]{0,1:T(8,128)(2,1)} %param.14) | copy-start | bytes 98308
  21.4 1.4 %collective-permute-start.7 = (bf16[272,256]{1,0:T(8,128)(2,1)S(1)}, bf16[272,256]{1,0:T(8,128)(2,1)S(1)}, u32[]{:S(2)}, u32[]{:S(2)}) collective-permute-start(bf16[272,256]{1,0:T(8,128)(2,1)S(1)} %collective-permute-done.refs_3_), channel_id=1, source_target_pairs={{0,4},{4,0},{8,12},{12,8},{16,20},{20,16},{24,28},{28,24},{1,5},{5... | collective-permute-start | bytes 417800 | tf_op jit(solution)/shard_map/ppermute | solution.py:387
  21.5 1.5 %collective-permute-start.8 = (bf16[272,256]{1,0:T(8,128)(2,1)S(1)}, bf16[272,256]{1,0:T(8,128)(2,1)S(1)}, u32[]{:S(2)}, u32[]{:S(2)}) collective-permute-start(bf16[272,256]{1,0:T(8,128)(2,1)S(1)} %collective-permute-done.1.refs_4_), channel_id=1, source_target_pairs={{0,4},{4,0},{8,12},{12,8},{16,20},{20,16},{24,28},{28,24},{1,5},{5... | collective-permute-start | bytes 417800 | tf_op jit(solution)/shard_map/ppermute | solution.py:387
  24.7 1.4 %collective-permute-start.10 = (bf16[128,512]{1,0:T(8,128)(2,1)S(1)}, bf16[128,512]{1,0:T(8,128)(2,1)S(1)}, u32[]{:S(2)}, u32[]{:S(2)}) collective-permute-start(bf16[128,512]{1,0:T(8,128)(2,1)S(1)} %get-tuple-element.61), channel_id=1, source_target_pairs={{0,4},{4,0},{8,12},{12,8},{16,20},{20,16},{24,28},{28,24},{1,5},{5... | collective-permute-start | bytes 393224 | tf_op jit(solution)/shard_map/ppermute | solution.py:400
  26.3 5.9 %collective-permute-start.11 = (bf16[80,512]{1,0:T(8,128)(2,1)S(1)}, bf16[80,512]{1,0:T(8,128)(2,1)S(1)}, u32[]{:S(2)}, u32[]{:S(2)}) collective-permute-start(bf16[80,512]{1,0:T(8,128)(2,1)S(1)} %get-tuple-element.64), channel_id=1, source_target_pairs={{0,1},{1,2},{2,3},{3,0},{4,5},{5,6},{6,7},{7,4},{8,9},{9,10},{10,1... | collective-permute-start | bytes 245768 | tf_op jit(solution)/shard_map/ppermute | solution.py:403
  27.9 5.8 %collective-permute-start.12 = (bf16[80,512]{1,0:T(8,128)(2,1)S(1)}, bf16[80,512]{1,0:T(8,128)(2,1)S(1)}, u32[]{:S(2)}, u32[]{:S(2)}) collective-permute-start(bf16[80,512]{1,0:T(8,128)(2,1)S(1)} %get-tuple-element.65), channel_id=1, source_target_pairs={{0,2},{1,3},{2,0},{3,1},{4,6},{5,7},{6,4},{7,5},{8,10},{9,11},{10,... | collective-permute-start | bytes 245768 | tf_op jit(solution)/shard_map/ppermute | solution.py:403
  29.0 4.8 %collective-permute-start.13 = (bf16[80,512]{1,0:T(8,128)(2,1)S(1)}, bf16[80,512]{1,0:T(8,128)(2,1)S(1)}, u32[]{:S(2)}, u32[]{:S(2)}) collective-permute-start(bf16[80,512]{1,0:T(8,128)(2,1)S(1)} %get-tuple-element.66), channel_id=1, source_target_pairs={{0,3},{1,0},{2,1},{3,2},{4,7},{5,4},{6,5},{7,6},{8,11},{9,8},{10,9... | collective-permute-start | bytes 245768 | tf_op jit(solution)/shard_map/ppermute | solution.py:403
  33.9 11.2 %collective-permute-start.14 = (bf16[64,512]{1,0:T(8,128)(2,1)S(1)}, bf16[64,512]{1,0:T(8,128)(2,1)S(1)}, u32[]{:S(2)}, u32[]{:S(2)}) collective-permute-start(bf16[64,512]{1,0:T(8,128)(2,1)S(1)} %get-tuple-element.70), channel_id=1, source_target_pairs={{0,8},{4,12},{8,16},{12,20},{16,24},{20,28},{24,0},{28,4},{1,9},{5... | collective-permute-start | bytes 196616 | tf_op jit(solution)/shard_map/ppermute | solution.py:407
  36.3 8.8 %collective-permute-start.15 = (bf16[64,512]{1,0:T(8,128)(2,1)S(1)}, bf16[64,512]{1,0:T(8,128)(2,1)S(1)}, u32[]{:S(2)}, u32[]{:S(2)}) collective-permute-start(bf16[64,512]{1,0:T(8,128)(2,1)S(1)} %get-tuple-element.71), channel_id=1, source_target_pairs={{0,16},{4,20},{8,24},{12,28},{16,0},{20,4},{24,8},{28,12},{1,17},{... | collective-permute-start | bytes 196616 | tf_op jit(solution)/shard_map/ppermute | solution.py:407
  41.2 4.4 %collective-permute-start.16 = (bf16[64,512]{1,0:T(8,128)(2,1)S(1)}, bf16[64,512]{1,0:T(8,128)(2,1)S(1)}, u32[]{:S(2)}, u32[]{:S(2)}) collective-permute-start(bf16[64,512]{1,0:T(8,128)(2,1)S(1)} %get-tuple-element.72), channel_id=1, source_target_pairs={{0,24},{4,28},{8,0},{12,4},{16,8},{20,12},{24,16},{28,20},{1,25},{... | collective-permute-start | bytes 196616 | tf_op jit(solution)/shard_map/ppermute | solution.py:407

commit v5 on v4

v5 whole, which is shorter than its diff:
```python
import functools

import jax
import jax.numpy as jnp
from jax import lax
from jax.experimental import pallas as pl
from jax.experimental.pallas import tpu as pltpu
from jax.sharding import PartitionSpec as P

QH = 32
KVH = 4
HD = 128
RANK = 64
BLOCK = 128
CORES = 2
PAD = 16
PACK_LIMIT = (64 << 20) - (1 << 18)

adapter_scale_factor = 2.0
far_below = -1e30
logit_scale = HD ** (-0.5)
log2_scale = logit_scale * 1.4426950408889634

VMEM = pl.BlockSpec(memory_space=pltpu.VMEM)
SMEM = pl.BlockSpec(memory_space=pltpu.SMEM)
ANY = pl.BlockSpec(memory_space=pl.ANY)
HBM = pl.BlockSpec(memory_space=pltpu.HBM)
BF16 = jnp.bfloat16
F32 = jnp.float32


def small(bytes_accessed):
    return dict(
        compiler_params=pltpu.CompilerParams(vmem_limit_bytes=8 << 20),
        cost_estimate=pl.CostEstimate(flops=0, bytes_accessed=bytes_accessed, transcendentals=0),
    )


def pack_kernel(heads_dev, tenant_hbm, keys, values, docs_hbm, message, tenant, docs, sems):
    tokens = keys.shape[0]
    kv = lax.axis_index("adp") * heads_dev // (QH // KVH)
    head = pl.ds(pl.multiple_of(kv * HD, HD), HD)
    copies = [
        pltpu.make_async_copy(docs_hbm, docs, sems.at[0]),
        pltpu.make_async_copy(tenant_hbm, tenant, sems.at[1]),
        pltpu.make_async_copy(keys.at[:, head], message.at[pl.ds(0, tokens), pl.ds(0, HD)], sems.at[2]),
        pltpu.make_async_copy(values.at[:, head], message.at[pl.ds(0, tokens), pl.ds(HD, HD)], sems.at[3]),
    ]
    for copy in copies:
        copy.start()
    for copy in copies[:2]:
        copy.wait()
    row = lax.broadcasted_iota(jnp.int32, (PAD, tokens), 0)
    told = jnp.broadcast_to(docs[...].astype(F32), (PAD, tokens))
    for block in range(tokens // BLOCK):
        told = jnp.where(row == 1 + block, tenant[block].astype(F32), told)
    message[tokens:, :] = told.astype(BF16)
    for copy in copies[2:]:
        copy.wait()


def pack(block_tenant, keys, values, docs, heads_dev):
    tokens = keys.shape[0]
    return pl.pallas_call(
        functools.partial(pack_kernel, heads_dev),
        in_specs=[HBM] * 4,
        out_specs=VMEM,
        out_shape=jax.ShapeDtypeStruct((tokens + PAD, 2 * HD), BF16),
        scratch_shapes=[
            pltpu.SMEM(block_tenant.shape, jnp.int32),
            pltpu.VMEM((1, tokens), jnp.int32),
            pltpu.SemaphoreType.DMA((4,)),
        ],
        name="pack",
        compiler_params=pltpu.CompilerParams(vmem_limit_bytes=PACK_LIMIT),
        cost_estimate=pl.CostEstimate(flops=0, bytes_accessed=1 << 18, transcendentals=0),
    )(block_tenant, keys, values, docs.reshape(1, tokens))


def columns_kernel(owners, adapter_b, after, *refs):
    outs, sems = refs[:-1], refs[-1]
    width = outs[0].shape[1]
    adp = lax.axis_index("adp")
    core = lax.rem(lax.axis_index("ctx"), CORES)
    copies = []
    for s, out in enumerate(outs):
        owner = lax.rem(adp + jnp.where(core == 0, s, owners - s), owners)
        start = pl.multiple_of(owner * width, 128)
        copies.append(pltpu.make_async_copy(adapter_b.at[0, :, pl.ds(start, width)], out, sems.at[s]))
        copies[-1].start()
    for copy in copies:
        copy.wait()


def columns(adapter_b, after, owners):
    width = adapter_b.shape[2] // owners
    count = owners // 2 + 1
    return pl.pallas_call(
        functools.partial(columns_kernel, owners),
        in_specs=[ANY, ANY],
        out_specs=[VMEM] * count,
        out_shape=[jax.ShapeDtypeStruct((RANK, width), BF16)] * count,
        scratch_shapes=[pltpu.SemaphoreType.DMA((count,))],
        name="columns",
        compiler_params=pltpu.CompilerParams(vmem_limit_bytes=8 << 20),
        cost_estimate=pl.CostEstimate(flops=1 << 33, bytes_accessed=1 << 19, transcendentals=0),
    )(adapter_b, after)


def lanes(x, times):
    return jnp.concatenate([x] * times, axis=1)


def rows(parts):
    return jnp.concatenate(parts, axis=0)


def attend_kernel(shifts, parts, first, last, owners, *refs):
    refs = list(refs)
    take = lambda count: [refs.pop(0) for _ in range(count)]
    q_ref, g_ref, docs_ref = take(3)
    own, other = take(len(shifts)), take(len(shifts))
    if not first:
        given = take(3)
    if last:
        (low_ref,) = take(1)
        b_refs = take(owners)
        dq_refs = take(parts[0])
        dq_ref, partial_ref = take(2)
        rank_refs = take(parts[0])
    sums = take(3)
    (bias,) = take(1)
    tokens, width = q_ref.shape
    half = width // CORES
    group = half // HD
    part_rows = group * tokens
    ctx = lax.axis_index("ctx")
    z, core = ctx // CORES, lax.rem(ctx, CORES)
    offset = lambda part: pl.multiple_of((core if part else 1 - core) * half, HD)
    doc_row = lambda ref: ref[tokens : tokens + PAD, :][:1].astype(F32)

    docs = doc_row(docs_ref)
    first_doc = jnp.min(docs)
    row = lax.broadcasted_iota(jnp.int32, (tokens, tokens), 0)
    lane = lax.broadcasted_iota(jnp.int32, (tokens, tokens), 1)
    doc_column = jnp.sum(jnp.where(row == lane, docs, 0.0), axis=1, keepdims=True)

    def stacked(ref, part):
        return rows([ref[:, pl.ds(offset(part) + i * HD, HD)] for i in range(group)])

    def place(ref, part):
        start = 0 if ref.shape[0] == part_rows else part * part_rows
        return slice(start, start + part_rows)

    def step(indices, old):
        messages = [ref for i in indices for ref in (own[i], other[i])]
        keys = rows([ref[:tokens, :HD] for ref in messages])
        values = rows([ref[:tokens, HD:] for ref in messages])
        count = len(messages) * tokens
        extended = jnp.concatenate([keys, jnp.ones((count, HD), BF16)], axis=1)
        for i, ref in enumerate(messages):
            key_docs = doc_row(ref)
            if old is None and i == 1:
                key_docs = jnp.where(core == 1, key_docs, -1.0)
            seen = key_docs == doc_column
            if old is None and i == 0:
                seen = seen & (lane <= row)
            bias[:, i * tokens : (i + 1) * tokens] = jnp.where(seen, 0.0, far_below)
        for part in parts:
            scores = lax.dot_general(
                stacked(q_ref, part), keys, (((1,), (1,)), ((), ())), preferred_element_type=F32
            ) + rows([bias[:, :count]] * group)
            new_top = jnp.broadcast_to(jnp.max(scores, axis=1, keepdims=True), (part_rows, 128))
            if old is not None:
                old_top = old[0][place(old[0], part), :]
                new_top = jnp.maximum(old_top, new_top)
            p = jnp.exp2((scores - lanes(new_top, count // 128)) * log2_scale)
            grads = lax.dot_general(
                stacked(g_ref, part), values, (((1,), (1,)), ((), ())), preferred_element_type=F32
            )
            by_key = jnp.dot(p.astype(BF16), extended, preferred_element_type=F32)
            by_grad = jnp.dot((p * grads).astype(BF16), extended, preferred_element_type=F32)
            if old is not None:
                decay = lanes(jnp.exp2((old_top - new_top) * log2_scale), 2)
                by_key = by_key + old[1][place(old[1], part), :] * decay
                by_grad = by_grad + old[2][place(old[2], part), :] * decay
            for ref, value in zip(sums, (new_top, by_key, by_grad)):
                ref[place(ref, part), :] = value

    if first:
        step([0], None)
    else:
        needed = []
        for index, shift in enumerate(shifts):
            latest = jnp.max(jnp.maximum(doc_row(own[index]), doc_row(other[index])))
            needed.append((z >= shift) & (latest == first_doc))
        for index in range(len(shifts)):
            old = sums if index else given
            pl.when(needed[index])(functools.partial(step, [index], old))
            if index == 0:

                @pl.when(jnp.logical_not(needed[0]))
                def _():
                    for part in parts:
                        for kept, ref in zip(sums, given):
                            kept[place(kept, part), :] = ref[place(ref, part), :]

    if not last:
        return
    _, by_key, by_grad = sums
    (part,) = parts
    for h in range(group):
        head_rows = slice(h * tokens, (h + 1) * tokens)
        inverse = 1.0 / by_key[head_rows, HD:]
        delta = by_grad[head_rows, HD:] * inverse
        dq = (by_grad[head_rows, :HD] - delta * by_key[head_rows, :HD]) * (inverse * logit_scale)
        dq_ref[:, h * HD : (h + 1) * HD] = dq.astype(BF16)

    adp = lax.axis_index("adp")
    told = docs_ref[tokens:, :HD].astype(F32)
    for block in range(tokens // BLOCK):
        block_rows = slice(block * BLOCK, (block + 1) * BLOCK)
        partial = adapter_scale_factor * jnp.dot(
            low_ref[:, block_rows], dq_ref[block_rows, :], preferred_element_type=F32
        )
        partial_ref[block * RANK : (block + 1) * RANK, :] = partial.astype(partial_ref.dtype)

        if part == 0:
            continue
        tenant = jnp.max(told[1 + block : 2 + block]).astype(jnp.int32)
        back = lax.rem(adp - tenant + owners, owners)
        holder = jnp.where(core == 0, back, lax.rem(owners - back, owners))
        for s in range(owners):

            @pl.when(holder == s)
            def _(s=s, block_rows=block_rows):
                rank_refs[0][block_rows, :] = adapter_scale_factor * sum(
                    lax.dot_general(
                        dq[block_rows, :],
                        b_refs[s][:, pl.ds(offset(each), half)],
                        (((1,), (1,)), ((), ())),
                        preferred_element_type=F32,
                    )
                    for each, dq in enumerate([*dq_refs, dq_ref])
                )


def attend(shifts, queries, grad_out, message, own, other, state=(), final=None):
    tokens, width = queries.shape
    half = width // CORES
    blocks = tokens // BLOCK
    parts = (0, 1) if final is None else (final[0],)
    stack = len(parts) * half // HD * tokens
    sums = [((stack, 128), F32), ((stack, 2 * HD), F32), ((stack, 2 * HD), F32)]
    inputs = [queries, grad_out, message, *own, *other, *state]
    scratch = [pltpu.VMEM((tokens, 2 * tokens), F32)]
    owners = 0
    if final is None:
        outs = sums
    else:
        part, low_rank, *rest = final
        b_cols = rest[1] if part else ()
        owners = len(b_cols)
        inputs += [low_rank.T, *b_cols, *rest[:1]]
        scratch = [pltpu.VMEM(*each) for each in sums] + scratch
        outs = [
            ((tokens, half), BF16),
            ((blocks * RANK, half), F32 if part else BF16),
        ]
        outs += [((tokens, RANK), F32)] * part
    return pl.pallas_call(
        functools.partial(attend_kernel, shifts, parts, not state, final is not None, owners),
        in_specs=[VMEM] * len(inputs),
        out_specs=[VMEM] * len(outs),
        out_shape=[jax.ShapeDtypeStruct(*each) for each in outs],
        scratch_shapes=scratch,
        compiler_params=pltpu.CompilerParams(vmem_limit_bytes=30 << 20),
        cost_estimate=pl.CostEstimate(
            flops=len(shifts) * 6 * len(parts) * tokens * tokens * width,
            bytes_accessed=4 << 20,
            transcendentals=0,
        ),
        name="attend_" + "_".join(map(str, shifts[:4])) + ("" if final is None else f"_part{part}"),
    )(*inputs)


def tenants_kernel(owners, mine_ref, other_ref, own_notes, other_notes, rank_ref, *outs):
    blocks = mine_ref.shape[0] // RANK
    width = mine_ref.shape[1]
    share = rank_ref.shape[0] // owners
    adp = lax.axis_index("adp")
    told = [ref[ref.shape[0] - PAD :, :HD].astype(F32) for ref in (own_notes, other_notes)]
    for s in range(owners):
        owner = lax.rem(adp + s, owners)
        total = jnp.zeros((RANK, width), F32)
        for block in range(blocks):
            part = slice(block * RANK, (block + 1) * RANK)
            for each, ref in zip(told, (mine_ref, other_ref)):
                chosen = lanes(each[1 + block : 2 + block] == owner.astype(F32), width // HD)
                total = total + jnp.where(chosen, ref[part, :].astype(F32), 0.0)
        outs[s][:RANK, :] = total.astype(BF16)
        outs[s][RANK:, :] = jnp.zeros((PAD, width), BF16)
        for part in range(share // PAD):
            start = pl.multiple_of(owner * share + part * PAD, PAD)
            outs[s][RANK:, part * HD : part * HD + RANK] = rank_ref[pl.ds(start, PAD), :].astype(BF16)


def by_tenant(mine, other, own_message, other_message, ranks, owners):
    width = mine.shape[1]
    return pl.pallas_call(
        functools.partial(tenants_kernel, owners),
        in_specs=[VMEM] * 5,
        out_specs=[VMEM] * owners,
        out_shape=[jax.ShapeDtypeStruct((RANK + PAD, width), BF16)] * owners,
        name="by_tenant",
        **small(1 << 20),
    )(mine, other, own_message, other_message, ranks)


def columns_owner_kernel(owners, *refs):
    pieces, outs = refs[:owners], refs[owners:]
    ctx, adp = lax.axis_index("ctx"), lax.axis_index("adp")
    z = ctx // CORES
    for s in range(owners):
        source = lax.rem(adp - z - s + 2 * owners, owners)
        for j in range(owners):

            @pl.when(source == j)
            def _(s=s, j=j):
                outs[s][...] = pieces[j][:RANK, :]


def by_columns_owner(pieces):
    owners = len(pieces)
    width = pieces[0].shape[1]
    return pl.pallas_call(
        functools.partial(columns_owner_kernel, owners),
        in_specs=[VMEM] * owners,
        out_specs=[VMEM] * owners,
        out_shape=[jax.ShapeDtypeStruct((RANK, width), BF16)] * owners,
        name="by_columns_owner",
        **small(1 << 20),
    )(*pieces)


def finish_kernel(owners, *refs):
    parts, pieces = refs[:CORES], refs[CORES : owners + CORES]
    dq_hbm, rank_out, sem = refs[owners + CORES :]
    half = parts[0].shape[1]
    core = lax.rem(lax.axis_index("ctx"), CORES)
    copies = []
    for part, ref in enumerate(parts):
        start = pl.multiple_of((core if part else 1 - core) * half, HD)
        copies.append(pltpu.make_async_copy(ref, dq_hbm.at[:, pl.ds(start, half)], sem.at[part]))
        copies[-1].start()
    for part in range(rank_out.shape[0] // PAD):
        rank_out[part * PAD : (part + 1) * PAD, :] = sum(
            piece[RANK:, part * HD : part * HD + RANK].astype(F32) for piece in pieces
        )
    for copy in copies:
        copy.wait()


def finish(dq, pieces, share):
    owners = len(pieces)
    return pl.pallas_call(
        functools.partial(finish_kernel, owners),
        in_specs=[VMEM] * (CORES + owners),
        out_specs=[ANY, VMEM],
        out_shape=[
            jax.ShapeDtypeStruct((dq[0].shape[0], CORES * dq[0].shape[1]), BF16),
            jax.ShapeDtypeStruct((share, RANK), F32),
        ],
        scratch_shapes=[pltpu.SemaphoreType.DMA((CORES,))],
        name="finish",
        **small(1 << 20),
    )(*dq, *pieces)


def on_device(queries, keys, values, grad_out, docs, block_tenant, low_rank, adapter_b):
    positions, owners = lax.axis_size("ctx"), lax.axis_size("adp")
    chips = positions // CORES
    tokens = queries.shape[0]
    heads_dev = queries.shape[1] // HD
    swap = [(c, c ^ 1) for c in range(positions)]
    up = lambda s: [(c, (c + CORES * s) % positions) for c in range(positions)]
    along = lambda s: [(a, (a + s) % owners) for a in range(owners)]

    message = pack(block_tenant, keys, values, docs, heads_dev)
    shifts = [2, *range(3, chips), 1]
    arrive = {s: lax.ppermute(message, "ctx", up(s)) for s in (2, 1, *range(3, chips))}
    own = [arrive[s] for s in shifts]
    mine_other = lax.ppermute(message, "ctx", swap)
    b_out = columns(adapter_b, mine_other, owners)

    def apart(s):
        return [
            (c * owners + a, c * owners + (a + (s if c % CORES == 0 else -s)) % owners)
            for c in range(positions)
            for a in range(owners)
        ]

    b_in = [lax.ppermute(b_out[s], ("ctx", "adp"), apart(s)) for s in range(1, owners // 2 + 1)]
    heads = (queries, grad_out, message)
    state = attend((0,), *heads, [message], [mine_other])
    own = [*own[1:], own[0]]
    own, state, b_in = lax.optimization_barrier((own, state, b_in))
    other = [lax.ppermute(m, "ctx", swap) for m in own]
    b_swapped = [lax.ppermute(x, "ctx", swap) for x in b_in[:-1]]
    b_cols = [b_out[0], *b_in, *reversed(b_swapped)]
    own, other = [[each[-2], each[-1], *each[:-2]] for each in (own, other)]
    last = functools.partial(attend, tuple(range(1, chips)), *heads, own, other, state)
    dq_other, partner = last((0, low_rank))
    other_part = lax.ppermute(partner, "ctx", swap)
    dq_mine, mine, ranks = last((1, low_rank, dq_other, b_cols))
    pieces = by_tenant(mine, other_part, message, mine_other, ranks, owners)
    pieces = [pieces[0]] + [
        lax.ppermute(pieces[s], "adp", along(s)) for s in range(1, owners)
    ]
    grad_queries, grad_low_rank = finish([dq_other, dq_mine], pieces, tokens // owners)
    pieces = by_columns_owner(pieces)
    pieces = [pieces[0]] + [lax.ppermute(pieces[s], "ctx", up(s)) for s in range(1, chips)]
    grad_adapter = sum(piece.astype(F32) for piece in pieces)[None]
    return grad_queries, grad_low_rank, grad_adapter


def solution(mesh):
    placed = (
        P("ctx", "adp"),
        P("ctx", None),
        P("ctx", None),
        P("ctx", "adp"),
        P("ctx"),
        P("ctx"),
        P("ctx", None),
        P("adp", None, None),
    )
    return jax.shard_map(
        on_device,
        mesh=mesh,
        in_specs=placed,
        out_specs=(P("ctx", "adp"), P(("ctx", "adp"), None), P("adp", None, "ctx")),
        check_vma=False,
    )
```

time: 46.6 us -> 45.8 us (0.983)
  waiting for transfers between devices: 8.76 us -> 7.88 us
    ppermute x3, waiting for transfers between devices: 3.47 us -> 1.26 us  [on_device(): lax.ppermute(message, 'ctx', up(s))]
    ppermute x7, waiting for transfers between devices: 0.63 us -> 2.44 us  [the longest x2 1.58 us: on_device(): lax.ppermute(b_out[s], ('ctx', 'adp'), apart(s))]
    ppermute x3, starting transfers between devices: 9.73 us -> 11.3 us  [on_device(): lax.ppermute(pieces[s], 'ctx', up(s))]
    ppermute x1, waiting for transfers between devices: 1.04 us -> 0.01 us  [on_device(): other_part = lax.ppermute(partner, 'ctx', swap)]
    ppermute x3, starting transfers between devices: 4.5 us -> 3.48 us  [on_device(): lax.ppermute(pieces[s], 'adp', along(s))]
    ppermute x7, starting transfers between devices: 5.59 us -> 4.6 us  [the longest x2 3.06 us: on_device(): lax.ppermute(b_out[s], ('ctx', 'adp'), apart(s))]
    ppermute x3, starting transfers between devices: 6.73 us -> 7.49 us  [on_device(): lax.ppermute(message, 'ctx', up(s))]
    ppermute x3, waiting for transfers between devices: 0.64 us -> 1.11 us  [on_device(): lax.ppermute(pieces[s], 'ctx', up(s))]
  transfers between devices with their start and end apart: 17 -> 17, of which waited for: 10 -> 8; matrix products, arithmetic and copies ran while one was open for 0% -> 0% of each run, Pallas kernels for 10% -> 14%
where the time goes in v5:
time: 45.8 us; the launch traced here: 45.6 us
  starting transfers between devices  27.1 us (59%)
  Pallas kernels  8.11 us (18%)
  waiting for transfers between devices  7.88 us (17%)
  local copies, waits for them, and re-layouts  1.07 us (2%)
  between operations  0.77 us (2%)
  other arithmetic  0.69 us (2%)
    ppermute x3, starting transfers between devices, on_device(): lax.ppermute(pieces[s], 'ctx', up(s))  11.3 us
    ppermute x3, starting transfers between devices, on_device(): lax.ppermute(message, 'ctx', up(s))  7.49 us
    pallas_call x3, Pallas kernels, attend(): pl.pallas_call(functools.partial(attend_kernel, shifts, parts, not state,...  4.72 us
    ppermute x3, starting transfers between devices, on_device(): lax.ppermute(pieces[s], 'adp', along(s))  3.48 us
    ppermute x3, waiting for transfers between devices, on_device(): lax.ppermute(pieces[s], 'adp', along(s))  3.07 us
    ppermute x2, starting transfers between devices, on_device(): lax.ppermute(b_out[s], ('ctx', 'adp'), apart(s))  3.06 us
    ppermute x2, waiting for transfers between devices, on_device(): lax.ppermute(b_out[s], ('ctx', 'adp'), apart(s))  1.58 us
    pallas_call x1, Pallas kernels, pack(): pl.pallas_call(functools.partial(pack_kernel, heads_dev), in_specs=[HBM]...  1.58 us
  transfers between devices with their start and end apart: 17, of which 8 were waited for; matrix products, arithmetic and copies ran while one was open for 0% of the time, Pallas kernels for 14%

profile of v5, /device:TPU:0, one launch (start us, length us, event | category | flops | bytes accessed | tf_op | source)
XLA Modules:
  0.0 45.6 jit_solution(1927074381112447657)
XLA Ops:
  0.6 1.6 %pack.1.refs_2_.refs_3_.own_notes = bf16[272,256]{1,0:T(8,128)(2,1)} custom-call(s32[2]{0:T(128)} %tenant_hbm.1, bf16[256,512]{1,0:T(8,128)(2,1)} %keys.1, bf16[256,512]{1,0:T(8,128)(2,1)} %values.1, s32[1,256]{1,0:T(1,128)} %bitcast.6), custom_call_target="tpu_custom_call" | custom-call | bytes 262144 | tf_op jit(solution)/shard_map/pack/pallas_call | solution.py:64
  2.2 0.0 copy-start
  2.2 0.0 copy-start.1
  2.2 0.0 copy-start.2
  2.3 0.5 %collective-permute-start.3 = (bf16[272,256]{1,0:T(8,128)(2,1)}, bf16[272,256]{1,0:T(8,128)(2,1)S(1)}, u32[]{:S(2)}, u32[]{:S(2)}) collective-permute-start(bf16[272,256]{1,0:T(8,128)(2,1)} %pack.1.refs_2_.refs_3_.own_notes), channel_id=1, source_target_pairs={{0,4},{4,0},{8,12},{12,8},{16,20},{20,16},{24,28},{28,24},{1,5},{5... | collective-permute-start | bytes 417800 | tf_op jit(solution)/shard_map/ppermute | solution.py:393
  2.8 3.7 %collective-permute-start.2 = (bf16[272,256]{1,0:T(8,128)(2,1)}, bf16[272,256]{1,0:T(8,128)(2,1)S(1)}, u32[]{:S(2)}, u32[]{:S(2)}) collective-permute-start(bf16[272,256]{1,0:T(8,128)(2,1)} %pack.1.refs_2_.refs_3_.own_notes), channel_id=1, source_target_pairs={{0,16},{4,20},{8,24},{12,28},{16,0},{20,4},{24,8},{28,12},{1,17},{... | collective-permute-start | bytes 417800 | tf_op jit(solution)/shard_map/ppermute | solution.py:391
  6.4 1.6 %collective-permute-start.1 = (bf16[272,256]{1,0:T(8,128)(2,1)}, bf16[272,256]{1,0:T(8,128)(2,1)S(1)}, u32[]{:S(2)}, u32[]{:S(2)}) collective-permute-start(bf16[272,256]{1,0:T(8,128)(2,1)} %pack.1.refs_2_.refs_3_.own_notes), channel_id=1, source_target_pairs={{0,8},{4,12},{8,16},{12,20},{16,24},{20,28},{24,0},{28,4},{1,9},{5... | collective-permute-start | bytes 417800 | tf_op jit(solution)/shard_map/ppermute | solution.py:391
  8.0 2.2 %collective-permute-start = (bf16[272,256]{1,0:T(8,128)(2,1)}, bf16[272,256]{1,0:T(8,128)(2,1)S(1)}, u32[]{:S(2)}, u32[]{:S(2)}) collective-permute-start(bf16[272,256]{1,0:T(8,128)(2,1)} %pack.1.refs_2_.refs_3_.own_notes), channel_id=1, source_target_pairs={{0,24},{4,28},{8,0},{12,4},{16,8},{20,12},{24,16},{28,20},{1,25},{... | collective-permute-start | bytes 417800 | tf_op jit(solution)/shard_map/ppermute | solution.py:391
  10.3 0.0 collective-permute-done.3.refs_4_.after.other_notes
  10.3 1.0 %copy-done.4 = bf16[1,64,4096]{2,1,0:T(8,128)(2,1)S(1)} copy-done((bf16[1,64,4096]{2,1,0:T(8,128)(2,1)S(1)}, bf16[1,64,4096]{2,1,0:T(8,128)(2,1)}, u32[]{:S(2)}) %copy-start.4) | copy-done | bytes 524312
  11.3 0.1 columns.1
  11.4 0.0 copy-start.3
  11.4 1.5 %collective-permute-start.4 = (bf16[64,1024]{1,0:T(8,128)(2,1)S(1)}, bf16[64,1024]{1,0:T(8,128)(2,1)S(1)}, u32[]{:S(2)}, u32[]{:S(2)}) collective-permute-start(bf16[64,1024]{1,0:T(8,128)(2,1)S(1)} %get-tuple-element.35), channel_id=1, source_target_pairs={{0,1},{1,2},{2,3},{3,0},{4,7},{5,4},{6,5},{7,6},{8,9},{9,10},{10,1... | collective-permute-start | bytes 393224 | tf_op jit(solution)/shard_map/ppermute | solution.py:403
  13.0 1.5 %collective-permute-start.5 = (bf16[64,1024]{1,0:T(8,128)(2,1)S(1)}, bf16[64,1024]{1,0:T(8,128)(2,1)S(1)}, u32[]{:S(2)}, u32[]{:S(2)}) collective-permute-start(bf16[64,1024]{1,0:T(8,128)(2,1)S(1)} %get-tuple-element.36), channel_id=1, source_target_pairs={{0,2},{1,3},{2,0},{3,1},{4,6},{5,7},{6,4},{7,5},{8,10},{9,11},{10,... | collective-permute-start | bytes 393224 | tf_op jit(solution)/shard_map/ppermute | solution.py:403
  14.5 2.7 %attend_0.1 = (f32[2048,128]{1,0:T(8,128)S(1)}, f32[2048,256]{1,0:T(8,128)S(1)}, f32[2048,256]{1,0:T(8,128)S(1)}) custom-call(bf16[256,1024]{1,0:T(8,128)(2,1)S(1)} %copy-done.1, bf16[256,1024]{1,0:T(8,128)(2,1)S(1)} %copy-done.2, bf16[272,256]{1,0:T(8,128)(2,1)S(1)} %copy-done, bf16[272,256]{1,0:T(8,128)(2,1)S(1)} %copy-done, ...), custom_call_target="tpu_custom_call" | custom-call | flops 805306368 | bytes 4194304 | tf_op jit(solution)/shard_map/attend_0/pallas_call | solution.py:271
  17.2 0.0 collective-permute-done.2.refs_4_
  17.2 0.0 collective-permute-done.1.refs_3_
  17.2 1.3 %collective-permute-done.refs_5_ = bf16[272,256]{1,0:T(8,128)(2,1)S(1)} collective-permute-done((bf16[272,256]{1,0:T(8,128)(2,1)}, bf16[272,256]{1,0:T(8,128)(2,1)S(1)}, u32[]{:S(2)}, u32[]{:S(2)}) %collective-permute-start) | collective-permute-done | bytes 139296 | tf_op jit(solution)/shard_map/ppermute | solution.py:391
  18.5 0.0 collective-permute-done.4.refs_14_
  18.5 1.6 %collective-permute-done.5.refs_15_ = bf16[64,1024]{1,0:T(8,128)(2,1)S(1)} collective-permute-done((bf16[64,1024]{1,0:T(8,128)(2,1)S(1)}, bf16[64,1024]{1,0:T(8,128)(2,1)S(1)}, u32[]{:S(2)}, u32[]{:S(2)}) %collective-permute-start.5) | collective-permute-done | bytes 131104 | tf_op jit(solution)/shard_map/ppermute | solution.py:403
  20.1 0.0 collective-permute-start.6
  20.1 0.5 %collective-permute-start.7 = (bf16[272,256]{1,0:T(8,128)(2,1)S(1)}, bf16[272,256]{1,0:T(8,128)(2,1)S(1)}, u32[]{:S(2)}, u32[]{:S(2)}) collective-permute-start(bf16[272,256]{1,0:T(8,128)(2,1)S(1)} %collective-permute-done.2.refs_4_), channel_id=1, source_target_pairs={{0,4},{4,0},{8,12},{12,8},{16,20},{20,16},{24,28},{28,24},{1,5},{5... | collective-permute-start | bytes 417800 | tf_op jit(solution)/shard_map/ppermute | solution.py:408
  20.6 0.0 collective-permute-start.8
  20.6 0.5 %collective-permute-start.9 = (bf16[64,1024]{1,0:T(8,128)(2,1)S(1)}, bf16[64,1024]{1,0:T(8,128)(2,1)S(1)}, u32[]{:S(2)}, u32[]{:S(2)}) collective-permute-start(bf16[64,1024]{1,0:T(8,128)(2,1)S(1)} %collective-permute-done.4.refs_14_), channel_id=1, source_target_pairs={{0,4},{4,0},{8,12},{12,8},{16,20},{20,16},{24,28},{28,24},{1,5},{5... | collective-permute-start | bytes 393224 | tf_op jit(solution)/shard_map/ppermute | solution.py:409
  21.1 0.3 collective-permute-done.6.refs_6_
  21.4 0.2 collective-permute-done.7.refs_7_
  21.6 0.3 collective-permute-done.8.refs_8_
  21.9 0.6 %attend_1_2_3_part0.1 = (bf16[256,512]{1,0:T(8,128)(2,1)S(1)}, bf16[128,512]{1,0:T(8,128)(2,1)S(1)}) custom-call(bf16[256,1024]{1,0:T(8,128)(2,1)S(1)} %copy-done.1, bf16[256,1024]{1,0:T(8,128)(2,1)S(1)} %copy-done.2, bf16[272,256]{1,0:T(8,128)(2,1)S(1)} %copy-done, bf16[272,256]{1,0:T(8,128)(2,1)S(1)} %collective-permute-done.1.refs_3_, ...), custom_call_target="tpu_custom_call" | custom-call | flops 1207959552 | bytes 4194304 | tf_op jit(solution)/shard_map/attend_1_2_3_part0/pallas_call | solution.py:271
  22.6 0.3 collective-permute-start.10
  22.8 0.0 collective-permute-done.9.refs_16_
  22.8 1.4 %attend_1_2_3_part1.1 = (bf16[256,512]{1,0:T(8,128)(2,1)S(1)}, f32[128,512]{1,0:T(8,128)S(1)}, f32[256,64]{1,0:T(8,128)S(1)}) custom-call(bf16[256,1024]{1,0:T(8,128)(2,1)S(1)} %copy-done.1, bf16[256,1024]{1,0:T(8,128)(2,1)S(1)} %copy-done.2, bf16[272,256]{1,0:T(8,128)(2,1)S(1)} %copy-done, bf16[272,256]{1,0:T(8,128)(2,1)S(1)} %collective-permute-done.1.refs_3_, ...), custom_call_target="tpu_custom_call" | custom-call | flops 1207959552 | bytes 4194304 | tf_op jit(solution)/shard_map/attend_1_2_3_part1/pallas_call | solution.py:271
  24.2 0.0 collective-permute-done.10.other_ref
  24.3 0.2 by_tenant.1
  24.5 0.1 collective-permute-start.11
  24.5 1.5 %collective-permute-start.12 = (bf16[80,512]{1,0:T(8,128)(2,1)S(1)}, bf16[80,512]{1,0:T(8,128)(2,1)S(1)}, u32[]{:S(2)}, u32[]{:S(2)}) collective-permute-start(bf16[80,512]{1,0:T(8,128)(2,1)S(1)} %get-tuple-element.53), channel_id=1, source_target_pairs={{0,2},{1,3},{2,0},{3,1},{4,6},{5,7},{6,4},{7,5},{8,10},{9,11},{10,... | collective-permute-start | bytes 245768 | tf_op jit(solution)/shard_map/ppermute | solution.py:418
  26.0 1.9 %collective-permute-start.13 = (bf16[80,512]{1,0:T(8,128)(2,1)S(1)}, bf16[80,512]{1,0:T(8,128)(2,1)S(1)}, u32[]{:S(2)}, u32[]{:S(2)}) collective-permute-start(bf16[80,512]{1,0:T(8,128)(2,1)S(1)} %get-tuple-element.54), channel_id=1, source_target_pairs={{0,3},{1,0},{2,1},{3,2},{4,7},{5,4},{6,5},{7,6},{8,11},{9,8},{10,9... | collective-permute-start | bytes 245768 | tf_op jit(solution)/shard_map/ppermute | solution.py:418
  27.9 2.8 %collective-permute-done.11.refs_3_.refs_1_ = bf16[80,512]{1,0:T(8,128)(2,1)S(1)} collective-permute-done((bf16[80,512]{1,0:T(8,128)(2,1)S(1)}, bf16[80,512]{1,0:T(8,128)(2,1)S(1)}, u32[]{:S(2)}, u32[]{:S(2)}) %collective-permute-start.11) | collective-permute-done | bytes 81952 | tf_op jit(solution)/shard_map/ppermute | solution.py:418
  30.7 0.3 collective-permute-done.12.refs_4_.refs_2_
  31.0 0.0 collective-permute-done.13.refs_5_.refs_3_
  31.0 0.1 by_columns_owner.1
  31.1 4.0 %collective-permute-start.14 = (bf16[64,512]{1,0:T(8,128)(2,1)S(1)}, bf16[64,512]{1,0:T(8,128)(2,1)S(1)}, u32[]{:S(2)}, u32[]{:S(2)}) collective-permute-start(bf16[64,512]{1,0:T(8,128)(2,1)S(1)} %get-tuple-element.58), channel_id=1, source_target_pairs={{0,8},{4,12},{8,16},{12,20},{16,24},{20,28},{24,0},{28,4},{1,9},{5... | collective-permute-start | bytes 196616 | tf_op jit(solution)/shard_map/ppermute | solution.py:422
  35.1 5.3 %collective-permute-start.15 = (bf16[64,512]{1,0:T(8,128)(2,1)S(1)}, bf16[64,512]{1,0:T(8,128)(2,1)S(1)}, u32[]{:S(2)}, u32[]{:S(2)}) collective-permute-start(bf16[64,512]{1,0:T(8,128)(2,1)S(1)} %get-tuple-element.59), channel_id=1, source_target_pairs={{0,16},{4,20},{8,24},{12,28},{16,0},{20,4},{24,8},{28,12},{1,17},{... | collective-permute-start | bytes 196616 | tf_op jit(solution)/shard_map/ppermute | solution.py:422
  40.4 1.9 %collective-permute-start.16 = (bf16[64,512]{1,0:T(8,128)(2,1)S(1)}, bf16[64,512]{1,0:T(8,128)(2,1)S(1)}, u32[]{:S(2)}, u32[]{:S(2)}) collective-permute-start(bf16[64,512]{1,0:T(8,128)(2,1)S(1)} %get-tuple-element.60), channel_id=1, source_target_pairs={{0,24},{4,28},{8,0},{12,4},{16,8},{20,12},{24,16},{28,20},{1,25},{... | collective-permute-start | bytes 196616 | tf_op jit(solution)/shard_map/ppermute | solution.py:422
  42.4 1.4 %finish.1 = (bf16[256,1024]{1,0:T(8,128)(2,1)}, f32[64,64]{1,0:T(8,128)}) custom-call(bf16[256,512]{1,0:T(8,128)(2,1)S(1)} %get-tuple-element.43.refs_17_.refs_0_, bf16[256,512]{1,0:T(8,128)(2,1)S(1)} %get-tuple-element.47.refs_1_, bf16[80,512]{1,0:T(8,128)(2,1)S(1)} %get-tuple-element.51.refs_2_.refs_0_, ...), custom_call_target="tpu_custom_call" | custom-call | bytes 1048576 | tf_op jit(solution)/shard_map/finish/pallas_call | solution.py:366
  43.8 0.0 collective-permute-done.14
  43.8 1.1 %collective-permute-done.15 = bf16[64,512]{1,0:T(8,128)(2,1)S(1)} collective-permute-done((bf16[64,512]{1,0:T(8,128)(2,1)S(1)}, bf16[64,512]{1,0:T(8,128)(2,1)S(1)}, u32[]{:S(2)}, u32[]{:S(2)}) %collective-permute-start.15) | collective-permute-done | bytes 65568 | tf_op jit(solution)/shard_map/ppermute | solution.py:422
  44.9 0.0 collective-permute-done.16
  44.9 0.7 %add_bitcast_fusion = f32[1,64,512]{2,1,0:T(8,128)} fusion(bf16[64,512]{1,0:T(8,128)(2,1)S(1)} %collective-permute-done.16, bf16[64,512]{1,0:T(8,128)(2,1)S(1)} %collective-permute-done.15, bf16[64,512]{1,0:T(8,128)(2,1)S(1)} %collective-permute-done.14, bf16[64,512]{1,0:T(8,128)(2,1)S(1)} %get-tuple-element.57), kind=kLoop, calls=%fused_computation | loop fusion | flops 229376 | bytes 393216 | tf_op jit(solution)/shard_map/broadcast_in_dim | solution.py:423
  (5 shorter events, 0.0 us)
Async XLA Ops:
  2.2 12.3 %copy-start = (bf16[272,256]{1,0:T(8,128)(2,1)S(1)}, bf16[272,256]{1,0:T(8,128)(2,1)}, u32[]{:S(2)}) copy-start(bf16[272,256]{1,0:T(8,128)(2,1)} %pack.1.refs_2_.refs_3_.own_notes) | copy-start | bytes 417796
  2.2 12.3 %copy-start.1 = (bf16[256,1024]{1,0:T(8,128)(2,1)S(1)}, bf16[256,1024]{1,0:T(8,128)(2,1)}, u32[]{:S(2)}) copy-start(bf16[256,1024]{1,0:T(8,128)(2,1)} %refs_0_.5) | copy-start | bytes 1572868
  2.2 12.3 %copy-start.2 = (bf16[256,1024]{1,0:T(8,128)(2,1)S(1)}, bf16[256,1024]{1,0:T(8,128)(2,1)}, u32[]{:S(2)}) copy-start(bf16[256,1024]{1,0:T(8,128)(2,1)} %refs_1_.5) | copy-start | bytes 1572868
  2.3 8.0 %collective-permute-start.3 = (bf16[272,256]{1,0:T(8,128)(2,1)}, bf16[272,256]{1,0:T(8,128)(2,1)S(1)}, u32[]{:S(2)}, u32[]{:S(2)}) collective-permute-start(bf16[272,256]{1,0:T(8,128)(2,1)} %pack.1.refs_2_.refs_3_.own_notes), channel_id=1, source_target_pairs={{0,4},{4,0},{8,12},{12,8},{16,20},{20,16},{24,28},{28,24},{1,5},{5... | collective-permute-start | bytes 417800 | tf_op jit(solution)/shard_map/ppermute | solution.py:393
  2.8 14.4 %collective-permute-start.2 = (bf16[272,256]{1,0:T(8,128)(2,1)}, bf16[272,256]{1,0:T(8,128)(2,1)S(1)}, u32[]{:S(2)}, u32[]{:S(2)}) collective-permute-start(bf16[272,256]{1,0:T(8,128)(2,1)} %pack.1.refs_2_.refs_3_.own_notes), channel_id=1, source_target_pairs={{0,16},{4,20},{8,24},{12,28},{16,0},{20,4},{24,8},{28,12},{1,17},{... | collective-permute-start | bytes 417800 | tf_op jit(solution)/shard_map/ppermute | solution.py:391
  6.4 10.8 %collective-permute-start.1 = (bf16[272,256]{1,0:T(8,128)(2,1)}, bf16[272,256]{1,0:T(8,128)(2,1)S(1)}, u32[]{:S(2)}, u32[]{:S(2)}) collective-permute-start(bf16[272,256]{1,0:T(8,128)(2,1)} %pack.1.refs_2_.refs_3_.own_notes), channel_id=1, source_target_pairs={{0,8},{4,12},{8,16},{12,20},{16,24},{20,28},{24,0},{28,4},{1,9},{5... | collective-permute-start | bytes 417800 | tf_op jit(solution)/shard_map/ppermute | solution.py:391
  8.0 10.5 %collective-permute-start = (bf16[272,256]{1,0:T(8,128)(2,1)}, bf16[272,256]{1,0:T(8,128)(2,1)S(1)}, u32[]{:S(2)}, u32[]{:S(2)}) collective-permute-start(bf16[272,256]{1,0:T(8,128)(2,1)} %pack.1.refs_2_.refs_3_.own_notes), channel_id=1, source_target_pairs={{0,24},{4,28},{8,0},{12,4},{16,8},{20,12},{24,16},{28,20},{1,25},{... | collective-permute-start | bytes 417800 | tf_op jit(solution)/shard_map/ppermute | solution.py:391
  10.3 1.0 %copy-start.4 = (bf16[1,64,4096]{2,1,0:T(8,128)(2,1)S(1)}, bf16[1,64,4096]{2,1,0:T(8,128)(2,1)}, u32[]{:S(2)}) copy-start(bf16[1,64,4096]{2,1,0:T(8,128)(2,1)} %adapter_b.1) | copy-start | bytes 1572868
  11.4 10.5 %copy-start.3 = (bf16[256,64]{0,1:T(8,128)(2,1)S(1)}, bf16[256,64]{0,1:T(8,128)(2,1)}, u32[]{:S(2)}) copy-start(bf16[256,64]{0,1:T(8,128)(2,1)} %param.14) | copy-start | bytes 98308
  11.4 7.0 %collective-permute-start.4 = (bf16[64,1024]{1,0:T(8,128)(2,1)S(1)}, bf16[64,1024]{1,0:T(8,128)(2,1)S(1)}, u32[]{:S(2)}, u32[]{:S(2)}) collective-permute-start(bf16[64,1024]{1,0:T(8,128)(2,1)S(1)} %get-tuple-element.35), channel_id=1, source_target_pairs={{0,1},{1,2},{2,3},{3,0},{4,7},{5,4},{6,5},{7,6},{8,9},{9,10},{10,1... | collective-permute-start | bytes 393224 | tf_op jit(solution)/shard_map/ppermute | solution.py:403
  13.0 7.1 %collective-permute-start.5 = (bf16[64,1024]{1,0:T(8,128)(2,1)S(1)}, bf16[64,1024]{1,0:T(8,128)(2,1)S(1)}, u32[]{:S(2)}, u32[]{:S(2)}) collective-permute-start(bf16[64,1024]{1,0:T(8,128)(2,1)S(1)} %get-tuple-element.36), channel_id=1, source_target_pairs={{0,2},{1,3},{2,0},{3,1},{4,6},{5,7},{6,4},{7,5},{8,10},{9,11},{10,... | collective-permute-start | bytes 393224 | tf_op jit(solution)/shard_map/ppermute | solution.py:403
  20.1 1.4 %collective-permute-start.6 = (bf16[272,256]{1,0:T(8,128)(2,1)S(1)}, bf16[272,256]{1,0:T(8,128)(2,1)S(1)}, u32[]{:S(2)}, u32[]{:S(2)}) collective-permute-start(bf16[272,256]{1,0:T(8,128)(2,1)S(1)} %collective-permute-done.1.refs_3_), channel_id=1, source_target_pairs={{0,4},{4,0},{8,12},{12,8},{16,20},{20,16},{24,28},{28,24},{1,5},{5... | collective-permute-start | bytes 417800 | tf_op jit(solution)/shard_map/ppermute | solution.py:408
  20.1 1.6 %collective-permute-start.7 = (bf16[272,256]{1,0:T(8,128)(2,1)S(1)}, bf16[272,256]{1,0:T(8,128)(2,1)S(1)}, u32[]{:S(2)}, u32[]{:S(2)}) collective-permute-start(bf16[272,256]{1,0:T(8,128)(2,1)S(1)} %collective-permute-done.2.refs_4_), channel_id=1, source_target_pairs={{0,4},{4,0},{8,12},{12,8},{16,20},{20,16},{24,28},{28,24},{1,5},{5... | collective-permute-start | bytes 417800 | tf_op jit(solution)/shard_map/ppermute | solution.py:408
  20.6 1.4 %collective-permute-start.8 = (bf16[272,256]{1,0:T(8,128)(2,1)S(1)}, bf16[272,256]{1,0:T(8,128)(2,1)S(1)}, u32[]{:S(2)}, u32[]{:S(2)}) collective-permute-start(bf16[272,256]{1,0:T(8,128)(2,1)S(1)} %collective-permute-done.refs_5_), channel_id=1, source_target_pairs={{0,4},{4,0},{8,12},{12,8},{16,20},{20,16},{24,28},{28,24},{1,5},{5... | collective-permute-start | bytes 417800 | tf_op jit(solution)/shard_map/ppermute | solution.py:408
  20.6 2.3 %collective-permute-start.9 = (bf16[64,1024]{1,0:T(8,128)(2,1)S(1)}, bf16[64,1024]{1,0:T(8,128)(2,1)S(1)}, u32[]{:S(2)}, u32[]{:S(2)}) collective-permute-start(bf16[64,1024]{1,0:T(8,128)(2,1)S(1)} %collective-permute-done.4.refs_14_), channel_id=1, source_target_pairs={{0,4},{4,0},{8,12},{12,8},{16,20},{20,16},{24,28},{28,24},{1,5},{5... | collective-permute-start | bytes 393224 | tf_op jit(solution)/shard_map/ppermute | solution.py:409
  22.6 1.7 %collective-permute-start.10 = (bf16[128,512]{1,0:T(8,128)(2,1)S(1)}, bf16[128,512]{1,0:T(8,128)(2,1)S(1)}, u32[]{:S(2)}, u32[]{:S(2)}) collective-permute-start(bf16[128,512]{1,0:T(8,128)(2,1)S(1)} %get-tuple-element.49), channel_id=1, source_target_pairs={{0,4},{4,0},{8,12},{12,8},{16,20},{20,16},{24,28},{28,24},{1,5},{5... | collective-permute-start | bytes 393224 | tf_op jit(solution)/shard_map/ppermute | solution.py:414
  24.5 6.3 %collective-permute-start.11 = (bf16[80,512]{1,0:T(8,128)(2,1)S(1)}, bf16[80,512]{1,0:T(8,128)(2,1)S(1)}, u32[]{:S(2)}, u32[]{:S(2)}) collective-permute-start(bf16[80,512]{1,0:T(8,128)(2,1)S(1)} %get-tuple-element.52), channel_id=1, source_target_pairs={{0,1},{1,2},{2,3},{3,0},{4,5},{5,6},{6,7},{7,4},{8,9},{9,10},{10,1... | collective-permute-start | bytes 245768 | tf_op jit(solution)/shard_map/ppermute | solution.py:418
  24.5 6.5 %collective-permute-start.12 = (bf16[80,512]{1,0:T(8,128)(2,1)S(1)}, bf16[80,512]{1,0:T(8,128)(2,1)S(1)}, u32[]{:S(2)}, u32[]{:S(2)}) collective-permute-start(bf16[80,512]{1,0:T(8,128)(2,1)S(1)} %get-tuple-element.53), channel_id=1, source_target_pairs={{0,2},{1,3},{2,0},{3,1},{4,6},{5,7},{6,4},{7,5},{8,10},{9,11},{10,... | collective-permute-start | bytes 245768 | tf_op jit(solution)/shard_map/ppermute | solution.py:418
  26.0 5.0 %collective-permute-start.13 = (bf16[80,512]{1,0:T(8,128)(2,1)S(1)}, bf16[80,512]{1,0:T(8,128)(2,1)S(1)}, u32[]{:S(2)}, u32[]{:S(2)}) collective-permute-start(bf16[80,512]{1,0:T(8,128)(2,1)S(1)} %get-tuple-element.54), channel_id=1, source_target_pairs={{0,3},{1,0},{2,1},{3,2},{4,7},{5,4},{6,5},{7,6},{8,11},{9,8},{10,9... | collective-permute-start | bytes 245768 | tf_op jit(solution)/shard_map/ppermute | solution.py:418
  31.1 12.7 %collective-permute-start.14 = (bf16[64,512]{1,0:T(8,128)(2,1)S(1)}, bf16[64,512]{1,0:T(8,128)(2,1)S(1)}, u32[]{:S(2)}, u32[]{:S(2)}) collective-permute-start(bf16[64,512]{1,0:T(8,128)(2,1)S(1)} %get-tuple-element.58), channel_id=1, source_target_pairs={{0,8},{4,12},{8,16},{12,20},{16,24},{20,28},{24,0},{28,4},{1,9},{5... | collective-permute-start | bytes 196616 | tf_op jit(solution)/shard_map/ppermute | solution.py:422
  35.1 9.8 %collective-permute-start.15 = (bf16[64,512]{1,0:T(8,128)(2,1)S(1)}, bf16[64,512]{1,0:T(8,128)(2,1)S(1)}, u32[]{:S(2)}, u32[]{:S(2)}) collective-permute-start(bf16[64,512]{1,0:T(8,128)(2,1)S(1)} %get-tuple-element.59), channel_id=1, source_target_pairs={{0,16},{4,20},{8,24},{12,28},{16,0},{20,4},{24,8},{28,12},{1,17},{... | collective-permute-start | bytes 196616 | tf_op jit(solution)/shard_map/ppermute | solution.py:422
  40.4 4.5 %collective-permute-start.16 = (bf16[64,512]{1,0:T(8,128)(2,1)S(1)}, bf16[64,512]{1,0:T(8,128)(2,1)S(1)}, u32[]{:S(2)}, u32[]{:S(2)}) collective-permute-start(bf16[64,512]{1,0:T(8,128)(2,1)S(1)} %get-tuple-element.60), channel_id=1, source_target_pairs={{0,24},{4,28},{8,0},{12,4},{16,8},{20,12},{24,16},{28,20},{1,25},{... | collective-permute-start | bytes 196616 | tf_op jit(solution)/shard_map/ppermute | solution.py:422

commit v6 on v5

--- a/solution.py
+++ b/solution.py
@@ -152,8 +152,11 @@
         start = 0 if ref.shape[0] == part_rows else part * part_rows
         return slice(start, start + part_rows)
 
-    def step(indices, old):
+    def step(indices, old, later_core=False):
         messages = [ref for i in indices for ref in (own[i], other[i])]
+        if later_core:
+            (i,) = indices
+            messages = [jnp.where(core == 1, own[i][...], other[i][...])]
         keys = rows([ref[:tokens, :HD] for ref in messages])
         values = rows([ref[:tokens, HD:] for ref in messages])
         count = len(messages) * tokens
@@ -190,13 +193,18 @@
     if first:
         step([0], None)
     else:
-        needed = []
+        needed, both = [], []
         for index, shift in enumerate(shifts):
-            latest = jnp.max(jnp.maximum(doc_row(own[index]), doc_row(other[index])))
+            doc_rows = doc_row(own[index]), doc_row(other[index])
+            latest = jnp.max(jnp.maximum(*doc_rows))
             needed.append((z >= shift) & (latest == first_doc))
+            both.append(jnp.max(jnp.where(core == 0, *doc_rows)) == first_doc)
         for index in range(len(shifts)):
             old = sums if index else given
-            pl.when(needed[index])(functools.partial(step, [index], old))
+            pl.when(needed[index] & both[index])(functools.partial(step, [index], old))
+            pl.when(needed[index] & jnp.logical_not(both[index]))(
+                functools.partial(step, [index], old, True)
+            )
             if index == 0:
 
                 @pl.when(jnp.logical_not(needed[0]))

time: 45.8 us -> 45.9 us (level)
  no operation moved by 1% of the time
where the time goes in v6:
time: 45.9 us; the launch traced here: 45.7 us
  starting transfers between devices  27.1 us (59%)
  Pallas kernels  8.17 us (18%)
  waiting for transfers between devices  7.9 us (17%)
  local copies, waits for them, and re-layouts  1.07 us (2%)
  between operations  0.77 us (2%)
  other arithmetic  0.69 us (2%)
    ppermute x3, starting transfers between devices, on_device(): lax.ppermute(pieces[s], 'ctx', up(s))  11.3 us
    ppermute x3, starting transfers between devices, on_device(): lax.ppermute(message, 'ctx', up(s))  7.49 us
    pallas_call x3, Pallas kernels, attend(): pl.pallas_call(functools.partial(attend_kernel, shifts, parts, not state,...  4.78 us
    ppermute x3, starting transfers between devices, on_device(): lax.ppermute(pieces[s], 'adp', along(s))  3.46 us
    ppermute x3, waiting for transfers between devices, on_device(): lax.ppermute(pieces[s], 'adp', along(s))  3.08 us
    ppermute x2, starting transfers between devices, on_device(): lax.ppermute(b_out[s], ('ctx', 'adp'), apart(s))  3.06 us
    ppermute x2, waiting for transfers between devices, on_device(): lax.ppermute(b_out[s], ('ctx', 'adp'), apart(s))  1.58 us
    pallas_call x1, Pallas kernels, pack(): pl.pallas_call(functools.partial(pack_kernel, heads_dev), in_specs=[HBM]...  1.58 us
  transfers between devices with their start and end apart: 17, of which 8 were waited for; matrix products, arithmetic and copies ran while one was open for 0% of the time, Pallas kernels for 14%

profile of v6, /device:TPU:0, one launch (start us, length us, event | category | flops | bytes accessed | tf_op | source)
XLA Modules:
  0.0 45.7 jit_solution(12086180922057317826)
XLA Ops:
  0.6 1.6 %pack.1.refs_2_.refs_3_.own_notes = bf16[272,256]{1,0:T(8,128)(2,1)} custom-call(s32[2]{0:T(128)} %tenant_hbm.1, bf16[256,512]{1,0:T(8,128)(2,1)} %keys.1, bf16[256,512]{1,0:T(8,128)(2,1)} %values.1, s32[1,256]{1,0:T(1,128)} %bitcast.6), custom_call_target="tpu_custom_call" | custom-call | bytes 262144 | tf_op jit(solution)/shard_map/pack/pallas_call | solution.py:64
  2.2 0.0 copy-start
  2.2 0.0 copy-start.1
  2.2 0.0 copy-start.2
  2.3 0.5 %collective-permute-start.3 = (bf16[272,256]{1,0:T(8,128)(2,1)}, bf16[272,256]{1,0:T(8,128)(2,1)S(1)}, u32[]{:S(2)}, u32[]{:S(2)}) collective-permute-start(bf16[272,256]{1,0:T(8,128)(2,1)} %pack.1.refs_2_.refs_3_.own_notes), channel_id=1, source_target_pairs={{0,4},{4,0},{8,12},{12,8},{16,20},{20,16},{24,28},{28,24},{1,5},{5... | collective-permute-start | bytes 417800 | tf_op jit(solution)/shard_map/ppermute | solution.py:401
  2.8 3.7 %collective-permute-start.2 = (bf16[272,256]{1,0:T(8,128)(2,1)}, bf16[272,256]{1,0:T(8,128)(2,1)S(1)}, u32[]{:S(2)}, u32[]{:S(2)}) collective-permute-start(bf16[272,256]{1,0:T(8,128)(2,1)} %pack.1.refs_2_.refs_3_.own_notes), channel_id=1, source_target_pairs={{0,16},{4,20},{8,24},{12,28},{16,0},{20,4},{24,8},{28,12},{1,17},{... | collective-permute-start | bytes 417800 | tf_op jit(solution)/shard_map/ppermute | solution.py:399
  6.4 1.6 %collective-permute-start.1 = (bf16[272,256]{1,0:T(8,128)(2,1)}, bf16[272,256]{1,0:T(8,128)(2,1)S(1)}, u32[]{:S(2)}, u32[]{:S(2)}) collective-permute-start(bf16[272,256]{1,0:T(8,128)(2,1)} %pack.1.refs_2_.refs_3_.own_notes), channel_id=1, source_target_pairs={{0,8},{4,12},{8,16},{12,20},{16,24},{20,28},{24,0},{28,4},{1,9},{5... | collective-permute-start | bytes 417800 | tf_op jit(solution)/shard_map/ppermute | solution.py:399
  8.0 2.2 %collective-permute-start = (bf16[272,256]{1,0:T(8,128)(2,1)}, bf16[272,256]{1,0:T(8,128)(2,1)S(1)}, u32[]{:S(2)}, u32[]{:S(2)}) collective-permute-start(bf16[272,256]{1,0:T(8,128)(2,1)} %pack.1.refs_2_.refs_3_.own_notes), channel_id=1, source_target_pairs={{0,24},{4,28},{8,0},{12,4},{16,8},{20,12},{24,16},{28,20},{1,25},{... | collective-permute-start | bytes 417800 | tf_op jit(solution)/shard_map/ppermute | solution.py:399
  10.3 0.0 collective-permute-done.3.refs_4_.after.other_notes
  10.3 1.0 %copy-done.4 = bf16[1,64,4096]{2,1,0:T(8,128)(2,1)S(1)} copy-done((bf16[1,64,4096]{2,1,0:T(8,128)(2,1)S(1)}, bf16[1,64,4096]{2,1,0:T(8,128)(2,1)}, u32[]{:S(2)}) %copy-start.4) | copy-done | bytes 524312
  11.3 0.1 columns.1
  11.4 0.0 copy-start.3
  11.4 1.5 %collective-permute-start.4 = (bf16[64,1024]{1,0:T(8,128)(2,1)S(1)}, bf16[64,1024]{1,0:T(8,128)(2,1)S(1)}, u32[]{:S(2)}, u32[]{:S(2)}) collective-permute-start(bf16[64,1024]{1,0:T(8,128)(2,1)S(1)} %get-tuple-element.35), channel_id=1, source_target_pairs={{0,1},{1,2},{2,3},{3,0},{4,7},{5,4},{6,5},{7,6},{8,9},{9,10},{10,1... | collective-permute-start | bytes 393224 | tf_op jit(solution)/shard_map/ppermute | solution.py:411
  13.0 1.5 %collective-permute-start.5 = (bf16[64,1024]{1,0:T(8,128)(2,1)S(1)}, bf16[64,1024]{1,0:T(8,128)(2,1)S(1)}, u32[]{:S(2)}, u32[]{:S(2)}) collective-permute-start(bf16[64,1024]{1,0:T(8,128)(2,1)S(1)} %get-tuple-element.36), channel_id=1, source_target_pairs={{0,2},{1,3},{2,0},{3,1},{4,6},{5,7},{6,4},{7,5},{8,10},{9,11},{10,... | collective-permute-start | bytes 393224 | tf_op jit(solution)/shard_map/ppermute | solution.py:411
  14.5 2.7 %attend_0.1 = (f32[2048,128]{1,0:T(8,128)S(1)}, f32[2048,256]{1,0:T(8,128)S(1)}, f32[2048,256]{1,0:T(8,128)S(1)}) custom-call(bf16[256,1024]{1,0:T(8,128)(2,1)S(1)} %copy-done.1, bf16[256,1024]{1,0:T(8,128)(2,1)S(1)} %copy-done.2, bf16[272,256]{1,0:T(8,128)(2,1)S(1)} %copy-done, bf16[272,256]{1,0:T(8,128)(2,1)S(1)} %copy-done, ...), custom_call_target="tpu_custom_call" | custom-call | flops 805306368 | bytes 4194304 | tf_op jit(solution)/shard_map/attend_0/pallas_call | solution.py:279
  17.2 0.0 collective-permute-done.2.refs_4_
  17.2 0.0 collective-permute-done.1.refs_3_
  17.2 1.3 %collective-permute-done.refs_5_ = bf16[272,256]{1,0:T(8,128)(2,1)S(1)} collective-permute-done((bf16[272,256]{1,0:T(8,128)(2,1)}, bf16[272,256]{1,0:T(8,128)(2,1)S(1)}, u32[]{:S(2)}, u32[]{:S(2)}) %collective-permute-start) | collective-permute-done | bytes 139296 | tf_op jit(solution)/shard_map/ppermute | solution.py:399
  18.5 0.0 collective-permute-done.4.refs_14_
  18.5 1.6 %collective-permute-done.5.refs_15_ = bf16[64,1024]{1,0:T(8,128)(2,1)S(1)} collective-permute-done((bf16[64,1024]{1,0:T(8,128)(2,1)S(1)}, bf16[64,1024]{1,0:T(8,128)(2,1)S(1)}, u32[]{:S(2)}, u32[]{:S(2)}) %collective-permute-start.5) | collective-permute-done | bytes 131104 | tf_op jit(solution)/shard_map/ppermute | solution.py:411
  20.1 0.0 collective-permute-start.6
  20.1 0.5 %collective-permute-start.7 = (bf16[272,256]{1,0:T(8,128)(2,1)S(1)}, bf16[272,256]{1,0:T(8,128)(2,1)S(1)}, u32[]{:S(2)}, u32[]{:S(2)}) collective-permute-start(bf16[272,256]{1,0:T(8,128)(2,1)S(1)} %collective-permute-done.2.refs_4_), channel_id=1, source_target_pairs={{0,4},{4,0},{8,12},{12,8},{16,20},{20,16},{24,28},{28,24},{1,5},{5... | collective-permute-start | bytes 417800 | tf_op jit(solution)/shard_map/ppermute | solution.py:416
  20.6 0.0 collective-permute-start.8
  20.6 0.5 %collective-permute-start.9 = (bf16[64,1024]{1,0:T(8,128)(2,1)S(1)}, bf16[64,1024]{1,0:T(8,128)(2,1)S(1)}, u32[]{:S(2)}, u32[]{:S(2)}) collective-permute-start(bf16[64,1024]{1,0:T(8,128)(2,1)S(1)} %collective-permute-done.4.refs_14_), channel_id=1, source_target_pairs={{0,4},{4,0},{8,12},{12,8},{16,20},{20,16},{24,28},{28,24},{1,5},{5... | collective-permute-start | bytes 393224 | tf_op jit(solution)/shard_map/ppermute | solution.py:417
  21.1 0.3 collective-permute-done.6.refs_6_
  21.4 0.2 collective-permute-done.7.refs_7_
  21.6 0.3 collective-permute-done.8.refs_8_
  21.9 0.7 %attend_1_2_3_part0.1 = (bf16[256,512]{1,0:T(8,128)(2,1)S(1)}, bf16[128,512]{1,0:T(8,128)(2,1)S(1)}) custom-call(bf16[256,1024]{1,0:T(8,128)(2,1)S(1)} %copy-done.1, bf16[256,1024]{1,0:T(8,128)(2,1)S(1)} %copy-done.2, bf16[272,256]{1,0:T(8,128)(2,1)S(1)} %copy-done, bf16[272,256]{1,0:T(8,128)(2,1)S(1)} %collective-permute-done.1.refs_3_, ...), custom_call_target="tpu_custom_call" | custom-call | flops 1207959552 | bytes 4194304 | tf_op jit(solution)/shard_map/attend_1_2_3_part0/pallas_call | solution.py:279
  22.6 0.3 collective-permute-start.10
  22.9 0.0 collective-permute-done.9.refs_16_
  22.9 1.4 %attend_1_2_3_part1.1 = (bf16[256,512]{1,0:T(8,128)(2,1)S(1)}, f32[128,512]{1,0:T(8,128)S(1)}, f32[256,64]{1,0:T(8,128)S(1)}) custom-call(bf16[256,1024]{1,0:T(8,128)(2,1)S(1)} %copy-done.1, bf16[256,1024]{1,0:T(8,128)(2,1)S(1)} %copy-done.2, bf16[272,256]{1,0:T(8,128)(2,1)S(1)} %copy-done, bf16[272,256]{1,0:T(8,128)(2,1)S(1)} %collective-permute-done.1.refs_3_, ...), custom_call_target="tpu_custom_call" | custom-call | flops 1207959552 | bytes 4194304 | tf_op jit(solution)/shard_map/attend_1_2_3_part1/pallas_call | solution.py:279
  24.3 0.0 collective-permute-done.10.other_ref
  24.3 0.2 by_tenant.1
  24.5 0.1 collective-permute-start.11
  24.6 1.5 %collective-permute-start.12 = (bf16[80,512]{1,0:T(8,128)(2,1)S(1)}, bf16[80,512]{1,0:T(8,128)(2,1)S(1)}, u32[]{:S(2)}, u32[]{:S(2)}) collective-permute-start(bf16[80,512]{1,0:T(8,128)(2,1)S(1)} %get-tuple-element.53), channel_id=1, source_target_pairs={{0,2},{1,3},{2,0},{3,1},{4,6},{5,7},{6,4},{7,5},{8,10},{9,11},{10,... | collective-permute-start | bytes 245768 | tf_op jit(solution)/shard_map/ppermute | solution.py:426
  26.1 1.9 %collective-permute-start.13 = (bf16[80,512]{1,0:T(8,128)(2,1)S(1)}, bf16[80,512]{1,0:T(8,128)(2,1)S(1)}, u32[]{:S(2)}, u32[]{:S(2)}) collective-permute-start(bf16[80,512]{1,0:T(8,128)(2,1)S(1)} %get-tuple-element.54), channel_id=1, source_target_pairs={{0,3},{1,0},{2,1},{3,2},{4,7},{5,4},{6,5},{7,6},{8,11},{9,8},{10,9... | collective-permute-start | bytes 245768 | tf_op jit(solution)/shard_map/ppermute | solution.py:426
  28.0 2.8 %collective-permute-done.11.refs_3_.refs_1_ = bf16[80,512]{1,0:T(8,128)(2,1)S(1)} collective-permute-done((bf16[80,512]{1,0:T(8,128)(2,1)S(1)}, bf16[80,512]{1,0:T(8,128)(2,1)S(1)}, u32[]{:S(2)}, u32[]{:S(2)}) %collective-permute-start.11) | collective-permute-done | bytes 81952 | tf_op jit(solution)/shard_map/ppermute | solution.py:426
  30.8 0.3 collective-permute-done.12.refs_4_.refs_2_
  31.1 0.0 collective-permute-done.13.refs_5_.refs_3_
  31.1 0.1 by_columns_owner.1
  31.2 4.0 %collective-permute-start.14 = (bf16[64,512]{1,0:T(8,128)(2,1)S(1)}, bf16[64,512]{1,0:T(8,128)(2,1)S(1)}, u32[]{:S(2)}, u32[]{:S(2)}) collective-permute-start(bf16[64,512]{1,0:T(8,128)(2,1)S(1)} %get-tuple-element.58), channel_id=1, source_target_pairs={{0,8},{4,12},{8,16},{12,20},{16,24},{20,28},{24,0},{28,4},{1,9},{5... | collective-permute-start | bytes 196616 | tf_op jit(solution)/shard_map/ppermute | solution.py:430
  35.1 5.4 %collective-permute-start.15 = (bf16[64,512]{1,0:T(8,128)(2,1)S(1)}, bf16[64,512]{1,0:T(8,128)(2,1)S(1)}, u32[]{:S(2)}, u32[]{:S(2)}) collective-permute-start(bf16[64,512]{1,0:T(8,128)(2,1)S(1)} %get-tuple-element.59), channel_id=1, source_target_pairs={{0,16},{4,20},{8,24},{12,28},{16,0},{20,4},{24,8},{28,12},{1,17},{... | collective-permute-start | bytes 196616 | tf_op jit(solution)/shard_map/ppermute | solution.py:430
  40.5 1.9 %collective-permute-start.16 = (bf16[64,512]{1,0:T(8,128)(2,1)S(1)}, bf16[64,512]{1,0:T(8,128)(2,1)S(1)}, u32[]{:S(2)}, u32[]{:S(2)}) collective-permute-start(bf16[64,512]{1,0:T(8,128)(2,1)S(1)} %get-tuple-element.60), channel_id=1, source_target_pairs={{0,24},{4,28},{8,0},{12,4},{16,8},{20,12},{24,16},{28,20},{1,25},{... | collective-permute-start | bytes 196616 | tf_op jit(solution)/shard_map/ppermute | solution.py:430
  42.4 1.4 %finish.1 = (bf16[256,1024]{1,0:T(8,128)(2,1)}, f32[64,64]{1,0:T(8,128)}) custom-call(bf16[256,512]{1,0:T(8,128)(2,1)S(1)} %get-tuple-element.43.refs_17_.refs_0_, bf16[256,512]{1,0:T(8,128)(2,1)S(1)} %get-tuple-element.47.refs_1_, bf16[80,512]{1,0:T(8,128)(2,1)S(1)} %get-tuple-element.51.refs_2_.refs_0_, ...), custom_call_target="tpu_custom_call" | custom-call | bytes 1048576 | tf_op jit(solution)/shard_map/finish/pallas_call | solution.py:374
  43.9 0.0 collective-permute-done.14
  43.9 1.1 %collective-permute-done.15 = bf16[64,512]{1,0:T(8,128)(2,1)S(1)} collective-permute-done((bf16[64,512]{1,0:T(8,128)(2,1)S(1)}, bf16[64,512]{1,0:T(8,128)(2,1)S(1)}, u32[]{:S(2)}, u32[]{:S(2)}) %collective-permute-start.15) | collective-permute-done | bytes 65568 | tf_op jit(solution)/shard_map/ppermute | solution.py:430
  45.0 0.0 collective-permute-done.16
  45.0 0.7 %add_bitcast_fusion = f32[1,64,512]{2,1,0:T(8,128)} fusion(bf16[64,512]{1,0:T(8,128)(2,1)S(1)} %collective-permute-done.16, bf16[64,512]{1,0:T(8,128)(2,1)S(1)} %collective-permute-done.15, bf16[64,512]{1,0:T(8,128)(2,1)S(1)} %collective-permute-done.14, bf16[64,512]{1,0:T(8,128)(2,1)S(1)} %get-tuple-element.57), kind=kLoop, calls=%fused_computation | loop fusion | flops 229376 | bytes 393216 | tf_op jit(solution)/shard_map/broadcast_in_dim | solution.py:431
  (5 shorter events, 0.0 us)
Async XLA Ops:
  2.2 12.3 %copy-start = (bf16[272,256]{1,0:T(8,128)(2,1)S(1)}, bf16[272,256]{1,0:T(8,128)(2,1)}, u32[]{:S(2)}) copy-start(bf16[272,256]{1,0:T(8,128)(2,1)} %pack.1.refs_2_.refs_3_.own_notes) | copy-start | bytes 417796
  2.2 12.3 %copy-start.1 = (bf16[256,1024]{1,0:T(8,128)(2,1)S(1)}, bf16[256,1024]{1,0:T(8,128)(2,1)}, u32[]{:S(2)}) copy-start(bf16[256,1024]{1,0:T(8,128)(2,1)} %refs_0_.5) | copy-start | bytes 1572868
  2.2 12.3 %copy-start.2 = (bf16[256,1024]{1,0:T(8,128)(2,1)S(1)}, bf16[256,1024]{1,0:T(8,128)(2,1)}, u32[]{:S(2)}) copy-start(bf16[256,1024]{1,0:T(8,128)(2,1)} %refs_1_.5) | copy-start | bytes 1572868
  2.3 8.0 %collective-permute-start.3 = (bf16[272,256]{1,0:T(8,128)(2,1)}, bf16[272,256]{1,0:T(8,128)(2,1)S(1)}, u32[]{:S(2)}, u32[]{:S(2)}) collective-permute-start(bf16[272,256]{1,0:T(8,128)(2,1)} %pack.1.refs_2_.refs_3_.own_notes), channel_id=1, source_target_pairs={{0,4},{4,0},{8,12},{12,8},{16,20},{20,16},{24,28},{28,24},{1,5},{5... | collective-permute-start | bytes 417800 | tf_op jit(solution)/shard_map/ppermute | solution.py:401
  2.8 14.4 %collective-permute-start.2 = (bf16[272,256]{1,0:T(8,128)(2,1)}, bf16[272,256]{1,0:T(8,128)(2,1)S(1)}, u32[]{:S(2)}, u32[]{:S(2)}) collective-permute-start(bf16[272,256]{1,0:T(8,128)(2,1)} %pack.1.refs_2_.refs_3_.own_notes), channel_id=1, source_target_pairs={{0,16},{4,20},{8,24},{12,28},{16,0},{20,4},{24,8},{28,12},{1,17},{... | collective-permute-start | bytes 417800 | tf_op jit(solution)/shard_map/ppermute | solution.py:399
  6.4 10.8 %collective-permute-start.1 = (bf16[272,256]{1,0:T(8,128)(2,1)}, bf16[272,256]{1,0:T(8,128)(2,1)S(1)}, u32[]{:S(2)}, u32[]{:S(2)}) collective-permute-start(bf16[272,256]{1,0:T(8,128)(2,1)} %pack.1.refs_2_.refs_3_.own_notes), channel_id=1, source_target_pairs={{0,8},{4,12},{8,16},{12,20},{16,24},{20,28},{24,0},{28,4},{1,9},{5... | collective-permute-start | bytes 417800 | tf_op jit(solution)/shard_map/ppermute | solution.py:399
  8.0 10.5 %collective-permute-start = (bf16[272,256]{1,0:T(8,128)(2,1)}, bf16[272,256]{1,0:T(8,128)(2,1)S(1)}, u32[]{:S(2)}, u32[]{:S(2)}) collective-permute-start(bf16[272,256]{1,0:T(8,128)(2,1)} %pack.1.refs_2_.refs_3_.own_notes), channel_id=1, source_target_pairs={{0,24},{4,28},{8,0},{12,4},{16,8},{20,12},{24,16},{28,20},{1,25},{... | collective-permute-start | bytes 417800 | tf_op jit(solution)/shard_map/ppermute | solution.py:399
  10.3 1.0 %copy-start.4 = (bf16[1,64,4096]{2,1,0:T(8,128)(2,1)S(1)}, bf16[1,64,4096]{2,1,0:T(8,128)(2,1)}, u32[]{:S(2)}) copy-start(bf16[1,64,4096]{2,1,0:T(8,128)(2,1)} %adapter_b.1) | copy-start | bytes 1572868
  11.4 10.5 %copy-start.3 = (bf16[256,64]{0,1:T(8,128)(2,1)S(1)}, bf16[256,64]{0,1:T(8,128)(2,1)}, u32[]{:S(2)}) copy-start(bf16[256,64]{0,1:T(8,128)(2,1)} %param.14) | copy-start | bytes 98308
  11.4 7.0 %collective-permute-start.4 = (bf16[64,1024]{1,0:T(8,128)(2,1)S(1)}, bf16[64,1024]{1,0:T(8,128)(2,1)S(1)}, u32[]{:S(2)}, u32[]{:S(2)}) collective-permute-start(bf16[64,1024]{1,0:T(8,128)(2,1)S(1)} %get-tuple-element.35), channel_id=1, source_target_pairs={{0,1},{1,2},{2,3},{3,0},{4,7},{5,4},{6,5},{7,6},{8,9},{9,10},{10,1... | collective-permute-start | bytes 393224 | tf_op jit(solution)/shard_map/ppermute | solution.py:411
  13.0 7.1 %collective-permute-start.5 = (bf16[64,1024]{1,0:T(8,128)(2,1)S(1)}, bf16[64,1024]{1,0:T(8,128)(2,1)S(1)}, u32[]{:S(2)}, u32[]{:S(2)}) collective-permute-start(bf16[64,1024]{1,0:T(8,128)(2,1)S(1)} %get-tuple-element.36), channel_id=1, source_target_pairs={{0,2},{1,3},{2,0},{3,1},{4,6},{5,7},{6,4},{7,5},{8,10},{9,11},{10,... | collective-permute-start | bytes 393224 | tf_op jit(solution)/shard_map/ppermute | solution.py:411
  20.1 1.4 %collective-permute-start.6 = (bf16[272,256]{1,0:T(8,128)(2,1)S(1)}, bf16[272,256]{1,0:T(8,128)(2,1)S(1)}, u32[]{:S(2)}, u32[]{:S(2)}) collective-permute-start(bf16[272,256]{1,0:T(8,128)(2,1)S(1)} %collective-permute-done.1.refs_3_), channel_id=1, source_target_pairs={{0,4},{4,0},{8,12},{12,8},{16,20},{20,16},{24,28},{28,24},{1,5},{5... | collective-permute-start | bytes 417800 | tf_op jit(solution)/shard_map/ppermute | solution.py:416
  20.1 1.6 %collective-permute-start.7 = (bf16[272,256]{1,0:T(8,128)(2,1)S(1)}, bf16[272,256]{1,0:T(8,128)(2,1)S(1)}, u32[]{:S(2)}, u32[]{:S(2)}) collective-permute-start(bf16[272,256]{1,0:T(8,128)(2,1)S(1)} %collective-permute-done.2.refs_4_), channel_id=1, source_target_pairs={{0,4},{4,0},{8,12},{12,8},{16,20},{20,16},{24,28},{28,24},{1,5},{5... | collective-permute-start | bytes 417800 | tf_op jit(solution)/shard_map/ppermute | solution.py:416
  20.6 1.4 %collective-permute-start.8 = (bf16[272,256]{1,0:T(8,128)(2,1)S(1)}, bf16[272,256]{1,0:T(8,128)(2,1)S(1)}, u32[]{:S(2)}, u32[]{:S(2)}) collective-permute-start(bf16[272,256]{1,0:T(8,128)(2,1)S(1)} %collective-permute-done.refs_5_), channel_id=1, source_target_pairs={{0,4},{4,0},{8,12},{12,8},{16,20},{20,16},{24,28},{28,24},{1,5},{5... | collective-permute-start | bytes 417800 | tf_op jit(solution)/shard_map/ppermute | solution.py:416
  20.6 2.3 %collective-permute-start.9 = (bf16[64,1024]{1,0:T(8,128)(2,1)S(1)}, bf16[64,1024]{1,0:T(8,128)(2,1)S(1)}, u32[]{:S(2)}, u32[]{:S(2)}) collective-permute-start(bf16[64,1024]{1,0:T(8,128)(2,1)S(1)} %collective-permute-done.4.refs_14_), channel_id=1, source_target_pairs={{0,4},{4,0},{8,12},{12,8},{16,20},{20,16},{24,28},{28,24},{1,5},{5... | collective-permute-start | bytes 393224 | tf_op jit(solution)/shard_map/ppermute | solution.py:417
  22.6 1.7 %collective-permute-start.10 = (bf16[128,512]{1,0:T(8,128)(2,1)S(1)}, bf16[128,512]{1,0:T(8,128)(2,1)S(1)}, u32[]{:S(2)}, u32[]{:S(2)}) collective-permute-start(bf16[128,512]{1,0:T(8,128)(2,1)S(1)} %get-tuple-element.49), channel_id=1, source_target_pairs={{0,4},{4,0},{8,12},{12,8},{16,20},{20,16},{24,28},{28,24},{1,5},{5... | collective-permute-start | bytes 393224 | tf_op jit(solution)/shard_map/ppermute | solution.py:422
  24.5 6.3 %collective-permute-start.11 = (bf16[80,512]{1,0:T(8,128)(2,1)S(1)}, bf16[80,512]{1,0:T(8,128)(2,1)S(1)}, u32[]{:S(2)}, u32[]{:S(2)}) collective-permute-start(bf16[80,512]{1,0:T(8,128)(2,1)S(1)} %get-tuple-element.52), channel_id=1, source_target_pairs={{0,1},{1,2},{2,3},{3,0},{4,5},{5,6},{6,7},{7,4},{8,9},{9,10},{10,1... | collective-permute-start | bytes 245768 | tf_op jit(solution)/shard_map/ppermute | solution.py:426
  24.6 6.5 %collective-permute-start.12 = (bf16[80,512]{1,0:T(8,128)(2,1)S(1)}, bf16[80,512]{1,0:T(8,128)(2,1)S(1)}, u32[]{:S(2)}, u32[]{:S(2)}) collective-permute-start(bf16[80,512]{1,0:T(8,128)(2,1)S(1)} %get-tuple-element.53), channel_id=1, source_target_pairs={{0,2},{1,3},{2,0},{3,1},{4,6},{5,7},{6,4},{7,5},{8,10},{9,11},{10,... | collective-permute-start | bytes 245768 | tf_op jit(solution)/shard_map/ppermute | solution.py:426
  26.1 5.0 %collective-permute-start.13 = (bf16[80,512]{1,0:T(8,128)(2,1)S(1)}, bf16[80,512]{1,0:T(8,128)(2,1)S(1)}, u32[]{:S(2)}, u32[]{:S(2)}) collective-permute-start(bf16[80,512]{1,0:T(8,128)(2,1)S(1)} %get-tuple-element.54), channel_id=1, source_target_pairs={{0,3},{1,0},{2,1},{3,2},{4,7},{5,4},{6,5},{7,6},{8,11},{9,8},{10,9... | collective-permute-start | bytes 245768 | tf_op jit(solution)/shard_map/ppermute | solution.py:426
  31.2 12.7 %collective-permute-start.14 = (bf16[64,512]{1,0:T(8,128)(2,1)S(1)}, bf16[64,512]{1,0:T(8,128)(2,1)S(1)}, u32[]{:S(2)}, u32[]{:S(2)}) collective-permute-start(bf16[64,512]{1,0:T(8,128)(2,1)S(1)} %get-tuple-element.58), channel_id=1, source_target_pairs={{0,8},{4,12},{8,16},{12,20},{16,24},{20,28},{24,0},{28,4},{1,9},{5... | collective-permute-start | bytes 196616 | tf_op jit(solution)/shard_map/ppermute | solution.py:430
  35.1 9.9 %collective-permute-start.15 = (bf16[64,512]{1,0:T(8,128)(2,1)S(1)}, bf16[64,512]{1,0:T(8,128)(2,1)S(1)}, u32[]{:S(2)}, u32[]{:S(2)}) collective-permute-start(bf16[64,512]{1,0:T(8,128)(2,1)S(1)} %get-tuple-element.59), channel_id=1, source_target_pairs={{0,16},{4,20},{8,24},{12,28},{16,0},{20,4},{24,8},{28,12},{1,17},{... | collective-permute-start | bytes 196616 | tf_op jit(solution)/shard_map/ppermute | solution.py:430
  40.5 4.5 %collective-permute-start.16 = (bf16[64,512]{1,0:T(8,128)(2,1)S(1)}, bf16[64,512]{1,0:T(8,128)(2,1)S(1)}, u32[]{:S(2)}, u32[]{:S(2)}) collective-permute-start(bf16[64,512]{1,0:T(8,128)(2,1)S(1)} %get-tuple-element.60), channel_id=1, source_target_pairs={{0,24},{4,28},{8,0},{12,4},{16,8},{20,12},{24,16},{28,20},{1,25},{... | collective-permute-start | bytes 196616 | tf_op jit(solution)/shard_map/ppermute | solution.py:430
